TPU v7x, 128 devices: a whole 4x4x4 slice. The times are simulated.
128 devices in a mesh: dp: 8 (over z, core), ctx: 16 (over y, x).
Axes of the slice: x: 4, y: 4, z: 4, core: 2. Of those that a mesh axis runs over, the one named last changes fastest.
Arguments:
- layer_input: bfloat16 [8, 2048, 1536], P('dp', 'ctx'), may hold values from -6 to 6
- cotangent: bfloat16 [8, 2048, 1536], P('dp', 'ctx'), may hold values from -6 to 6
- attn_gain: bfloat16 [1536], P('dp'), may hold values from 0.25 to 1.75
- w_query: bfloat16 [1536, 1536], P('dp'), may hold values from -0.15625 to 0.15625
- w_key: bfloat16 [1536, 768], P('dp'), may hold values from -0.15625 to 0.15625
- w_value: bfloat16 [1536, 768], P('dp'), may hold values from -0.15625 to 0.15625
- w_out: bfloat16 [1536, 1536], P(None, 'dp'), may hold values from -0.625 to 0.625
- mlp_gain: bfloat16 [1536], P('dp'), may hold values from 0.25 to 1.75
- w_gate: bfloat16 [1536, 4096], P('dp'), may hold values from -0.15625 to 0.15625
- w_up: bfloat16 [1536, 4096], P('dp'), may hold values from -0.15625 to 0.15625
- w_down: bfloat16 [4096, 1536], P(None, 'dp'), may hold values from -0.09375 to 0.09375
- doc_lengths: int32 [8, 4], P('dp'), may hold values from 1 to 2045, as said below
- rope_pos: int32 [8, 2048], P('dp', 'ctx'), may hold values from 0 to 2559, as said below
- pad_lengths: int32 [8], P('dp'), may hold values from 0 to 63
Outputs:
- output: bfloat16 [8, 2048, 1536], P('dp', 'ctx')
- input_grad: bfloat16 [8, 2048, 1536], P('dp', 'ctx')
- attn_gain_grad: float32 [1536], P('dp')
- w_query_grad: float32 [1536, 1536], P('dp')
- w_key_grad: float32 [1536, 768], P('dp')
- w_value_grad: float32 [1536, 768], P('dp')
- w_out_grad: float32 [1536, 1536], P(None, 'dp')
- mlp_gain_grad: float32 [1536], P('dp')
- w_gate_grad: float32 [1536, 4096], P('dp')
- w_up_grad: float32 [1536, 4096], P('dp')
- w_down_grad: float32 [4096, 1536], P(None, 'dp')
Inputs may be any that keep to these rules, and one draw needn't show every extreme that they name: `doc_lengths`: each row's lengths sum to 2048; the second document starts within the first 64 tokens and ends within the last 128 tokens. `rope_pos`: within each document positions start at 0 and rise by 1 or 2 from one token to the next.
All inputs are finite; a program needn't handle non-finite values.
Results may differ from a plain program's by a relative error of at most 0.025.
Values may be sent and summed in bfloat16 or wider, within the bound.
A program may use at most 256 MiB of HBM per device.

v0:
```python
import math

import jax
import jax.numpy as jnp
from jax import lax
from jax.sharding import PartitionSpec as P

HQ = 16
HK = 8
HD = 96
WINDOW = 1024


EPSILON = 1e-05
THETA_BASE = 100000.0
NEG_LARGE = -1e30


def turned_gather(arrays, axis, dims):
    turned = [jnp.moveaxis(a, dim, 0) for a, dim in zip(arrays, dims)]
    widths = [t[0].size for t in turned]
    both = jnp.concatenate([t.reshape(-1, w) for t, w in zip(turned, widths)], axis=1)
    out = lax.all_gather(both, axis, axis=0, tiled=True)
    pieces = jnp.split(out, [sum(widths[:k]) for k in range(1, len(widths))], axis=1)
    return tuple(
        (
            jnp.moveaxis(b.reshape(-1, *t.shape[1:]), 0, dim)
            for b, t, dim in zip(pieces, turned, dims)
        )
    )


def passed_along(block, axis, distance):
    devices = range(lax.axis_size(axis))
    route = [(i - distance, i) for i in devices if i - distance in devices]
    return lax.ppermute(block, axis, route)


def in_one_piece(arrays, axis, dim, along):
    widths = [math.prod(a.shape[along:]) for a in arrays]
    both = jnp.concatenate(
        [a.reshape(*a.shape[:along], w) for a, w in zip(arrays, widths)], axis=along
    )
    out = lax.psum_scatter(both, axis, scatter_dimension=dim, tiled=True)
    pieces = jnp.split(out, [sum(widths[:k]) for k in range(1, len(widths))], axis=along)
    return tuple((b.reshape(*out.shape[:along], *a.shape[along:]) for a, b in zip(arrays, pieces)))


def rotate(values, positions):
    half_dim = values.shape[-1] // 2
    freq_table = THETA_BASE ** (
        -(jnp.arange(half_dim).astype(jnp.float32) * 2.0 / values.shape[-1])
    )
    angles = positions.astype(jnp.float32)[:, None] * freq_table[None, :]
    cosine = jnp.cos(angles)[:, None, :]
    sine = jnp.sin(angles)[:, None, :]
    first_half = values[..., :half_dim]
    second_half = values[..., half_dim:]
    return jnp.concatenate(
        [first_half * cosine - second_half * sine, second_half * cosine + first_half * sine],
        axis=-1,
    )


def permitted(query_pos, key_pos, doc_ends, pad_len, seq_len):
    seg_query = jnp.sum(query_pos[:, None] >= doc_ends[None, :], axis=-1)
    seg_key = jnp.sum(key_pos[:, None] >= doc_ends[None, :], axis=-1)
    behind = query_pos[:, None] - key_pos[None, :]
    usable = (key_pos < seq_len - pad_len) & (key_pos >= 0)
    return (
        (behind >= 0)
        & (behind < WINDOW)
        & (seg_query[:, None] == seg_key[None, :])
        & (usable[None, :] | (behind == 0))
    )


def cross_rows(left, right):
    return lax.dot_general(
        left, right, (((0,), (0,)), ((), ())), preferred_element_type=jnp.float32
    )


def times_trans(left, right):
    return lax.dot_general(
        left, right, (((1,), (1,)), ((), ())), preferred_element_type=jnp.float32
    )


def on_device(
    layer_input,
    cotangent,
    attn_gain,
    w_query,
    w_key,
    w_value,
    w_out,
    mlp_gain,
    w_gate,
    w_up,
    w_down,
    doc_lengths,
    rope_pos,
    pad_lengths,
):
    block_len = layer_input.shape[1]
    ctx_count = lax.axis_size("ctx")
    seq_len = block_len * ctx_count
    ctx_index = lax.axis_index("ctx")
    query_pos = ctx_index * block_len + jnp.arange(block_len, dtype=jnp.int32)
    doc_ends = jnp.cumsum(doc_lengths[0])
    pad_len = pad_lengths[0]
    positions = rope_pos[0]
    group_size = HQ // HK
    scale = HD ** (-0.5)
    reach = min(ctx_count - 1, (WINDOW + block_len - 2) // block_len)
    gain_a, wq_full, wk_full, wv_full, wo_full = turned_gather(
        (attn_gain, w_query, w_key, w_value, w_out), "dp", (0, 0, 0, 0, 1)
    )
    gain_m, wg_full, wu_full, wd_full = turned_gather(
        (mlp_gain, w_gate, w_up, w_down), "dp", (0, 0, 0, 1)
    )
    inputs = layer_input[0].astype(jnp.float32)
    inv_one = lax.rsqrt(jnp.mean(inputs * inputs, axis=-1, keepdims=True) + EPSILON)
    normed_one = inputs * inv_one
    hidden_one = (normed_one * gain_a.astype(jnp.float32)).astype(jnp.bfloat16)
    q_flat = jnp.dot(hidden_one, wq_full, preferred_element_type=jnp.float32)
    queries = (
        rotate(q_flat.reshape(block_len, HQ, HD), positions)
        .astype(jnp.bfloat16)
        .reshape(block_len, HK, group_size, HD)
    )
    k_flat = jnp.dot(hidden_one, wk_full, preferred_element_type=jnp.float32)
    keys_own = (
        rotate(k_flat.reshape(block_len, HK, HD), positions)
        .astype(jnp.bfloat16)
        .reshape(block_len, HK * HD)
    )
    values_own = jnp.dot(hidden_one, wv_full, preferred_element_type=jnp.float32).astype(
        jnp.bfloat16
    )
    key_list = [keys_own]
    value_list = [values_own]
    for shift_by in range(1, reach + 1):
        moved_keys, moved_values = passed_along((keys_own, values_own), "ctx", shift_by)
        key_list.insert(0, moved_keys)
        value_list.insert(0, moved_values)
    keys_all = jnp.concatenate(key_list, axis=0)
    values_all = jnp.concatenate(value_list, axis=0)
    key_start = (ctx_index - reach) * block_len
    key_count = keys_all.shape[0]
    key_pos = key_start + jnp.arange(key_count, dtype=jnp.int32)
    key_heads = keys_all.reshape(key_count, HK, HD)
    value_heads = values_all.reshape(key_count, HK, HD)
    scores = (
        jnp.einsum("qgrd,kgd->grqk", queries, key_heads, preferred_element_type=jnp.float32) * scale
    )
    allowed = permitted(query_pos, key_pos, doc_ends, pad_len, seq_len)
    scores = jnp.where(allowed[None, None], scores, NEG_LARGE)
    top_score = jnp.max(scores, axis=-1, keepdims=True)
    expo = jnp.exp(scores - top_score)
    prob_full = expo / jnp.sum(expo, axis=-1, keepdims=True)
    prob_low = prob_full.astype(jnp.bfloat16)
    attended = jnp.einsum(
        "grqk,kgd->qgrd", prob_low, value_heads, preferred_element_type=jnp.float32
    )
    attended = attended.reshape(block_len, HQ * HD).astype(jnp.bfloat16)
    resid = inputs + jnp.dot(attended, wo_full, preferred_element_type=jnp.float32)
    inv_two = lax.rsqrt(jnp.mean(resid * resid, axis=-1, keepdims=True) + EPSILON)
    normed_two = resid * inv_two
    hidden_two = (normed_two * gain_m.astype(jnp.float32)).astype(jnp.bfloat16)
    gate_pre = jnp.dot(hidden_two, wg_full, preferred_element_type=jnp.float32)
    up_pre = jnp.dot(hidden_two, wu_full, preferred_element_type=jnp.float32)
    sigmoid_gate = jax.nn.sigmoid(gate_pre)
    activated = gate_pre * sigmoid_gate
    mixed = (activated * up_pre).astype(jnp.bfloat16)
    output = resid + jnp.dot(mixed, wd_full, preferred_element_type=jnp.float32)
    grad_out = cotangent[0].astype(jnp.float32)
    grad_down = grad_out.astype(jnp.bfloat16)
    dw_down = cross_rows(mixed, grad_down)
    grad_mixed = times_trans(grad_down, wd_full)
    grad_gate = (
        grad_mixed * up_pre * sigmoid_gate * (1.0 + gate_pre * (1.0 - sigmoid_gate))
    ).astype(jnp.bfloat16)
    grad_up = (grad_mixed * activated).astype(jnp.bfloat16)
    dw_gate = cross_rows(hidden_two, grad_gate)
    dw_up = cross_rows(hidden_two, grad_up)
    grad_hidden_two = times_trans(grad_gate, wg_full) + times_trans(grad_up, wu_full)
    dgain_m = jnp.sum(grad_hidden_two * normed_two, axis=0)
    scaled_two = grad_hidden_two * gain_m.astype(jnp.float32)
    grad_resid = grad_out + inv_two * (
        scaled_two - normed_two * jnp.mean(scaled_two * normed_two, axis=-1, keepdims=True)
    )
    grad_branch = grad_resid.astype(jnp.bfloat16)
    dw_out = cross_rows(attended, grad_branch)
    grad_att = (
        times_trans(grad_branch, wo_full)
        .astype(jnp.bfloat16)
        .reshape(block_len, HK, group_size, HD)
    )
    grad_probs = jnp.einsum(
        "qgrd,kgd->grqk", grad_att, value_heads, preferred_element_type=jnp.float32
    )
    grad_vals = jnp.einsum(
        "grqk,qgrd->kgd", prob_low, grad_att, preferred_element_type=jnp.float32
    ).reshape(key_count, HK * HD)
    row_inner = jnp.sum(prob_full * grad_probs, axis=-1, keepdims=True)
    grad_scores = (prob_full * (grad_probs - row_inner)).astype(jnp.bfloat16)
    grad_queries = (
        jnp.einsum("grqk,kgd->qgrd", grad_scores, key_heads, preferred_element_type=jnp.float32)
        * scale
    )
    grad_keys = (
        jnp.einsum("grqk,qgrd->kgd", grad_scores, queries, preferred_element_type=jnp.float32)
        * scale
    ).reshape(key_count, HK * HD)
    own_keys = grad_keys[key_count - block_len :]
    own_vals = grad_vals[key_count - block_len :]
    for shift_by in range(1, reach + 1):
        piece_start = (reach - shift_by) * block_len
        back_keys, back_vals = (
            passed_along(
                grad_keys[piece_start : piece_start + block_len].astype(jnp.bfloat16),
                "ctx",
                -shift_by,
            ).astype(jnp.float32),
            passed_along(
                grad_vals[piece_start : piece_start + block_len].astype(jnp.bfloat16),
                "ctx",
                -shift_by,
            ).astype(jnp.float32),
        )
        own_keys = own_keys + back_keys
        own_vals = own_vals + back_vals
    grad_q_pre = (
        rotate(grad_queries.reshape(block_len, HQ, HD), -positions)
        .reshape(block_len, HQ * HD)
        .astype(jnp.bfloat16)
    )
    grad_k_pre = (
        rotate(own_keys.reshape(block_len, HK, HD), -positions)
        .reshape(block_len, HK * HD)
        .astype(jnp.bfloat16)
    )
    grad_v_pre = own_vals.astype(jnp.bfloat16)
    dw_query = cross_rows(hidden_one, grad_q_pre)
    dw_key = cross_rows(hidden_one, grad_k_pre)
    dw_value = cross_rows(hidden_one, grad_v_pre)
    grad_hidden_one = (
        times_trans(grad_q_pre, wq_full)
        + times_trans(grad_k_pre, wk_full)
        + times_trans(grad_v_pre, wv_full)
    )
    dgain_a = jnp.sum(grad_hidden_one * normed_one, axis=0)
    scaled_one = grad_hidden_one * gain_a.astype(jnp.float32)
    grad_in = grad_resid + inv_one * (
        scaled_one - normed_one * jnp.mean(scaled_one * normed_one, axis=-1, keepdims=True)
    )
    mlp_rows = (
        *tuple(
            (
                part.astype(jnp.float32)
                for part in in_one_piece(
                    (
                        dgain_m.astype(jnp.bfloat16),
                        dw_gate.astype(jnp.bfloat16),
                        dw_up.astype(jnp.bfloat16),
                    ),
                    "dp",
                    0,
                    1,
                )
            )
        ),
        lax.psum_scatter(
            dw_down.astype(jnp.bfloat16), "dp", scatter_dimension=1, tiled=True
        ).astype(jnp.float32),
    )
    attn_rows = (
        *tuple(
            (
                part.astype(jnp.float32)
                for part in in_one_piece(
                    (
                        dgain_a.astype(jnp.bfloat16),
                        dw_query.astype(jnp.bfloat16),
                        dw_key.astype(jnp.bfloat16),
                        dw_value.astype(jnp.bfloat16),
                    ),
                    "dp",
                    0,
                    1,
                )
            )
        ),
        lax.psum_scatter(dw_out.astype(jnp.bfloat16), "dp", scatter_dimension=1, tiled=True).astype(
            jnp.float32
        ),
    )
    results = (
        lax.psum(attn_rows[0].astype(jnp.bfloat16), "ctx").astype(jnp.float32),
        lax.psum(attn_rows[1].astype(jnp.bfloat16), "ctx").astype(jnp.float32),
        lax.psum(attn_rows[2].astype(jnp.bfloat16), "ctx").astype(jnp.float32),
        lax.psum(attn_rows[3].astype(jnp.bfloat16), "ctx").astype(jnp.float32),
        lax.psum(attn_rows[4].astype(jnp.bfloat16), "ctx").astype(jnp.float32),
        lax.psum(mlp_rows[0].astype(jnp.bfloat16), "ctx").astype(jnp.float32),
        lax.psum(mlp_rows[1].astype(jnp.bfloat16), "ctx").astype(jnp.float32),
        lax.psum(mlp_rows[2].astype(jnp.bfloat16), "ctx").astype(jnp.float32),
        lax.psum(mlp_rows[3].astype(jnp.bfloat16), "ctx").astype(jnp.float32),
    )
    return (
        output.astype(jnp.bfloat16)[None],
        grad_in.astype(jnp.bfloat16)[None],
        results[0],
        results[1],
        results[2],
        results[3],
        results[4],
        results[5],
        results[6],
        results[7],
        results[8],
    )


def solution(mesh):
    in_specs = (
        P("dp", "ctx", None),
        P("dp", "ctx", None),
        P("dp"),
        P("dp", None),
        P("dp", None),
        P("dp", None),
        P(None, "dp"),
        P("dp"),
        P("dp", None),
        P("dp", None),
        P(None, "dp"),
        P("dp", None),
        P("dp", "ctx"),
        P("dp"),
    )
    out_specs = (
        P("dp", "ctx", None),
        P("dp", "ctx", None),
        P("dp"),
        P("dp", None),
        P("dp", None),
        P("dp", None),
        P(None, "dp"),
        P("dp"),
        P("dp", None),
        P("dp", None),
        P(None, "dp"),
    )
    return jax.shard_map(
        on_device, mesh=mesh, in_specs=in_specs, out_specs=out_specs, check_vma=False
    )
```

profile of v0, /device:TPU:1, one launch (start us, length us, event | category | flops | bytes accessed | tf_op | source)
XLA Modules:
  0.0 977.6 jit_solution(729281655652782674)
XLA Ops:
  8.2 4.4 concatenate.53
  12.7 9.6 concatenate.68
  26.5 65.7 %all-gather.3.cloned.1.call-done = bf16[1536,4609]{1,0:T(8,128)(2,1)} async-done(((bf16[192,4609]{1,0:T(8,128)(2,1)}), bf16[1536,4609]{1,0:T(8,128)(2,1)}) %all-gather.3.cloned.1.call-update) | async-done | bytes 14158864 | tf_op jit(solution)/shard_map/all_gather | solution.py:23
  93.3 2.8 fusion.67
  96.1 3.8 collective-permute-start.7
  99.9 4.3 collective-permute-start.6
  104.2 4.0 collective-permute-start.5
  108.2 3.2 collective-permute-start.1
  111.4 3.1 collective-permute-start
  114.5 4.7 slice_bitcast_fusion.1
  119.2 2.8 copy.71
  122.1 7.3 slice_bitcast_fusion
  129.4 6.7 copy.72
  136.0 3.8 fusion.112
  146.1 2.0 collective-permute-start.4
  148.2 2.8 collective-permute-done.3
  150.9 2.8 collective-permute-start.15
  153.7 5.7 collective-permute-done.4
  161.4 5.0 collective-permute-start.13
  173.3 2.2 copy.70
  175.5 7.9 collective-permute-done.8
  188.8 4.2 collective-permute-start.12
  193.0 2.8 collective-permute-done.11
  195.8 8.7 collective-permute-done.12
  206.8 6.6 fusion.146
  213.4 6.8 fusion.64
  220.2 5.2 multiply_reduce_fusion.2
  225.4 45.9 %all-gather.5.cloned.1.call-done = bf16[1536,12289]{1,0:T(8,128)(2,1)} async-done(((bf16[192,12289]{1,0:T(8,128)(2,1)}), bf16[1536,12289]{1,0:T(8,128)(2,1)}) %all-gather.5.cloned.1.call-update) | async-done | bytes 37751824 | tf_op jit(solution)/shard_map/all_gather | solution.py:23
  272.6 7.2 fusion.17
  279.8 7.3 fusion.7
  287.1 10.6 %multiply_convert_fusion.1 = (bf16[128,4096]{1,0:T(8,128)(2,1)S(1)}, bf16[128,4096]{1,0:T(8,128)(2,1)S(1)}, bf16[128,4096]{1,0:T(8,128)(2,1)}) fusion(f32[128,4096]{1,0:T(8,128)S(1)} %fusion.17, f32[128,4096]{1,0:T(8,128)S(1)} %fusion.7, bf16[128,1536]{1,0:T(8,128)(2,1)S(1)} %multiply_convert_fusion.3, bf16[1536,12289]{1,0:T(8,128)(2,1)} %all-gather.5.cloned.1.call-done), kind=kOutput, calls=%fused_computation.56 | convolution fusion | flops 1618477056 | bytes 20316160 | tf_op jit(solution)/shard_map/dot_general | solution.py:172
  297.7 8.7 fusion.5
  306.5 9.3 multiply_reduce_fusion
  317.2 4.8 fusion.40
  324.0 8.0 fusion.150
  331.9 9.5 fusion.13
  341.4 10.3 %fusion.15 = bf16[8,2,128,1152]{2,3,1,0:T(8,128)(2,1)} fusion(f32[8,1152,128,2]{2,1,3,0:T(8,128)} %get-tuple-element.113, f32[8,2,128]{2,1,0:T(2,128)S(1)} %get-tuple-element.112, f32[8,2,128,1152]{2,3,1,0:T(8,128)} %get-tuple-element.108, f32[8,2,128]{2,1,0:T(2,128)S(1)} %copy-done.32), kind=kLoop, calls=%fused_computation.20 | loop fusion | flops 9437184 | bytes 23609344 | tf_op jit(solution)/shard_map/convert_element_type | solution.py:208
  351.7 3.4 fusion.61
  365.2 4.9 fusion.27
  370.1 3.6 convolution_convert_fusion.3
  376.3 2.9 collective-permute-done.30
  389.3 4.0 collective-permute-done.23
  395.8 15.6 %collective-permute-done.22 = bf16[128,768]{0,1:T(8,128)(2,1)S(1)} collective-permute-done((bf16[128,768]{0,1:T(8,128)(2,1)S(1)}, bf16[128,768]{0,1:T(8,128)(2,1)S(1)}, u32[]{:S(2)}, u32[]{:S(2)}) %collective-permute-start.22) | collective-permute-done | bytes 196640 | tf_op jit(solution)/shard_map/ppermute | solution.py:36
  413.6 4.2 collective-permute-done.19
  419.6 2.3 convolution_convert_fusion.6
  421.9 3.0 convolution_add_fusion.1
  424.9 4.6 fusion.82
  429.5 46.0 %concatenate.71 = bf16[1536,3073]{0,1:T(8,128)(2,1)} concatenate(bf16[1536,1]{0,1:T(2,128)(2,1)S(1)} %convert_element_type.446, bf16[1536,1536]{0,1:T(8,128)(2,1)} %convolution_convert_fusion.3, bf16[1536,768]{0,1:T(8,128)(2,1)} %convolution_convert_fusion.6, bf16[1536,768]{0,1:T(8,128)(2,1)S(1)} %convolution_convert_fusion.5), dimensions={1} | concatenate | bytes 18880512 | tf_op jit(solution)/shard_map/concatenate | solution.py:41
  475.5 13.3 %copy.93 = bf16[1536,3073]{1,0:T(8,128)(2,1)} copy(bf16[1536,3073]{0,1:T(8,128)(2,1)} %concatenate.71) | data formatting | bytes 18880512
  489.8 7.8 convolution_convert_fusion.2
  497.6 6.4 convolution_convert_fusion.1
  504.0 51.2 %concatenate.72 = bf16[1536,8193]{1,0:T(8,128)(2,1)} concatenate(bf16[1536,1]{1,0:T(8,128)(2,1)S(1)} %convert_element_type.468, bf16[1536,4096]{1,0:T(8,128)(2,1)} %convolution_convert_fusion.2, bf16[1536,4096]{1,0:T(8,128)(2,1)} %convolution_convert_fusion.1), dimensions={1} | concatenate | bytes 50337792 | tf_op jit(solution)/shard_map/concatenate | solution.py:41
  556.2 3.7 convolution_convert_fusion.4
  561.2 6.6 convolution_convert_fusion
  573.8 133.6 %reduce-scatter.9.cloned.1.call-done = bf16[192,8193]{1,0:T(8,128)(2,1)} async-done(((bf16[1536,8193]{1,0:T(8,128)(2,1)}), bf16[192,8193]{1,0:T(8,128)(2,1)}) %reduce-scatter.9.cloned.1.call-update) | async-done | bytes 3146128 | tf_op jit(solution)/shard_map/reduce_scatter | solution.py:44
  707.4 4.8 fusion.142
  712.2 34.1 %reduce-scatter.7.cloned.1.call-done = bf16[1536,192]{0,1:T(8,128)(2,1)} async-done(((bf16[1536,1536]{0,1:T(8,128)(2,1)}), bf16[1536,192]{0,1:T(8,128)(2,1)}) %reduce-scatter.7.cloned.1.call-update) | async-done | bytes 589840 | tf_op jit(solution)/shard_map/reduce_scatter | solution.py:296
  746.3 76.2 %reduce-scatter.11.cloned.1.call-done = bf16[4096,192]{0,1:T(8,128)(2,1)} async-done(((bf16[4096,1536]{0,1:T(8,128)(2,1)}), bf16[4096,192]{0,1:T(8,128)(2,1)}) %reduce-scatter.11.cloned.1.call-update) | async-done | bytes 1572880 | tf_op jit(solution)/shard_map/reduce_scatter | solution.py:275
  823.7 10.5 %fusion.49 = bf16[1,128,1536]{2,1,0:T(8,128)(2,1)} fusion(f32[128,1536]{1,0:T(8,128)S(1)} %copy-done.5, bf16[128,4096]{1,0:T(8,128)(2,1)S(1)} %copy-done.6, bf16[1536,12289]{1,0:T(8,128)(2,1)} %all-gather.5.cloned.1.call-done), kind=kOutput, calls=%fused_computation.54 | convolution fusion | flops 1611005952 | bytes 14811136 | tf_op jit(solution)/shard_map/dot_general | solution.py:177
  837.1 34.8 %all-reduce = (bf16[192]{0:T(256)(128)(2,1)S(1)}, bf16[192]{0:T(256)(128)(2,1)S(1)}) all-reduce(bf16[192]{0:T(256)(128)(2,1)S(1)} %slice_reduce_fusion.1, bf16[192]{0:T(256)(128)(2,1)S(1)} %slice_reduce_fusion), channel_id=1, replica_groups=mesh['dp'=8,'ctx'=16] {'ctx'}, use_global_device_ids=true, to_apply=%region_12.13 | all-reduce | flops 384 | bytes 1536 | tf_op jit(solution)/shard_map/psum | solution.py:301
  873.0 84.7 %all-reduce.4.cloned.1.call-done = (bf16[192,1536]{0,1:T(8,128)(2,1)}, bf16[192,768]{0,1:T(8,128)(2,1)}, bf16[192,768]{0,1:T(8,128)(2,1)}, bf16[1536,192]{0,1:T(...) async-done(((bf16[192,1536]{0,1:T(8,128)(2,1)}, bf16[192,768]{0,1:T(8,128)(2,1)}, bf16[192,768]{0,1:T(8,128)(2,1)}, ...) | async-done | bytes 6488080 | tf_op jit(solution)/shard_map/psum | solution.py:302
  957.6 2.6 copy.81
  964.3 2.0 convert_element_type.461
  966.3 2.0 convert_element_type.462
  (209 shorter events, 82.5 us)
Async XLA Ops:
  7.2 5.4 copy-start.34
  7.2 5.5 copy-start.8
  7.2 5.5 copy-start.7
  7.2 84.9 %all-gather.3.cloned.1.call-start = ((), (), s32[]{:S(2)}) async-start(), calls=%async_computation.4 | async-start | bytes 16367616 | tf_op jit(solution)/shard_map/all_gather | solution.py:23
  12.5 258.7 %all-gather.5.cloned.1.call-start = ((), (), s32[]{:S(2)}) async-start(), calls=%async_computation.5 | async-start | bytes 42909696 | tf_op jit(solution)/shard_map/all_gather | solution.py:23
  22.3 545.9 %reduce-scatter.13.cloned.1.call-start = ((), (), s32[]{:S(2)}) async-start(), calls=%async_computation.9 | async-start | bytes 11059200
  23.6 401.3 %copy-start.29 = (f32[128]{0:T(128)}, f32[128]{0:T(128)S(1)}, u32[]{:S(2)}) copy-start(f32[128]{0:T(128)S(1)} %add_rsqrt_fusion.1) | copy-start | bytes 1540
  96.1 74.3 %collective-permute-start.7 = (bf16[128,768]{1,0:T(8,128)(2,1)S(1)}, bf16[128,768]{1,0:T(8,128)(2,1)}, u32[]{:S(2)}, u32[]{:S(2)}) collective-permute-start(bf16[128,768]{1,0:T(8,128)(2,1)S(1)} %fusion.67), channel_id=1, source_target_pairs={{0,1},{1,2},{2,3},{3,4},{4,5},{5,6},{6,7},{7,8},{8,9},{9,10},{10,1... | collective-permute-start | bytes 589832 | tf_op jit(solution)/shard_map/ppermute | solution.py:36
  99.9 67.5 %collective-permute-start.6 = (bf16[128,768]{1,0:T(8,128)(2,1)S(1)}, bf16[128,768]{1,0:T(8,128)(2,1)}, u32[]{:S(2)}, u32[]{:S(2)}) collective-permute-start(bf16[128,768]{1,0:T(8,128)(2,1)S(1)} %fusion.67), channel_id=1, source_target_pairs={{0,2},{1,3},{2,4},{3,5},{4,6},{5,7},{6,8},{7,9},{8,10},{9,11},{10,... | collective-permute-start | bytes 589832 | tf_op jit(solution)/shard_map/ppermute | solution.py:36
  104.2 57.2 %collective-permute-start.5 = (bf16[128,768]{1,0:T(8,128)(2,1)S(1)}, bf16[128,768]{1,0:T(8,128)(2,1)}, u32[]{:S(2)}, u32[]{:S(2)}) collective-permute-start(bf16[128,768]{1,0:T(8,128)(2,1)S(1)} %fusion.67), channel_id=1, source_target_pairs={{0,3},{1,4},{2,5},{3,6},{4,7},{5,8},{6,9},{7,10},{8,11},{9,12},{10... | collective-permute-start | bytes 589832 | tf_op jit(solution)/shard_map/ppermute | solution.py:36
  108.2 35.0 %collective-permute-start.1 = (bf16[128,768]{1,0:T(8,128)(2,1)S(1)}, bf16[128,768]{1,0:T(8,128)(2,1)}, u32[]{:S(2)}, u32[]{:S(2)}) collective-permute-start(bf16[128,768]{1,0:T(8,128)(2,1)S(1)} %fusion.67), channel_id=1, source_target_pairs={{0,7},{1,8},{2,9},{3,10},{4,11},{5,12},{6,13},{7,14},{8,15},{16,23... | collective-permute-start | bytes 589832 | tf_op jit(solution)/shard_map/ppermute | solution.py:36
  111.4 29.6 %collective-permute-start = (bf16[128,768]{1,0:T(8,128)(2,1)S(1)}, bf16[128,768]{1,0:T(8,128)(2,1)}, u32[]{:S(2)}, u32[]{:S(2)}) collective-permute-start(bf16[128,768]{1,0:T(8,128)(2,1)S(1)} %fusion.67), channel_id=1, source_target_pairs={{0,8},{1,9},{2,10},{3,11},{4,12},{5,13},{6,14},{7,15},{16,24},{17,... | collective-permute-start | bytes 589832 | tf_op jit(solution)/shard_map/ppermute | solution.py:36
  140.0 73.4 %copy-start.21 = (bf16[128,16,48]{0,2,1:T(8,128)(2,1)}, bf16[128,16,48]{0,2,1:T(8,128)(2,1)S(1)}, u32[]{:S(2)}) copy-start(bf16[128,16,48]{0,2,1:T(8,128)(2,1)S(1)} %get-tuple-element.93) | copy-start | bytes 589828
  140.0 73.4 %copy-start.23 = (bf16[128,16,48]{0,2,1:T(8,128)(2,1)}, bf16[128,16,48]{0,2,1:T(8,128)(2,1)S(1)}, u32[]{:S(2)}) copy-start(bf16[128,16,48]{0,2,1:T(8,128)(2,1)S(1)} %get-tuple-element.94) | copy-start | bytes 589828
  140.9 5.2 collective-permute-start.2
  143.2 7.7 collective-permute-start.3
  146.1 13.3 %collective-permute-start.4 = (bf16[128,768]{1,0:T(8,128)(2,1)S(1)}, bf16[128,768]{1,0:T(8,128)(2,1)S(1)}, u32[]{:S(2)}, u32[]{:S(2)}) collective-permute-start(bf16[128,768]{1,0:T(8,128)(2,1)S(1)} %fusion.67), channel_id=1, source_target_pairs={{0,4},{1,5},{2,6},{3,7},{4,8},{5,9},{6,10},{7,11},{8,12},{9,13},{1... | collective-permute-start | bytes 589832 | tf_op jit(solution)/shard_map/ppermute | solution.py:36
  150.9 55.7 %collective-permute-start.15 = (bf16[128,768]{0,1:T(8,128)(2,1)S(1)}, bf16[128,768]{0,1:T(8,128)(2,1)S(1)}, u32[]{:S(2)}, u32[]{:S(2)}) collective-permute-start(bf16[128,768]{0,1:T(8,128)(2,1)S(1)} %bitcast.283), channel_id=1, source_target_pairs={{0,1},{1,2},{2,3},{3,4},{4,5},{5,6},{6,7},{7,8},{8,9},{9,10},{10,1... | collective-permute-start | bytes 589832 | tf_op jit(solution)/shard_map/ppermute | solution.py:36
  159.4 46.3 %collective-permute-start.14 = (bf16[128,768]{0,1:T(8,128)(2,1)S(1)}, bf16[128,768]{0,1:T(8,128)(2,1)}, u32[]{:S(2)}, u32[]{:S(2)}) collective-permute-start(bf16[128,768]{0,1:T(8,128)(2,1)S(1)} %bitcast.284), channel_id=1, source_target_pairs={{0,2},{1,3},{2,4},{3,5},{4,6},{5,7},{6,8},{7,9},{8,10},{9,11},{10,... | collective-permute-start | bytes 589832 | tf_op jit(solution)/shard_map/ppermute | solution.py:36
  161.4 43.2 %collective-permute-start.13 = (bf16[128,768]{0,1:T(8,128)(2,1)S(1)}, bf16[128,768]{0,1:T(8,128)(2,1)}, u32[]{:S(2)}, u32[]{:S(2)}) collective-permute-start(bf16[128,768]{0,1:T(8,128)(2,1)S(1)} %bitcast.285), channel_id=1, source_target_pairs={{0,3},{1,4},{2,5},{3,6},{4,7},{5,8},{6,9},{7,10},{8,11},{9,12},{10... | collective-permute-start | bytes 589832 | tf_op jit(solution)/shard_map/ppermute | solution.py:36
  167.4 18.2 %collective-permute-start.9 = (bf16[128,768]{0,1:T(8,128)(2,1)S(1)}, bf16[128,768]{0,1:T(8,128)(2,1)}, u32[]{:S(2)}, u32[]{:S(2)}) collective-permute-start(bf16[128,768]{0,1:T(8,128)(2,1)S(1)} %bitcast.286), channel_id=1, source_target_pairs={{0,7},{1,8},{2,9},{3,10},{4,11},{5,12},{6,13},{7,14},{8,15},{16,23... | collective-permute-start | bytes 589832 | tf_op jit(solution)/shard_map/ppermute | solution.py:36
  170.4 13.0 %collective-permute-start.8 = (bf16[128,768]{0,1:T(8,128)(2,1)S(1)}, bf16[128,768]{0,1:T(8,128)(2,1)}, u32[]{:S(2)}, u32[]{:S(2)}) collective-permute-start(bf16[128,768]{0,1:T(8,128)(2,1)S(1)} %bitcast.287), channel_id=1, source_target_pairs={{0,8},{1,9},{2,10},{3,11},{4,12},{5,13},{6,14},{7,15},{16,24},{17,... | collective-permute-start | bytes 589832 | tf_op jit(solution)/shard_map/ppermute | solution.py:36
  183.4 5.4 collective-permute-start.10
  185.7 10.1 %collective-permute-start.11 = (bf16[128,768]{0,1:T(8,128)(2,1)S(1)}, bf16[128,768]{0,1:T(8,128)(2,1)S(1)}, u32[]{:S(2)}, u32[]{:S(2)}) collective-permute-start(bf16[128,768]{0,1:T(8,128)(2,1)S(1)} %bitcast.289), channel_id=1, source_target_pairs={{0,5},{1,6},{2,7},{3,8},{4,9},{5,10},{6,11},{7,12},{8,13},{9,14},{... | collective-permute-start | bytes 589832 | tf_op jit(solution)/shard_map/ppermute | solution.py:36
  188.8 15.8 %collective-permute-start.12 = (bf16[128,768]{0,1:T(8,128)(2,1)S(1)}, bf16[128,768]{0,1:T(8,128)(2,1)S(1)}, u32[]{:S(2)}, u32[]{:S(2)}) collective-permute-start(bf16[128,768]{0,1:T(8,128)(2,1)S(1)} %bitcast.290), channel_id=1, source_target_pairs={{0,4},{1,5},{2,6},{3,7},{4,8},{5,9},{6,10},{7,11},{8,12},{9,13},{1... | collective-permute-start | bytes 589832 | tf_op jit(solution)/shard_map/ppermute | solution.py:36
  213.4 6.8 copy-start.31
  220.2 52.4 %copy-start.12 = (bf16[1,128,1536]{2,1,0:T(8,128)(2,1)S(1)}, bf16[1,128,1536]{2,1,0:T(8,128)(2,1)}, u32[]{:S(2)}) copy-start(bf16[1,128,1536]{2,1,0:T(8,128)(2,1)} %param.15) | copy-start | bytes 1179652
  225.4 81.1 %copy-start.4 = (f32[128,1536]{1,0:T(8,128)}, f32[128,1536]{1,0:T(8,128)S(1)}, u32[]{:S(2)}) copy-start(f32[128,1536]{1,0:T(8,128)S(1)} %get-tuple-element.110) | copy-start | bytes 2359300
  272.6 14.5 %copy-start.2 = (bf16[128,1536]{1,0:T(8,128)(2,1)}, bf16[128,1536]{1,0:T(8,128)(2,1)S(1)}, u32[]{:S(2)}) copy-start(bf16[128,1536]{1,0:T(8,128)(2,1)S(1)} %multiply_convert_fusion.3) | copy-start | bytes 1179652
  297.7 8.7 copy-start.17
  297.7 8.8 copy-start.19
  306.5 9.3 copy-start.13
  317.1 6.8 copy-start.22
  317.2 6.8 copy-start.24
  317.2 6.8 copy-start.32
  356.9 8.1 copy-start.27
  357.0 8.1 copy-start.28
  357.3 16.4 %collective-permute-start.31 = (bf16[128,768]{0,1:T(8,128)(2,1)S(1)}, bf16[128,768]{0,1:T(8,128)(2,1)S(1)}, u32[]{:S(2)}, u32[]{:S(2)}) collective-permute-start(bf16[128,768]{0,1:T(8,128)(2,1)S(1)} %bitcast.282), channel_id=1, source_target_pairs={{8,0},{9,1},{10,2},{11,3},{12,4},{13,5},{14,6},{15,7},{24,16},{25,... | collective-permute-start | bytes 589832 | tf_op jit(solution)/shard_map/ppermute | solution.py:36
  358.6 16.4 %collective-permute-start.24 = (bf16[128,768]{0,1:T(8,128)(2,1)S(1)}, bf16[128,768]{0,1:T(8,128)(2,1)S(1)}, u32[]{:S(2)}, u32[]{:S(2)}) collective-permute-start(bf16[128,768]{0,1:T(8,128)(2,1)S(1)} %bitcast.281), channel_id=1, source_target_pairs={{1,0},{2,1},{3,2},{4,3},{5,4},{6,5},{7,6},{8,7},{9,8},{10,9},{11,1... | collective-permute-start | bytes 589832 | tf_op jit(solution)/shard_map/ppermute | solution.py:36
  359.9 19.3 %collective-permute-start.30 = (bf16[128,768]{0,1:T(8,128)(2,1)S(1)}, bf16[128,768]{0,1:T(8,128)(2,1)S(1)}, u32[]{:S(2)}, u32[]{:S(2)}) collective-permute-start(bf16[128,768]{0,1:T(8,128)(2,1)S(1)} %bitcast.279), channel_id=1, source_target_pairs={{7,0},{8,1},{9,2},{10,3},{11,4},{12,5},{13,6},{14,7},{15,8},{23,16... | collective-permute-start | bytes 589832 | tf_op jit(solution)/shard_map/ppermute | solution.py:36
  361.2 19.6 %collective-permute-start.29 = (bf16[128,768]{0,1:T(8,128)(2,1)S(1)}, bf16[128,768]{0,1:T(8,128)(2,1)S(1)}, u32[]{:S(2)}, u32[]{:S(2)}) collective-permute-start(bf16[128,768]{0,1:T(8,128)(2,1)S(1)} %bitcast.276), channel_id=1, source_target_pairs={{6,0},{7,1},{8,2},{9,3},{10,4},{11,5},{12,6},{13,7},{14,8},{15,9},... | collective-permute-start | bytes 589832 | tf_op jit(solution)/shard_map/ppermute | solution.py:36
  362.7 19.5 %collective-permute-start.28 = (bf16[128,768]{0,1:T(8,128)(2,1)S(1)}, bf16[128,768]{0,1:T(8,128)(2,1)S(1)}, u32[]{:S(2)}, u32[]{:S(2)}) collective-permute-start(bf16[128,768]{0,1:T(8,128)(2,1)S(1)} %bitcast.273), channel_id=1, source_target_pairs={{5,0},{6,1},{7,2},{8,3},{9,4},{10,5},{11,6},{12,7},{13,8},{14,9},{... | collective-permute-start | bytes 589832 | tf_op jit(solution)/shard_map/ppermute | solution.py:36
  373.7 10.9 %collective-permute-start.27 = (bf16[128,768]{0,1:T(8,128)(2,1)S(1)}, bf16[128,768]{0,1:T(8,128)(2,1)S(1)}, u32[]{:S(2)}, u32[]{:S(2)}) collective-permute-start(bf16[128,768]{0,1:T(8,128)(2,1)S(1)} %bitcast.270), channel_id=1, source_target_pairs={{4,0},{5,1},{6,2},{7,3},{8,4},{9,5},{10,6},{11,7},{12,8},{13,9},{1... | collective-permute-start | bytes 589832 | tf_op jit(solution)/shard_map/ppermute | solution.py:36
  375.0 10.9 %collective-permute-start.26 = (bf16[128,768]{0,1:T(8,128)(2,1)S(1)}, bf16[128,768]{0,1:T(8,128)(2,1)S(1)}, u32[]{:S(2)}, u32[]{:S(2)}) collective-permute-start(bf16[128,768]{0,1:T(8,128)(2,1)S(1)} %bitcast.268), channel_id=1, source_target_pairs={{3,0},{4,1},{5,2},{6,3},{7,4},{8,5},{9,6},{10,7},{11,8},{12,9},{13... | collective-permute-start | bytes 589832 | tf_op jit(solution)/shard_map/ppermute | solution.py:36
  379.2 8.5 collective-permute-start.25
  380.8 12.4 %collective-permute-start.23 = (bf16[128,768]{0,1:T(8,128)(2,1)S(1)}, bf16[128,768]{0,1:T(8,128)(2,1)S(1)}, u32[]{:S(2)}, u32[]{:S(2)}) collective-permute-start(bf16[128,768]{0,1:T(8,128)(2,1)S(1)} %bitcast.280), channel_id=1, source_target_pairs={{8,0},{9,1},{10,2},{11,3},{12,4},{13,5},{14,6},{15,7},{24,16},{25,... | collective-permute-start | bytes 589832 | tf_op jit(solution)/shard_map/ppermute | solution.py:36
  382.1 12.4 %collective-permute-start.16 = (bf16[128,768]{0,1:T(8,128)(2,1)S(1)}, bf16[128,768]{0,1:T(8,128)(2,1)S(1)}, u32[]{:S(2)}, u32[]{:S(2)}) collective-permute-start(bf16[128,768]{0,1:T(8,128)(2,1)S(1)} %bitcast.278), channel_id=1, source_target_pairs={{1,0},{2,1},{3,2},{4,3},{5,4},{6,5},{7,6},{8,7},{9,8},{10,9},{11,1... | collective-permute-start | bytes 589832 | tf_op jit(solution)/shard_map/ppermute | solution.py:36
  384.6 26.9 %collective-permute-start.22 = (bf16[128,768]{0,1:T(8,128)(2,1)S(1)}, bf16[128,768]{0,1:T(8,128)(2,1)S(1)}, u32[]{:S(2)}, u32[]{:S(2)}) collective-permute-start(bf16[128,768]{0,1:T(8,128)(2,1)S(1)} %bitcast.277), channel_id=1, source_target_pairs={{7,0},{8,1},{9,2},{10,3},{11,4},{12,5},{13,6},{14,7},{15,8},{23,16... | collective-permute-start | bytes 589832 | tf_op jit(solution)/shard_map/ppermute | solution.py:36
  385.9 27.7 %collective-permute-start.21 = (bf16[128,768]{0,1:T(8,128)(2,1)S(1)}, bf16[128,768]{0,1:T(8,128)(2,1)S(1)}, u32[]{:S(2)}, u32[]{:S(2)}) collective-permute-start(bf16[128,768]{0,1:T(8,128)(2,1)S(1)} %bitcast.275), channel_id=1, source_target_pairs={{6,0},{7,1},{8,2},{9,3},{10,4},{11,5},{12,6},{13,7},{14,8},{15,9},... | collective-permute-start | bytes 589832 | tf_op jit(solution)/shard_map/ppermute | solution.py:36
  387.7 25.9 %collective-permute-start.20 = (bf16[128,768]{0,1:T(8,128)(2,1)S(1)}, bf16[128,768]{0,1:T(8,128)(2,1)S(1)}, u32[]{:S(2)}, u32[]{:S(2)}) collective-permute-start(bf16[128,768]{0,1:T(8,128)(2,1)S(1)} %bitcast.274), channel_id=1, source_target_pairs={{5,0},{6,1},{7,2},{8,3},{9,4},{10,5},{11,6},{12,7},{13,8},{14,9},{... | collective-permute-start | bytes 589832 | tf_op jit(solution)/shard_map/ppermute | solution.py:36
  393.2 24.6 %collective-permute-start.19 = (bf16[128,768]{0,1:T(8,128)(2,1)S(1)}, bf16[128,768]{0,1:T(8,128)(2,1)S(1)}, u32[]{:S(2)}, u32[]{:S(2)}) collective-permute-start(bf16[128,768]{0,1:T(8,128)(2,1)S(1)} %bitcast.272), channel_id=1, source_target_pairs={{4,0},{5,1},{6,2},{7,3},{8,4},{9,5},{10,6},{11,7},{12,8},{13,9},{1... | collective-permute-start | bytes 589832 | tf_op jit(solution)/shard_map/ppermute | solution.py:36
  394.5 23.3 %collective-permute-start.18 = (bf16[128,768]{0,1:T(8,128)(2,1)S(1)}, bf16[128,768]{0,1:T(8,128)(2,1)S(1)}, u32[]{:S(2)}, u32[]{:S(2)}) collective-permute-start(bf16[128,768]{0,1:T(8,128)(2,1)S(1)} %bitcast.271), channel_id=1, source_target_pairs={{3,0},{4,1},{5,2},{6,3},{7,4},{8,5},{9,6},{10,7},{11,8},{12,9},{13... | collective-permute-start | bytes 589832 | tf_op jit(solution)/shard_map/ppermute | solution.py:36
  411.4 7.9 collective-permute-start.17
  488.9 218.5 %reduce-scatter.9.cloned.1.call-start = ((), (), s32[]{:S(2)}) async-start(), calls=%async_computation.7 | async-start | bytes 28753920 | tf_op jit(solution)/shard_map/reduce_scatter | solution.py:44
  489.8 7.8 copy-start.18
  555.2 191.1 %reduce-scatter.7.cloned.1.call-start = ((), (), s32[]{:S(2)}) async-start(), calls=%async_computation.6 | async-start | bytes 5308416 | tf_op jit(solution)/shard_map/reduce_scatter | solution.py:296
  560.0 262.6 %reduce-scatter.11.cloned.1.call-start = ((), (), s32[]{:S(2)}) async-start(), calls=%async_computation.8 | async-start | bytes 14155776 | tf_op jit(solution)/shard_map/reduce_scatter | solution.py:275
  567.9 389.8 %all-reduce.4.cloned.1.call-start = ((), (), s32[]{:S(2)}) async-start(), calls=%async_computation.10 | async-start | bytes 13762560 | tf_op jit(solution)/shard_map/psum | solution.py:302
  823.7 10.5 %copy-start.37 = (f32[128]{0:T(128)S(1)}, f32[128]{0:T(128)}, u32[]{:S(2)}) copy-start(f32[128]{0:T(128)} %get-tuple-element.58) | copy-start | bytes 1540
  823.7 10.5 %copy-start.20 = (f32[128,1536]{1,0:T(8,128)S(1)}, f32[128,1536]{1,0:T(8,128)}, u32[]{:S(2)}) copy-start(f32[128,1536]{1,0:T(8,128)} %get-tuple-element.118) | copy-start | bytes 2359300
  823.7 10.5 %copy-start.30 = (f32[128]{0:T(128)S(1)}, f32[128]{0:T(128)}, u32[]{:S(2)}) copy-start(f32[128]{0:T(128)} %copy-done.29) | copy-start | bytes 1540
  957.6 4.5 copy-start.26
  957.6 5.5 copy-start.25
  957.6 6.6 copy-start.11
  (13 other events, 20.2 us)
Sparse Core Ops, SparseCore 0:
  12.7 79.4 all-gather.2
  93.8 177.3 all-gather.4
  489.0 78.0 reduce-scatter.12
  569.5 137.8 reduce-scatter.8
  709.8 36.4 reduce-scatter.6
  748.7 73.7 reduce-scatter.10
  828.6 128.9 all-reduce.3
where the time goes:
time: 991 us; the launch traced here: 978 us
  waiting for transfers between devices  499 us (50%)
  local copies, waits for them, and re-layouts  184 us (19%)
  matrix products  150 us (15%)
  starting transfers between devices  65.7 us (7%)
  blocking collectives  34.8 us (4%)
  other arithmetic  27.7 us (3%)
  between operations  16.3 us (2%)
    reduce_scatter x1, waiting for transfers between devices, in_one_piece(): out = lax.psum_scatter(both, axis, scatter_dimension=dim, tiled=True)  134 us
    all_gather x2, waiting for transfers between devices, turned_gather(): out = lax.all_gather(both, axis, axis=0, tiled=True)  112 us
    concatenate x2, local copies, waits for them, and re-layouts, in_one_piece(): jnp.concatenate([a.reshape(*a.shape[:along], w) for a, w in zip(arrays, w...  97.2 us
    psum x1, waiting for transfers between devices, on_device(): lax.psum(attn_rows[1].astype(jnp.bfloat16), 'ctx').astype(jnp.float32)  84.7 us
    reduce_scatter x1, waiting for transfers between devices, on_device(): lax.psum_scatter(dw_down.astype(jnp.bfloat16), 'dp', scatter_dimension=1,...  76.2 us
    ppermute x32, starting transfers between devices, passed_along(): return lax.ppermute(block, axis, route)  65 us
    ppermute x32, waiting for transfers between devices, passed_along(): return lax.ppermute(block, axis, route)  58.6 us
    dot_general x7, matrix products, times_trans(): lax.dot_general(left, right, (((1,), (1,)), ((), ())), preferred_element_...  42.5 us
  transfers between devices with their start and end apart: 39, of which 19 were waited for; matrix products, arithmetic and copies ran while one was open for 19% of the time, Pallas kernels for 0%

commit v1 on v0

v1 whole, which is shorter than its diff:
```python
import functools

import jax
import jax.numpy as jnp
from jax import lax
from jax.experimental import pallas as pl
from jax.experimental.pallas import tpu as pltpu
from jax.sharding import PartitionSpec as P

HQ = 16
HK = 8
HD = 96
WINDOW = 1024
D = 1536
FF = 4096
BLOCK = 128
LENGTH = 2048
DP = 8
CTX = 16
ZN = 4
SHARD = D // DP
FSH = FF // DP
GROUP = 4 * HD

EPSILON = 1e-05
THETA_BASE = 100000.0
NEG_LARGE = -1e30

BF = jnp.bfloat16
F32 = jnp.float32
MESH = pl.DeviceIdType.MESH
ANY = pl.BlockSpec(memory_space=pl.ANY)
VMEM = pl.BlockSpec(memory_space=pltpu.VMEM)


def mod(a, n):
    return lax.rem(a + n, n)


class Place:
    def __init__(self):
        self.dp = lax.axis_index("dp")
        self.ctx = lax.axis_index("ctx")
        self.z, self.core = self.dp // 2, lax.rem(self.dp, 2)
        self.y, self.x = self.ctx // 4, lax.rem(self.ctx, 4)

    def at_x(self, k):
        return (self.dp, self.y * 4 + mod(self.x + k, 4))

    def at_y(self, k):
        return (self.dp, mod(self.y + k, 4) * 4 + self.x)

    def at_z(self, k):
        return (mod(self.z + k, 4) * 2 + self.core, self.ctx)

    def at_dp(self, k):
        return (mod(self.dp + k, DP), self.ctx)

    def at_ctx(self, k):
        return (self.dp, mod(self.ctx + k, CTX))

    def sibling(self):
        return (self.z * 2 + 1 - self.core, self.ctx)


class Net:
    def __init__(self, send, recv, local):
        self.send, self.recv, self.local = send, recv, local
        self.n, self.m = 0, 0

    def remote(self, src, dst, peer):
        copy = pltpu.make_async_remote_copy(
            src_ref=src,
            dst_ref=dst,
            send_sem=self.send.at[self.n],
            recv_sem=self.recv.at[self.n],
            device_id=peer,
            device_id_type=MESH,
        )
        self.n += 1
        copy.start()
        return copy

    def copy(self, src, dst):
        copy = pltpu.make_async_copy(src, dst, self.local.at[self.m])
        self.m += 1
        copy.start()
        return copy


def greet(peers):
    barrier = pltpu.get_barrier_semaphore()
    for peer in peers:
        pl.semaphore_signal(barrier, inc=1, device_id=peer, device_id_type=MESH)
    pl.semaphore_wait(barrier, len(peers))


def xy_peers(p):
    return [p.at_x(k) for k in (1, 2, 3)] + [p.at_y(k) for k in (1, 2, 3)]


def z_peers(p):
    return [p.at_z(k) for k in (1, 2, 3)] + [p.sibling()]


class GatherXY:
    def __init__(self, net, p, own, slot):
        self.net, self.p, self.slot = net, p, slot
        self.kept = [net.copy(own(h), slot(h, p.y, p.x)) for h in (0, 1)]
        self.first, self.rest = {}, []
        for k in (1, 2, 3):
            for h in (0, 1):
                here = slot(h, p.y, p.x)
                along = net.remote(own(h), here, p.at_x(k) if h == 0 else p.at_y(k))
                self.first[h, k] = along
        for k in (1, 2, 3):
            for h in (0, 1):
                here = slot(h, p.y, p.x)
                self.rest.append(net.remote(own(h), here, p.at_y(k) if h == 0 else p.at_x(k)))

    def forward(self):
        net, p = self.net, self.p
        for k in (1, 3, 2):
            for h in (0, 1):
                self.first[h, k].wait_recv()
                if h == 0:
                    block = self.slot(0, p.y, mod(p.x - k, 4))
                else:
                    block = self.slot(1, mod(p.y - k, 4), p.x)
                for m in (1, 2, 3):
                    self.rest.append(net.remote(block, block, p.at_y(m) if h == 0 else p.at_x(m)))

    def end(self):
        for copy in self.first.values():
            copy.wait_send()
        for copy in self.rest:
            copy.wait()
        for copy in self.kept:
            copy.wait()


class GatherDP:
    def __init__(self, net, p, own, slot):
        self.net, self.p, self.slot = net, p, slot
        here = slot(p.dp)
        self.kept = net.copy(own, here)
        self.first = {k: net.remote(own, here, p.at_z(k)) for k in (1, 3, 2)}
        self.rest = [net.remote(own, here, p.sibling())]

    def forward(self):
        net, p = self.net, self.p
        for k in (1, 3, 2):
            self.first[k].wait_recv()
            block = self.slot(mod(p.z - k, 4) * 2 + p.core)
            self.rest.append(net.remote(block, block, p.sibling()))

    def end(self):
        for copy in self.first.values():
            copy.wait_send()
        for copy in self.rest:
            copy.wait()
        self.kept.wait()


class Exchange:
    def __init__(self, net, p, src, slot):
        self.kept = net.copy(src(p.dp), slot(p.dp))
        self.sent = [net.remote(src(mod(p.dp + k, DP)), slot(p.dp), p.at_dp(k)) for k in range(1, DP)]

    def end(self):
        for copy in self.sent:
            copy.wait()
        self.kept.wait()


def add_rows(out, terms):
    rows = out.shape[0]

    def step(r, carry):
        at = pl.ds(pl.multiple_of(r * 16, 16), 16)
        total = terms[0][at, :].astype(F32)
        for term in terms[1:]:
            total = total + term[at, :].astype(F32)
        out[at, :] = total.astype(out.dtype)
        return carry

    lax.fori_loop(0, rows // 16, step, 0)


class ScatterDP:
    def __init__(self, net, p, part, mine, sib, got, out):
        self.net, self.p = net, p
        self.mine, self.sib, self.got, self.out = mine, sib, got, out
        self.loads = [net.copy(part(2 * z + p.core), mine.at[z]) for z in range(ZN)]
        self.swaps = [net.remote(part(2 * z + 1 - p.core), sib.at[z], p.sibling()) for z in range(ZN)]

    def forward(self):
        net, p = self.net, self.p
        self.sent = []
        for copy in self.loads + self.swaps:
            copy.wait()
        for k in (2, 1, 3, 0):
            z = mod(p.z + k, 4)
            block = self.mine.at[z]
            add_rows(block, [block, self.sib.at[z]])
            if k:
                self.sent.append(net.remote(block, self.got.at[k - 1], p.at_z(k)))

    def end(self):
        for copy in self.sent:
            copy.wait()
        add_rows(self.out, [self.mine.at[self.p.z]] + [self.got.at[k] for k in range(3)])


class ScatterXY:
    def __init__(self, net, p, cut, first, second, wide, piece, along):
        self.net, self.p, self.along = net, p, along
        self.first, self.second, self.wide, self.piece = first, second, wide, piece
        self.loads = [
            net.copy(cut(0, None, p.x), wide[0]),
            net.copy(cut(1, p.y, None), wide[1]),
        ]
        self.sent = []
        for k in (1, 3, 2):
            self.sent.append(net.remote(cut(0, None, mod(p.x + k, 4)), first[0].at[k - 1], p.at_x(k)))
            self.sent.append(net.remote(cut(1, mod(p.y + k, 4), None), first[1].at[k - 1], p.at_y(k)))

    def forward(self):
        net, p = self.net, self.p
        for copy in self.loads + self.sent:
            copy.wait()
        self.sent = []
        for h in (0, 1):
            add_all(self.wide[h], [self.wide[h]] + [self.first[h].at[k] for k in range(3)])
            for k in (1, 3, 2):
                block = self.along(h, self.wide[h], mod((p.y if h == 0 else p.x) + k, 4))
                peer = p.at_y(k) if h == 0 else p.at_x(k)
                self.sent.append(net.remote(block, self.second[h].at[k - 1], peer))

    def end(self):
        p = self.p
        for copy in self.sent:
            copy.wait()
        for h in (0, 1):
            own = self.along(h, self.wide[h], p.y if h == 0 else p.x)
            add_all(self.piece(h), [own] + [self.second[h].at[k] for k in range(3)])


def add_all(out, terms):
    lead = out.shape[:-2]
    if not lead:
        return add_rows(out, terms)
    count = 1
    for n in lead:
        count *= n
    rows = out.shape[-2] // 16

    def step(i, carry):
        j, r = i // rows, lax.rem(i, rows)
        index = []
        for n in reversed(lead):
            index.insert(0, lax.rem(j, n))
            j = j // n
        at = (*index, pl.ds(pl.multiple_of(r * 16, 16), 16), slice(None))
        total = terms[0][at].astype(F32)
        for term in terms[1:]:
            total = total + term[at].astype(F32)
        out[at] = total.astype(out.dtype)
        return carry

    lax.fori_loop(0, count * rows, step, 0)


def call(body, ident, outs, out_places, remotes, locals_, scratch, *args, vmem=56):
    return pl.pallas_call(
        body,
        out_shape=outs,
        in_specs=[ANY] * len(args),
        out_specs=out_places,
        scratch_shapes=[
            *scratch,
            pltpu.SemaphoreType.DMA((remotes,)),
            pltpu.SemaphoreType.DMA((remotes,)),
            pltpu.SemaphoreType.DMA((locals_,)),
        ],
        compiler_params=pltpu.CompilerParams(
            collective_id=ident, has_side_effects=True, vmem_limit_bytes=vmem << 20
        ),
    )(*args)


def shape(*dims, dtype=BF):
    return jax.ShapeDtypeStruct(dims, dtype)


def half(ref, h, n=64):
    return ref.at[pl.ds(h * n, n)]


def first_exchange(h1, pos, wgrp, w_out_t, wpiece):
    def body(h1, pos, wgrp, w_out_t, wpiece, seq, posq, wjob, wdh, wo, wfp, send, recv, local):
        p = Place()
        net = Net(send, recv, local)
        greet(xy_peers(p) + [p.at_dp(k) for k in range(1, DP)])
        rows = GatherXY(
            net, p, lambda h: half(h1, h), lambda h, y, x: seq.at[y * 4 + x, pl.ds(h * 64, 64)]
        )
        spots = GatherXY(
            net, p, lambda h: half(pos, h, 8), lambda h, y, x: posq.at[y * 4 + x, pl.ds(h * 8, 8)]
        )
        job = GatherDP(net, p, wgrp.at[p.ctx // 2], lambda i: wjob.at[i])
        ffw = Exchange(net, p, lambda i: wpiece.at[i], lambda i: wfp.at[:, i])
        out = GatherDP(net, p, w_out_t, lambda i: wo.at[i])
        grp = Exchange(net, p, lambda i: wgrp.at[i], lambda i: wdh.at[i])
        spots.forward()
        job.forward()
        rows.forward()
        out.forward()
        for part in (rows, spots, job, ffw, out, grp):
            part.end()

    return call(
        body,
        1,
        (
            shape(CTX, BLOCK, D),
            shape(CTX, 16, BLOCK, dtype=F32),
            shape(DP, SHARD, GROUP),
            shape(DP, SHARD, GROUP),
            shape(DP, SHARD, D),
            shape(3, DP, 48, 128),
        ),
        [ANY] * 6,
        90,
        8,
        [],
        h1,
        pos,
        wgrp,
        w_out_t,
        wpiece,
    )


def heads_home(att):
    def body(att, out, send, recv, local):
        p = Place()
        net = Net(send, recv, local)
        greet([p.at_ctx(k) for k in range(1, CTX)])
        lanes = lambda c: pl.ds(pl.multiple_of(c * BLOCK, BLOCK), BLOCK)
        kept = net.copy(att.at[:, lanes(p.ctx)], out.at[p.ctx])
        sent = [
            net.remote(att.at[:, lanes(mod(p.ctx + k, CTX))], out.at[p.ctx], p.at_ctx(k))
            for k in range(1, CTX)
        ]
        for copy in sent:
            copy.wait()
        kept.wait()

    return call(body, 2, shape(CTX, HD, BLOCK), ANY, 15, 1, [], att)


def middle_exchange(h2, dd, wfp):
    def body(h2, dd, wfp, h2_all, dd_all, wf, send, recv, local):
        p = Place()
        net = Net(send, recv, local)
        greet(xy_peers(p) + z_peers(p))
        hid = GatherDP(net, p, h2, lambda i: h2_all.at[i])
        wts = GatherXY(
            net,
            p,
            lambda h: wfp.at[:, pl.ds(4 * h, 4)],
            lambda h, y, x: wf.at[
                :,
                pl.ds(4 * h, 4),
                pl.ds(pl.multiple_of(y * 48, 16), 48),
                pl.ds(pl.multiple_of(x * 128, 128), 128),
            ],
        )
        hid.forward()
        cot = GatherDP(net, p, dd, lambda i: dd_all.at[i])
        wts.forward()
        cot.forward()
        for part in (hid, cot, wts):
            part.end()

    return call(
        body,
        3,
        (shape(DP, BLOCK, D), shape(DP, BLOCK, D), shape(3, DP, SHARD, FSH)),
        [ANY] * 3,
        46,
        4,
        [],
        h2,
        dd,
        wfp,
    )


def scatter_dp_scratch():
    return [
        pltpu.VMEM((ZN, BLOCK, D), BF),
        pltpu.VMEM((ZN, BLOCK, D), BF),
        pltpu.VMEM((3, BLOCK, D), BF),
    ]


def back_exchange(dh2, dwf):
    def body(dh2, dwf, out, piece, mine, sib, got, f0, f1, s0, s1, w0, w1, send, recv, local):
        p = Place()
        net = Net(send, recv, local)
        greet(xy_peers(p) + z_peers(p))
        hid = ScatterDP(net, p, lambda i: dh2.at[i], mine, sib, got, out)

        def cut(h, y, x):
            rows = slice(None) if y is None else pl.ds(pl.multiple_of(y * 48, 16), 48)
            lanes = slice(None) if x is None else pl.ds(pl.multiple_of(x * 128, 128), 128)
            return dwf.at[:, pl.ds(4 * h, 4), rows, lanes]

        def along(h, ref, at):
            if h == 0:
                return ref.at[:, :, pl.ds(pl.multiple_of(at * 48, 16), 48), :]
            return ref.at[:, :, :, pl.ds(pl.multiple_of(at * 128, 128), 128)]

        wts = ScatterXY(
            net, p, cut, (f0, f1), (s0, s1), (w0, w1), lambda h: piece.at[:, pl.ds(4 * h, 4)], along
        )
        hid.forward()
        wts.forward()
        hid.end()
        wts.end()

    return call(
        body,
        4,
        (shape(BLOCK, D, dtype=F32), shape(3, DP, 48, 128)),
        [VMEM] * 2,
        20,
        6,
        [
            *scatter_dp_scratch(),
            pltpu.VMEM((3, 3, 4, SHARD, 128), BF),
            pltpu.VMEM((3, 3, 4, 48, FSH), BF),
            pltpu.VMEM((3, 3, 4, 48, 128), BF),
            pltpu.VMEM((3, 3, 4, 48, 128), BF),
            pltpu.VMEM((3, 4, SHARD, 128), BF),
            pltpu.VMEM((3, 4, 48, FSH), BF),
        ],
        dh2,
        dwf,
    )


def heads_out(dat, att, da_t, piece):
    def body(dat, att, da_t, piece, heads, att_all, da_all, grads, send, recv, local):
        p = Place()
        net = Net(send, recv, local)
        greet([p.at_ctx(k) for k in range(1, CTX)] + [p.at_dp(k) for k in range(1, DP)])
        kept = net.copy(dat.at[p.ctx], heads.at[p.ctx])
        sent = [
            net.remote(dat.at[mod(p.ctx + k, CTX)], heads.at[p.ctx], p.at_ctx(k))
            for k in range(1, CTX)
        ]
        atts = GatherDP(net, p, att, lambda i: att_all.at[i])
        das = Exchange(net, p, lambda i: da_t.at[i], lambda i: da_all.at[i])
        wts = Exchange(net, p, lambda i: piece.at[:, i], lambda i: grads.at[i])
        atts.forward()
        for copy in sent:
            copy.wait()
        kept.wait()
        for part in (atts, das, wts):
            part.end()

    return call(
        body,
        5,
        (
            shape(CTX, HD, BLOCK),
            shape(DP, D, BLOCK),
            shape(DP, SHARD, BLOCK),
            shape(DP, 3, 48, 128),
        ),
        [ANY] * 4,
        36,
        4,
        [],
        dat,
        att,
        da_t,
        piece,
    )


def grads_home(dqkv, dwj, dwo):
    def body(
        dqkv, dwj, dwo, out, pair, piece, full, mine, sib, got, away, f0, s0, w0, send, recv, local
    ):
        p = Place()
        net = Net(send, recv, local)
        group, rank = p.ctx // 2, lax.rem(p.ctx, 2)
        home = group == p.dp
        partner = (p.dp, p.ctx + 1 - 2 * rank)

        barrier = pltpu.get_barrier_semaphore()
        others = xy_peers(p) + z_peers(p)
        for peer in others:
            pl.semaphore_signal(barrier, inc=1, device_id=peer, device_id_type=MESH)
        for i in range(DP):
            for r in range(2):
                own = home & (p.dp == i) & (rank == r)

                @pl.when(jnp.logical_not(own))
                def _():
                    peer = (jnp.int32(i), 2 * p.dp + r)
                    pl.semaphore_signal(barrier, inc=1, device_id=peer, device_id_type=MESH)

        pl.semaphore_wait(barrier, CTX + len(others) - home.astype(jnp.int32))

        lanes = lambda c: pl.ds(pl.multiple_of(c * BLOCK, BLOCK), BLOCK)
        slot = p.dp * 2 + rank

        def message(k, spot):
            c = mod(p.ctx + k, CTX)
            return pltpu.make_async_remote_copy(
                src_ref=dqkv.at[:, lanes(c)],
                dst_ref=out.at[spot],
                send_sem=send.at[k],
                recv_sem=recv.at[spot],
                device_id=(group, c),
                device_id_type=MESH,
            )

        own = pltpu.make_async_copy(dqkv.at[:, lanes(p.ctx)], out.at[slot], local.at[0])
        net.m = 1

        @pl.when(home)
        def _():
            own.start()

        @pl.when(jnp.logical_not(home))
        def _():
            message(0, slot).start()

        for k in range(1, CTX):
            message(k, slot).start()
        net.n = CTX

        hid = ScatterDP(net, p, lambda i: dwj.at[i], mine, sib, got, full)
        wide = [net.copy(dwo.at[:, pl.ds(pl.multiple_of(p.x * 384, 128), 384)], w0)]
        for k in (1, 3, 2):
            cut = dwo.at[:, pl.ds(pl.multiple_of(mod(p.x + k, 4) * 384, 128), 384)]
            wide.append(net.remote(cut, f0.at[k - 1], p.at_x(k)))
        hid.forward()
        for copy in wide:
            copy.wait()
        add_rows(w0, [w0] + [f0.at[k] for k in range(3)])
        tall = []
        for k in (1, 3, 2):
            cut = w0.at[pl.ds(pl.multiple_of(mod(p.y + k, 4) * 48, 16), 48)]
            tall.append(net.remote(cut, s0.at[k - 1], p.at_y(k)))
        hid.end()
        theirs = full.at[pl.ds(pl.multiple_of((1 - rank) * 96, 16), 96)]
        swap = net.remote(theirs, away, partner)
        for copy in tall:
            copy.wait()
        add_rows(piece, [w0.at[pl.ds(pl.multiple_of(p.y * 48, 16), 48)]] + [s0.at[k] for k in range(3)])
        swap.wait()
        add_rows(pair, [full.at[pl.ds(pl.multiple_of(rank * 96, 16), 96)], away])

        for k in range(1, CTX):
            message(k, slot).wait_send()

        @pl.when(home)
        def _():
            own.wait()

        @pl.when(jnp.logical_not(home))
        def _():
            message(0, slot).wait_send()

        for spot in range(CTX):
            here = home & (slot == spot)

            @pl.when(jnp.logical_not(here))
            def _():
                message(0, spot).wait_recv()

    return call(
        body,
        6,
        (shape(CTX, 3 * HD, BLOCK), shape(96, GROUP), shape(48, 384)),
        [ANY, VMEM, VMEM],
        40,
        8,
        [
            pltpu.VMEM((SHARD, GROUP), BF),
            pltpu.VMEM((ZN, SHARD, GROUP), BF),
            pltpu.VMEM((ZN, SHARD, GROUP), BF),
            pltpu.VMEM((3, SHARD, GROUP), BF),
            pltpu.VMEM((96, GROUP), BF),
            pltpu.VMEM((3, SHARD, 384), BF),
            pltpu.VMEM((3, 48, 384), BF),
            pltpu.VMEM((SHARD, 384), BF),
        ],
        dqkv,
        dwj,
        dwo,
    )


def last_exchange(dh1, ypart, grads, pair, piece):
    def body(dh1, ypart, grads, pair, piece, e1, ysum, gff, gqkv, gout, *rest):
        scratch, (send, recv, local) = rest[:-3], rest[-3:]
        p = Place()
        net = Net(send, recv, local)
        greet(xy_peers(p) + z_peers(p))
        inp = ScatterDP(net, p, lambda i: dh1.at[i], *scratch[:3], e1)
        wts = GatherXY(
            net,
            p,
            lambda h: grads.at[pl.ds(4 * h, 4)],
            lambda h, y, x: gff.at[
                pl.ds(4 * h, 4),
                :,
                pl.ds(pl.multiple_of(y * 48, 16), 48),
                pl.ds(pl.multiple_of(x * 128, 128), 128),
            ],
        )
        qkv = GatherXY(
            net, p, lambda h: half(pair, h, 48), lambda h, y, x: gqkv.at[y * 4 + x, pl.ds(h * 48, 48)]
        )
        proj = GatherXY(
            net,
            p,
            lambda h: piece.at[pl.ds(32 * h, 32 - 16 * h)],
            lambda h, y, x: gout.at[
                pl.ds(pl.multiple_of(y * 48 + 32 * h, 16), 32 - 16 * h),
                pl.ds(pl.multiple_of(x * 384, 128), 384),
            ],
        )
        inp.forward()
        res = ScatterDP(net, p, lambda i: ypart.at[i], *scratch[3:6], ysum)
        wts.forward()
        qkv.forward()
        proj.forward()
        res.forward()
        inp.end()
        res.end()
        for part in (wts, qkv, proj):
            part.end()

    return call(
        body,
        7,
        (
            shape(BLOCK, D, dtype=F32),
            shape(BLOCK, D, dtype=F32),
            shape(DP, 3, SHARD, FSH),
            shape(CTX, 96, GROUP),
            shape(SHARD, D),
        ),
        [VMEM, VMEM, ANY, ANY, ANY],
        110,
        16,
        scatter_dp_scratch() + scatter_dp_scratch(),
        dh1,
        ypart,
        grads,
        pair,
        piece,
    )


CHUNK = 256
CHUNKS = LENGTH // CHUNK
SCALE = HD ** (-0.5)


def span(j):
    return max(0, j * CHUNK - WINDOW), (j + 1) * CHUNK


def score_block(k, q_t, hi, j):
    low, high = span(j)
    s = jnp.dot(k[low:high, :], q_t[:, j * CHUNK : (j + 1) * CHUNK], preferred_element_type=F32)
    s = s * SCALE
    key = low + lax.broadcasted_iota(jnp.int32, s.shape, 0)
    query = j * CHUNK + lax.broadcasted_iota(jnp.int32, s.shape, 1)
    last = hi[low:high, :]
    last = jnp.concatenate([last] * (CHUNK // 128), axis=1)
    return jnp.where((query >= key) & (query <= last), s, NEG_LARGE)


def attend(q_t, k_t, v_t, hi):
    def body(q_t, k_t, v_t, hi, out, top, total, k):
        k[...] = k_t[...].T
        for j in range(CHUNKS):
            low, high = span(j)
            at = slice(j * CHUNK, (j + 1) * CHUNK)
            s = score_block(k, q_t, hi, j)
            m = jnp.max(s, axis=0, keepdims=True)
            e = jnp.exp(s - m)
            t = jnp.sum(e, axis=0, keepdims=True)
            prob = (e * (1.0 / t)).astype(BF)
            o = jnp.dot(v_t[:, low:high], prob, preferred_element_type=F32)
            out[:, at] = o.astype(BF)
            top[:, at] = m
            total[:, at] = t

    return pl.pallas_call(
        body,
        out_shape=(shape(HD, LENGTH), shape(1, LENGTH, dtype=F32), shape(1, LENGTH, dtype=F32)),
        in_specs=[VMEM] * 4,
        out_specs=[VMEM] * 3,
        scratch_shapes=[pltpu.VMEM((LENGTH, HD), BF)],
        compiler_params=pltpu.CompilerParams(vmem_limit_bytes=56 << 20),
        cost_estimate=pl.CostEstimate(flops=800_000_000, bytes_accessed=4 << 20, transcendentals=2_000_000),
    )(q_t, k_t, v_t, hi)


def attend_back(q_t, k_t, v_t, do_blocks, hi, top, total):
    def body(q_t, k_t, v_t, do_blocks, hi, top, total, dq, dk_t, dv_t, k, v, q, do, do_t, dk, dv):
        k[...] = k_t[...].T
        v[...] = v_t[...].T
        q[...] = q_t[...].T
        for b in range(CTX):
            do_t[:, b * BLOCK : (b + 1) * BLOCK] = do_blocks[b]
        do[...] = do_t[...].T
        dk[...] = jnp.zeros_like(dk)
        dv[...] = jnp.zeros_like(dv)
        for j in range(CHUNKS):
            low, high = span(j)
            at = slice(j * CHUNK, (j + 1) * CHUNK)
            s = score_block(k, q_t, hi, j)
            prob = jnp.exp(s - top[:, at]) * (1.0 / total[:, at])
            dp = jnp.dot(v[low:high, :], do_t[:, at], preferred_element_type=F32)
            inner = jnp.sum(prob * dp, axis=0, keepdims=True)
            ds = (prob * (dp - inner)).astype(BF)
            dq[:, at] = jnp.dot(k_t[:, low:high], ds, preferred_element_type=F32) * SCALE
            dk[low:high, :] += jnp.dot(ds, q[at, :], preferred_element_type=F32)
            dv[low:high, :] += jnp.dot(prob.astype(BF), do[at, :], preferred_element_type=F32)
        dk_t[...] = dk[...].T * SCALE
        dv_t[...] = dv[...].T

    return pl.pallas_call(
        body,
        out_shape=(shape(HD, LENGTH, dtype=F32),) * 3,
        in_specs=[VMEM] * 7,
        out_specs=[VMEM] * 3,
        scratch_shapes=[
            pltpu.VMEM((LENGTH, HD), BF),
            pltpu.VMEM((LENGTH, HD), BF),
            pltpu.VMEM((LENGTH, HD), BF),
            pltpu.VMEM((LENGTH, HD), BF),
            pltpu.VMEM((HD, LENGTH), BF),
            pltpu.VMEM((LENGTH, HD), F32),
            pltpu.VMEM((LENGTH, HD), F32),
        ],
        compiler_params=pltpu.CompilerParams(vmem_limit_bytes=56 << 20),
        cost_estimate=pl.CostEstimate(flops=2_000_000_000, bytes_accessed=6 << 20, transcendentals=2_000_000),
    )(q_t, k_t, v_t, do_blocks, hi, top, total)


def dot(left, right, contract):
    return lax.dot_general(left, right, (contract, ((), ())), preferred_element_type=F32)


def turn(values, cosine, sine):
    a, b = values[: HD // 2], values[HD // 2 :]
    return jnp.concatenate([a * cosine - b * sine, b * cosine + a * sine], axis=0)


def on_device(
    layer_input,
    cotangent,
    attn_gain,
    w_query,
    w_key,
    w_value,
    w_out,
    mlp_gain,
    w_gate,
    w_up,
    w_down,
    doc_lengths,
    rope_pos,
    pad_lengths,
):
    ctx = lax.axis_index("ctx")
    row, col = ctx // 4, lax.rem(ctx, 4)
    rank = lax.rem(ctx, 2)
    gain_a = attn_gain.astype(F32)
    gain_m = mlp_gain.astype(F32)

    inputs = layer_input[0].astype(F32)
    inv_one = lax.rsqrt(jnp.mean(inputs * inputs, axis=-1, keepdims=True) + EPSILON)
    u1 = inputs * inv_one

    wgrp = jnp.concatenate(
        [w_query.reshape(SHARD, HK, 2 * HD), w_key.reshape(SHARD, HK, HD), w_value.reshape(SHARD, HK, HD)],
        axis=2,
    )
    wgrp = (wgrp.astype(F32) * gain_a[:, None, None]).astype(BF).transpose(1, 0, 2)
    w_out_t = w_out.T

    def wide_piece(w):
        rows = lax.dynamic_slice_in_dim(w, row * 48, 48, 0).reshape(48, DP, 4, 128)
        return lax.dynamic_slice_in_dim(rows, col, 1, 2)[:, :, 0].transpose(1, 0, 2)

    gains = lax.dynamic_slice_in_dim(gain_m, row * 48, 48, 0)[None, :, None]
    down = lax.dynamic_slice_in_dim(w_down.reshape(DP, 4, 128, SHARD), col, 1, 1)[:, 0]
    down = lax.dynamic_slice_in_dim(down, row * 48, 48, 2).transpose(0, 2, 1)
    wpiece = jnp.stack(
        [
            (wide_piece(w_gate).astype(F32) * gains).astype(BF),
            (wide_piece(w_up).astype(F32) * gains).astype(BF),
            down,
        ],
        axis=1,
    )
    pos = jnp.broadcast_to(rope_pos.astype(F32), (16, BLOCK))

    seq, posq, wjob, wdh, wo, wfp = first_exchange(u1.astype(BF), pos, wgrp, w_out_t, wpiece)
    seq = seq.reshape(LENGTH, D)
    wo = wo.reshape(D, D)

    freq = THETA_BASE ** (-(jnp.arange(HD // 2).astype(F32) * 2.0 / HD))
    angles = freq[:, None] * posq[:, 0, :].reshape(1, LENGTH)
    cosine, sine = jnp.cos(angles), jnp.sin(angles)

    ends = jnp.cumsum(doc_lengths[0])
    token = jnp.arange(LENGTH, dtype=jnp.int32)
    seg = jnp.sum(token[:, None] >= ends[None, :], axis=-1)
    doc_end = jnp.sum(jnp.where(seg[:, None] == jnp.arange(4)[None, :], ends[None, :], 0), axis=-1)
    hi = jnp.minimum(token + WINDOW - 1, doc_end - 1)
    hi = jnp.where(token >= LENGTH - pad_lengths[0], token, hi)
    hi = jnp.broadcast_to(hi[:, None], (LENGTH, 128)).astype(jnp.int32)

    proj = dot(wjob.reshape(D, GROUP), seq, ((0,), (1,)))
    q_t = turn(lax.dynamic_slice_in_dim(proj, rank * HD, HD, 0), cosine, sine).astype(BF)
    k_t = turn(proj[2 * HD : 3 * HD], cosine, sine).astype(BF)
    v_t = proj[3 * HD :].astype(BF)
    att_t, top, total = attend(q_t, k_t, v_t, hi)

    att = heads_home(att_t).reshape(D, BLOCK)
    resid = inputs + dot(att, wo, ((0,), (1,)))
    inv_two = lax.rsqrt(jnp.mean(resid * resid, axis=-1, keepdims=True) + EPSILON)
    u2 = resid * inv_two
    dd = cotangent[0]

    hid, cot, wf = middle_exchange(u2.astype(BF), dd, wfp)
    hid = hid.reshape(DP * BLOCK, D)
    cot = cot.reshape(DP * BLOCK, D)
    wf = wf.reshape(3, D, FSH)
    gate = dot(hid, wf[0], ((1,), (0,)))
    up = dot(hid, wf[1], ((1,), (0,)))
    sig = jax.nn.sigmoid(gate)
    act = gate * sig
    mixed = (act * up).astype(BF)
    dmix = dot(cot, wf[2], ((1,), (0,)))
    dgate = (dmix * up * sig * (1.0 + gate * (1.0 - sig))).astype(BF)
    dup = (dmix * act).astype(BF)
    ypart = dot(mixed, wf[2], ((1,), (1,))).astype(BF).reshape(DP, BLOCK, D)
    epart = dot(dgate, wf[0], ((1,), (1,))) + dot(dup, wf[1], ((1,), (1,)))
    dwf = jnp.stack(
        [
            dot(hid, dgate, ((0,), (0,))).astype(BF),
            dot(hid, dup, ((0,), (0,))).astype(BF),
            dot(cot, mixed, ((0,), (0,))).astype(BF),
        ]
    ).reshape(3, DP, SHARD, FSH)

    e2, piece = back_exchange(epart.astype(BF).reshape(DP, BLOCK, D), dwf)
    dy = dd.astype(F32)
    dresid = dy + inv_two * (e2 - u2 * jnp.mean(e2 * u2, axis=-1, keepdims=True))
    da = dresid.astype(BF)
    dat = dot(wo, da, ((0,), (1,))).astype(BF).reshape(CTX, HD, BLOCK)
    da_t = da.T.reshape(DP, SHARD, BLOCK)

    do_blocks, att_all, da_all, grads = heads_out(dat, att, da_t, piece)
    dq, dk, dv = attend_back(q_t, k_t, v_t, do_blocks, hi, top, total)
    dq = turn(dq, cosine, -sine).astype(BF)
    dk = turn(dk, cosine, -sine).astype(BF)
    dv = dv.astype(BF)
    none = jnp.zeros_like(dq)
    wide = jnp.concatenate(
        [jnp.where(rank == 0, dq, none), jnp.where(rank == 1, dq, none), dk, dv], axis=0
    )
    dwj = dot(seq, wide, ((0,), (1,))).astype(BF).reshape(DP, SHARD, GROUP)
    dwo = dot(da_all, att_all, ((0, 2), (0, 2))).astype(BF)

    back, pair, opiece = grads_home(jnp.concatenate([dq, dk, dv], axis=0), dwj, dwo)
    back = back.reshape(DP, 2, 3 * HD, BLOCK)
    both = back[:, 0, HD:].astype(F32) + back[:, 1, HD:].astype(F32)
    group = jnp.concatenate([back[:, 0, :HD], back[:, 1, :HD], both.astype(BF)], axis=1)
    dh1 = lax.dot_general(
        group.transpose(0, 2, 1).reshape(DP * BLOCK, GROUP),
        wdh.reshape(D, GROUP),
        (((1,), (1,)), ((), ())),
        preferred_element_type=F32,
    )

    e1, ysum, gff, gqkv, gout = last_exchange(
        dh1.astype(BF).reshape(DP, BLOCK, D), ypart, grads, pair, opiece
    )
    output = (resid + ysum).astype(BF)
    grad_in = dresid + inv_one * (e1 - u1 * jnp.mean(e1 * u1, axis=-1, keepdims=True))

    gqkv = gqkv.reshape(HK, 2 * 96, GROUP).astype(F32).transpose(1, 0, 2)
    dwq = gqkv[:, :, : 2 * HD].reshape(SHARD, D)
    dwk = gqkv[:, :, 2 * HD : 3 * HD].reshape(SHARD, HK * HD)
    dwv = gqkv[:, :, 3 * HD :].reshape(SHARD, HK * HD)
    dgain_a = (
        jnp.sum(dwq * w_query.astype(F32), axis=1)
        + jnp.sum(dwk * w_key.astype(F32), axis=1)
        + jnp.sum(dwv * w_value.astype(F32), axis=1)
    )
    gff = gff.astype(F32)
    dwg = gff[:, 0].transpose(1, 0, 2).reshape(SHARD, FF)
    dwu = gff[:, 1].transpose(1, 0, 2).reshape(SHARD, FF)
    dwd = gff[:, 2].transpose(0, 2, 1).reshape(FF, SHARD)
    dgain_m = jnp.sum(dwg * w_gate.astype(F32), axis=1) + jnp.sum(dwu * w_up.astype(F32), axis=1)
    rows_a, rows_m = gain_a[:, None], gain_m[:, None]
    return (
        output[None],
        grad_in.astype(BF)[None],
        dgain_a,
        dwq * rows_a,
        dwk * rows_a,
        dwv * rows_a,
        gout.astype(F32).T,
        dgain_m,
        dwg * rows_m,
        dwu * rows_m,
        dwd,
    )


def solution(mesh):
    in_specs = (
        P("dp", "ctx", None),
        P("dp", "ctx", None),
        P("dp"),
        P("dp", None),
        P("dp", None),
        P("dp", None),
        P(None, "dp"),
        P("dp"),
        P("dp", None),
        P("dp", None),
        P(None, "dp"),
        P("dp", None),
        P("dp", "ctx"),
        P("dp"),
    )
    out_specs = (
        P("dp", "ctx", None),
        P("dp", "ctx", None),
        P("dp"),
        P("dp", None),
        P("dp", None),
        P("dp", None),
        P(None, "dp"),
        P("dp"),
        P("dp", None),
        P("dp", None),
        P(None, "dp"),
    )
    return jax.shard_map(
        on_device, mesh=mesh, in_specs=in_specs, out_specs=out_specs, check_vma=False
    )
```

time: 991 us -> 442 us (0.45)
  waiting for transfers between devices: 499 us -> 0 us
  Pallas kernels: 0 us -> 300 us
  local copies, waits for them, and re-layouts: 184 us -> 40.3 us
  matrix products: 150 us -> 48.2 us
  starting transfers between devices: 65.7 us -> 0 us
  blocking collectives: 34.8 us -> 0 us
  other arithmetic: 27.7 us -> 44.2 us
  between operations: 16.3 us -> 2.4 us
    pallas_call x0 -> x9, Pallas kernels: none -> 300 us  [the longest x7 280 us: call(): pl.pallas_call(body, out_shape=outs, in_specs=[ANY] * len(args), out_spec...]
    reduce_scatter x3 -> x0, waiting for transfers between devices: 244 us -> none  [the longest x1 134 us: in_one_piece(): out = lax.psum_scatter(both, axis, scatter_dimension=dim, tiled=True)]
    concatenate x6 -> x0, local copies, waits for them, and re-layouts: 113 us -> none  [the longest x2 97.2 us: in_one_piece(): jnp.concatenate([a.reshape(*a.shape[:along], w) for a, w in zip(arrays, w...]
    all_gather x2 -> x0, waiting for transfers between devices: 112 us -> none  [turned_gather(): out = lax.all_gather(both, axis, axis=0, tiled=True)]
    dot_general x26 -> x15, matrix products: 144 us -> 48.2 us  [the longest x14 43.3 us: dot(): lax.dot_general(left, right, (contract, ((), ())), preferred_element_type...]
    psum x1 -> x0, waiting for transfers between devices: 84.7 us -> none  [on_device(): lax.psum(attn_rows[1].astype(jnp.bfloat16), 'ctx').astype(jnp.float32)]
    ppermute x32 -> x0, starting transfers between devices: 65 us -> none  [passed_along(): return lax.ppermute(block, axis, route)]
    ppermute x32 -> x0, waiting for transfers between devices: 58.6 us -> none  [passed_along(): return lax.ppermute(block, axis, route)]
  transfers between devices with their start and end apart: 39 -> 0, of which waited for: 19 -> 0; matrix products, arithmetic and copies ran while one was open for 19% -> 0% of each run, Pallas kernels for 0% -> 0%
where the time goes in v1:
time: 442 us; the launch traced here: 435 us
  Pallas kernels  300 us (68%)
  matrix products  48.2 us (11%)
  other arithmetic  44.2 us (10%)
  local copies, waits for them, and re-layouts  40.3 us (9%)
    pallas_call x7, Pallas kernels, call(): pl.pallas_call(body, out_shape=outs, in_specs=[ANY] * len(args), out_spec...  280 us
    dot_general x14, matrix products, dot(): lax.dot_general(left, right, (contract, ((), ())), preferred_element_type...  43.3 us
    unnamed x6, other arithmetic  11.9 us
    pallas_call x1, Pallas kernels, attend_back(): pl.pallas_call(body, out_shape=(shape(HD, LENGTH, dtype=F32),) * 3, in_sp...  10.9 us

profile of v1, /device:TPU:1, one launch (start us, length us, event | category | flops | bytes accessed | tf_op | source)
XLA Modules:
  0.0 434.9 jit_solution(13346217345377768307)
XLA Ops:
  0.7 1.0 constant_dynamic-slice_fusion.4
  2.0 1.0 constant_dynamic-slice_fusion.2
  3.9 2.9 reshape.211
  9.7 1.6 fusion.2.wgrp
  11.5 0.9 fusion.5.h1
  13.0 58.0 %shard_map.221 = (bf16[16,128,1536]{2,1,0:T(8,128)(2,1)}, f32[16,16,128]{2,1,0:T(8,128)}, bf16[8,192,384]{2,1,0:T(8,128)(2,1)}, bf16[8,192,384]{2,1,0:T(8,128)(2...) custom-call(bf16[128,1536]{1,0:T(8,128)(2,1)} %fusion.5.h1, f32[16,128]{1,0:T(8,128)} %broadcast_in_dim.23.pos, ...), custom_call_target="tpu_custom_call" | custom-call | tf_op jit(solution)/shard_map/pallas_call | solution.py:275
  71.0 5.1 %fusion.61 = f32[384,2048]{1,0:T(8,128)S(1)} fusion(bf16[1536,384]{1,0:T(8,128)(2,1)} %bitcast.187, bf16[2048,1536]{1,0:T(8,128)(2,1)} %bitcast.178), kind=kOutput, calls=%fused_computation.138 | convolution fusion | flops 2415919104 | bytes 10616832 | tf_op jit(solution)/shard_map/dot_general | solution.py:766
  76.1 0.8 slice.80
  77.0 2.0 fusion.43
  81.3 0.8 reduce-window.8
  83.0 1.3 broadcast_in_dim.25.hi
  84.3 8.8 %shard_map.222 = (bf16[96,2048]{1,0:T(8,128)(2,1)}, f32[1,2048]{1,0:T(1,128)}, f32[1,2048]{1,0:T(1,128)}) custom-call(bf16[96,2048]{1,0:T(8,128)(2,1)} %pad_maximum_fusion.2.q_t, bf16[96,2048]{1,0:T(8,128)(2,1)} %pad_maximum_fusion.3.k_t, bf16[96,2048]{1,0:T(8,128)(2,1)} %slice.131.v_t, s32[2048,128]{1,0:T(8,128)} %broadcast_in_dim.25.hi), custom_call_target="tpu_custom_call" | custom-call | flops 800000000 | bytes 4194304 | tf_op jit(solution)/shard_map/pallas_call | solution.py:711
  93.1 10.7 %shard_map.223 = bf16[16,96,128]{2,1,0:T(8,128)(2,1)} custom-call(bf16[96,2048]{1,0:T(8,128)(2,1)} %get-tuple-element.43.att), custom_call_target="tpu_custom_call" | custom-call | tf_op jit(solution)/shard_map/pallas_call | solution.py:275
  103.8 2.7 multiply_reduce_fusion.4
  106.5 0.9 multiply_convert_fusion.4.h2
  107.4 44.3 %shard_map.224 = (bf16[8,128,1536]{2,1,0:T(8,128)(2,1)}, bf16[8,128,1536]{2,1,0:T(8,128)(2,1)}, bf16[3,8,192,512]{3,2,1,0:T(8,128)(2,1)}) custom-call(bf16[128,1536]{1,0:T(8,128)(2,1)} %multiply_convert_fusion.4.h2, bf16[128,1536]{1,0:T(8,128)(2,1)} %bitcast.161, bf16[3,8,48,128]{3,2,1,0:T(8,128)(2,1)} %get-tuple-element.45.wfp), custom_call_target="tpu_custom_call" | custom-call | tf_op jit(solution)/shard_map/pallas_call | solution.py:275
  151.8 2.8 fusion.57
  155.1 1.8 fusion.62
  157.0 1.8 fusion.63
  158.8 2.7 multiply_convert_fusion.1
  161.5 2.3 convolution_convert_fusion.4
  163.8 1.9 convolution_convert_fusion.3
  165.6 1.9 convolution_convert_fusion.2
  167.5 2.5 pad_maximum_fusion.dwf
  169.9 1.8 fusion.64
  171.8 3.5 add_convert_fusion
  175.3 47.3 %shard_map.225 = (f32[128,1536]{1,0:T(8,128)}, bf16[3,8,48,128]{3,2,1,0:T(8,128)(2,1)}) custom-call(bf16[8,128,1536]{2,1,0:T(8,128)(2,1)} %bitcast.144, bf16[3,8,192,512]{3,2,1,0:T(8,128)(2,1)} %pad_maximum_fusion.dwf), custom_call_target="tpu_custom_call" | custom-call | tf_op jit(solution)/shard_map/pallas_call | solution.py:275
  222.6 1.4 multiply_reduce_fusion.3
  224.4 2.2 convolution_convert_fusion.6
  226.6 0.9 copy.58
  227.5 30.9 %shard_map.226 = (bf16[16,96,128]{2,1,0:T(8,128)(2,1)}, bf16[8,1536,128]{2,1,0:T(8,128)(2,1)}, bf16[8,192,128]{2,1,0:T(8,128)(2,1)}, bf16[8,3,48,128]{3,2,1,0:T(8,128)(2,1)}) custom-call(bf16[16,96,128]{2,1,0:T(8,128)(2,1)} %bitcast.159, bf16[1536,128]{1,0:T(8,128)(2,1)} %bitcast.148, bf16[8,192,128]{2,1,0:T(8,128)(2,1)} %bitcast.160, ...), custom_call_target="tpu_custom_call" | custom-call | tf_op jit(solution)/shard_map/pallas_call | solution.py:275
  258.4 4.0 fusion.dwo
  262.5 10.9 %shard_map.227 = (f32[96,2048]{1,0:T(8,128)}, f32[96,2048]{1,0:T(8,128)}, f32[96,2048]{1,0:T(8,128)}) custom-call(bf16[96,2048]{1,0:T(8,128)(2,1)} %pad_maximum_fusion.2.q_t, bf16[96,2048]{1,0:T(8,128)(2,1)} %pad_maximum_fusion.3.k_t, bf16[96,2048]{1,0:T(8,128)(2,1)} %slice.131.v_t, bf16[16,96,128]{2,1,0:T(8,128)(2,1)} %get-tuple-element.51.do_blocks, ...), custom_call_target="tpu_custom_call" | custom-call | flops 2000000000 | bytes 6291456 | tf_op jit(solution)/shard_map/pallas_call | solution.py:746
  273.4 2.7 constant_dynamic-update-slice_fusion.3
  276.1 2.8 constant_dynamic-update-slice_fusion.2
  279.0 0.8 select_dynamic-update-slice_fusion.1
  279.8 0.8 select_dynamic-update-slice_fusion
  280.6 2.4 constant_dynamic-update-slice_fusion.5
  283.0 2.4 constant_dynamic-update-slice_fusion.4
  285.4 0.8 convert_dynamic-update-slice_fusion
  286.2 8.1 %convolution_convert_fusion.5 = bf16[1536,384]{1,0:T(8,128)(2,1)} fusion(bf16[2048,1536]{1,0:T(8,128)(2,1)} %bitcast.179, bf16[384,2048]{1,0:T(8,128)(2,1)} %get-tuple-element.104), kind=kOutput, calls=%fused_computation.12 | convolution fusion | flops 2416508928 | bytes 9043968 | tf_op jit(solution)/shard_map/dot_general | solution.py:766
  294.4 34.9 %shard_map.228 = (bf16[16,288,128]{2,1,0:T(8,128)(2,1)}, bf16[96,384]{1,0:T(8,128)(2,1)}, bf16[48,384]{1,0:T(8,128)(2,1)}) custom-call(bf16[288,2048]{1,0:T(8,128)(2,1)} %copy-done.11, bf16[8,192,384]{2,1,0:T(8,128)(2,1)} %bitcast.165, bf16[192,1536]{1,0:T(8,128)(2,1)} %fusion.dwo), custom_call_target="tpu_custom_call" | custom-call | tf_op jit(solution)/shard_map/pallas_call | solution.py:275
  329.3 1.2 fusion.60
  331.0 1.1 fusion.59
  332.9 4.9 %convolution_convert_fusion.1 = bf16[1024,1536]{1,0:T(8,128)(2,1)} fusion(bf16[1024,384]{1,0:T(8,128)(2,1)S(1)} %bitcast.168, bf16[1536,384]{1,0:T(8,128)(2,1)} %bitcast.186), kind=kOutput, calls=%fused_computation.3 | convolution fusion | flops 1209532416 | bytes 5111808 | tf_op jit(solution)/shard_map/dot_general | solution.py:897
  337.8 3.5 convolution_convert_fusion
  341.3 54.0 %shard_map.229 = (f32[128,1536]{1,0:T(8,128)}, f32[128,1536]{1,0:T(8,128)}, bf16[8,3,192,512]{3,2,1,0:T(8,128)(2,1)}, bf16[16,96,384]{2,1,0:T(8,128)(2,1)}, bf16[192,1536]{1,0:T(8,128)(2,1)}) custom-call(bf16[8,128,1536]{2,1,0:T(8,128)(2,1)} %bitcast.150, bf16[8,128,1536]{2,1,0:T(8,128)(2,1)} %bitcast.151, bf16[8,3,48,128]{3,2,1,0:T(8,128)(2,1)} %get-tuple-element.61.grads, ...), custom_call_target="tpu_custom_call" | custom-call | tf_op jit(solution)/shard_map/pallas_call | solution.py:275
  395.3 3.6 convert_element_type.200
  399.0 3.0 slice_bitcast_fusion
  402.0 2.2 copy.76
  406.1 4.3 broadcast_multiply_fusion
  411.0 2.0 copy.78
  413.2 1.3 fusion.58
  414.5 1.3 copy.64
  415.8 2.2 reshape.230
  418.0 2.5 copy.65
  420.5 2.2 reshape.231
  422.7 2.6 broadcast_multiply_fusion.3
  425.4 0.9 copy.63
  426.3 1.5 reshape.229
  427.9 2.7 broadcast_multiply_fusion.2
  431.1 1.1 convert_bitcast_fusion.1
  432.5 1.1 fusion.47
  433.6 0.8 fusion.46
  (107 shorter events, 13.2 us)
Async XLA Ops:
  0.6 3.1 copy-start.27
  3.9 4.0 copy-start.25
  3.9 3.9 copy-start.9
  6.8 1.8 copy-start.17
  7.9 1.3 copy-start.16
  9.2 2.1 copy-start.1
  9.7 2.7 copy-start.26
  11.5 59.5 %copy-start.21 = (f32[128]{0:T(128)}, f32[128]{0:T(128)S(1)}, u32[]{:S(2)}) copy-start(f32[128]{0:T(128)S(1)} %add_rsqrt_fusion.1) | copy-start | bytes 1540
  83.0 20.7 %copy-start = (bf16[8,192,1536]{2,1,0:T(8,128)(2,1)S(1)}, bf16[8,192,1536]{2,1,0:T(8,128)(2,1)}, u32[]{:S(2)}) copy-start(bf16[8,192,1536]{2,1,0:T(8,128)(2,1)} %get-tuple-element.44) | copy-start | bytes 14155780
  151.7 3.3 copy-start.23
  154.6 2.3 copy-start.12
  155.1 2.0 copy-start.24
  161.5 4.2 copy-start.29
  175.3 48.8 %copy-start.14 = (bf16[1,128,1536]{2,1,0:T(8,128)(2,1)S(1)}, bf16[1,128,1536]{2,1,0:T(8,128)(2,1)}, u32[]{:S(2)}) copy-start(bf16[1,128,1536]{2,1,0:T(8,128)(2,1)} %param.15) | copy-start | bytes 1179652
  222.6 1.5 copy-start.6
  224.4 2.2 copy-start.2
  273.4 7.2 %copy-start.4 = (f32[96,2048]{1,0:T(8,128)S(1)}, f32[96,2048]{1,0:T(8,128)}, u32[]{:S(2)}) copy-start(f32[96,2048]{1,0:T(8,128)} %get-tuple-element.55) | copy-start | bytes 2359300
  279.8 5.6 %copy-start.18 = (f32[96,2048]{1,0:T(8,128)S(1)}, f32[96,2048]{1,0:T(8,128)}, u32[]{:S(2)}) copy-start(f32[96,2048]{1,0:T(8,128)} %get-tuple-element.56) | copy-start | bytes 2359300
  286.2 8.1 %copy-start.11 = (bf16[288,2048]{1,0:T(8,128)(2,1)}, bf16[288,2048]{1,0:T(8,128)(2,1)S(1)}, u32[]{:S(2)}) copy-start(bf16[288,2048]{1,0:T(8,128)(2,1)S(1)} %get-tuple-element.105.dqkv) | copy-start | bytes 3538948
  332.9 4.9 %copy-start.13 = (bf16[1,8,192,512]{3,2,1,0:T(8,128)(2,1)S(1)}, bf16[1,8,192,512]{3,2,1,0:T(8,128)(2,1)}, u32[]{:S(2)}) copy-start(bf16[1,8,192,512]{3,2,1,0:T(8,128)(2,1)} %copy-done.12) | copy-start | bytes 4718596
  332.9 4.9 %copy-start.30 = (bf16[1024,512]{1,0:T(8,128)(2,1)S(1)}, bf16[1024,512]{1,0:T(8,128)(2,1)}, u32[]{:S(2)}) copy-start(bf16[1024,512]{1,0:T(8,128)(2,1)} %copy-done.29) | copy-start | bytes 3145732
  404.2 0.7 copy-start.28
  404.2 1.4 copy-start.7
  404.2 1.9 copy-start.8
  411.0 2.0 copy-start.15
  426.3 1.6 copy-start.10
  427.9 3.2 copy-start.20
  427.9 4.4 %copy-start.5 = (f32[128,1536]{1,0:T(8,128)S(1)}, f32[128,1536]{1,0:T(8,128)}, u32[]{:S(2)}) copy-start(f32[128,1536]{1,0:T(8,128)} %get-tuple-element.65) | copy-start | bytes 2359300
  427.9 4.4 %copy-start.22 = (f32[128]{0:T(128)S(1)}, f32[128]{0:T(128)}, u32[]{:S(2)}) copy-start(f32[128]{0:T(128)} %copy-done.21) | copy-start | bytes 1540
  430.5 2.0 copy-start.3
  432.3 1.3 copy-start.19

commit v2 on v1

v2 whole, which is shorter than its diff:
```python
import functools

import jax
import jax.numpy as jnp
from jax import lax
from jax.experimental import pallas as pl
from jax.experimental.pallas import tpu as pltpu
from jax.sharding import PartitionSpec as P

HQ = 16
HK = 8
HD = 96
WINDOW = 1024
D = 1536
FF = 4096
BLOCK = 128
LENGTH = 2048
DP = 8
CTX = 16
ZN = 4
SHARD = D // DP
FSH = FF // DP
GROUP = 4 * HD

EPSILON = 1e-05
THETA_BASE = 100000.0
NEG_LARGE = -1e30

BF = jnp.bfloat16
F32 = jnp.float32
MESH = pl.DeviceIdType.MESH
ANY = pl.BlockSpec(memory_space=pl.ANY)
VMEM = pl.BlockSpec(memory_space=pltpu.VMEM)


def mod(a, n):
    return lax.rem(a + n, n)


class Place:
    def __init__(self):
        self.dp = lax.axis_index("dp")
        self.ctx = lax.axis_index("ctx")
        self.z, self.core = self.dp // 2, lax.rem(self.dp, 2)
        self.y, self.x = self.ctx // 4, lax.rem(self.ctx, 4)

    def at_x(self, k):
        return (self.dp, self.y * 4 + mod(self.x + k, 4))

    def at_y(self, k):
        return (self.dp, mod(self.y + k, 4) * 4 + self.x)

    def at_z(self, k):
        return (mod(self.z + k, 4) * 2 + self.core, self.ctx)

    def at_dp(self, k):
        return (mod(self.dp + k, DP), self.ctx)

    def at_ctx(self, k):
        return (self.dp, mod(self.ctx + k, CTX))

    def sibling(self):
        return (self.z * 2 + 1 - self.core, self.ctx)


class Net:
    def __init__(self, send, recv, local):
        self.send, self.recv, self.local = send, recv, local
        self.n, self.m = 0, 0

    def remote(self, src, dst, peer):
        assert self.n < self.send.shape[0]
        copy = pltpu.make_async_remote_copy(
            src_ref=src,
            dst_ref=dst,
            send_sem=self.send.at[self.n],
            recv_sem=self.recv.at[self.n],
            device_id=peer,
            device_id_type=MESH,
        )
        self.n += 1
        copy.start()
        return copy

    def copy(self, src, dst):
        assert self.m < self.local.shape[0]
        copy = pltpu.make_async_copy(src, dst, self.local.at[self.m])
        self.m += 1
        copy.start()
        return copy


def greet(peers):
    barrier = pltpu.get_barrier_semaphore()
    for peer in peers:
        pl.semaphore_signal(barrier, inc=1, device_id=peer, device_id_type=MESH)
    pl.semaphore_wait(barrier, len(peers))


def xy_peers(p):
    return [p.at_x(k) for k in (1, 2, 3)] + [p.at_y(k) for k in (1, 2, 3)]


def z_peers(p):
    return [p.at_z(k) for k in (1, 2, 3)] + [p.sibling()]


class GatherXY:
    def __init__(self, net, p, own, slot):
        self.net, self.p, self.slot = net, p, slot
        self.kept = [net.copy(own(h), slot(h, p.y, p.x)) for h in (0, 1)]
        self.first, self.rest = {}, []
        for k in (1, 2, 3):
            for h in (0, 1):
                here = slot(h, p.y, p.x)
                along = net.remote(own(h), here, p.at_x(k) if h == 0 else p.at_y(k))
                self.first[h, k] = along
        for k in (1, 2, 3):
            for h in (0, 1):
                here = slot(h, p.y, p.x)
                self.rest.append(net.remote(own(h), here, p.at_y(k) if h == 0 else p.at_x(k)))

    def forward(self):
        net, p = self.net, self.p
        for k in (1, 3, 2):
            for h in (0, 1):
                self.first[h, k].wait_recv()
                if h == 0:
                    block = self.slot(0, p.y, mod(p.x - k, 4))
                else:
                    block = self.slot(1, mod(p.y - k, 4), p.x)
                for m in (1, 2, 3):
                    self.rest.append(net.remote(block, block, p.at_y(m) if h == 0 else p.at_x(m)))

    def end(self):
        for copy in self.first.values():
            copy.wait_send()
        for copy in self.rest:
            copy.wait()
        for copy in self.kept:
            copy.wait()


class Exchange:
    def __init__(self, net, p, src, slot):
        self.kept = net.copy(src(p.dp), slot(p.dp))
        self.sent = [net.remote(src(mod(p.dp + k, DP)), slot(p.dp), p.at_dp(k)) for k in range(1, DP)]

    def end(self):
        for copy in self.sent:
            copy.wait()
        self.kept.wait()


def near_peers(p):
    return [p.at_x(1), p.at_x(3), p.at_y(1), p.at_y(3)]


def near_z(p):
    return [p.at_z(1), p.at_z(3), p.sibling()]


class RingXY:
    def __init__(self, net, p, own, slot, part):
        self.net, self.p, self.part = net, p, part
        self.spot = lambda h, a, b: slot(h, b, a) if h == 0 else slot(h, a, b)
        self.me = [(p.x, p.y), (p.y, p.x)]
        self.first = [p.at_x, p.at_y]
        self.second = [p.at_y, p.at_x]
        self.kept = [net.copy(own(h), self.spot(h, *self.me[h])) for h in (0, 1)]
        self.near, self.far, self.side, self.last = {}, {}, {}, []
        for k in (1, 3):
            for h in (0, 1):
                here = self.spot(h, *self.me[h])
                self.near[h, k] = net.remote(own(h), here, self.first[h](k))
        for k in (1, 3):
            for h in (0, 1):
                here = self.spot(h, *self.me[h])
                self.side[h, 0, k] = net.remote(own(h), here, self.second[h](k))

    def send(self, h, a, block):
        for k in (1, 3):
            self.side[h, a, k] = self.net.remote(block, block, self.second[h](k))

    def relay(self, h, a):
        mine, other = self.me[h]
        for k in (1, 3):
            self.side[h, a, k].wait_recv()
            block = self.part(self.spot(h, mod(mine + a, 4), mod(other - k, 4)), k // 2)
            self.last.append(self.net.remote(block, block, self.second[h](k)))

    def forward(self):
        for k in (1, 3):
            for h in (0, 1):
                mine, other = self.me[h]
                self.near[h, k].wait_recv()
                block = self.spot(h, mod(mine - k, 4), other)
                cut = self.part(block, k // 2)
                self.far[h, k] = self.net.remote(cut, cut, self.first[h](k))
                self.send(h, 4 - k, block)

    def middle(self):
        for h in (0, 1):
            self.relay(h, 0)
        for h in (0, 1):
            for k in (1, 3):
                self.far[h, k].wait_recv()
            mine, other = self.me[h]
            self.send(h, 2, self.spot(h, mod(mine + 2, 4), other))

    def finish(self):
        for a in (1, 3, 2):
            for h in (0, 1):
                self.relay(h, a)

    def end(self):
        for copies in (self.near, self.far, self.side):
            for copy in copies.values():
                copy.wait_send()
        for copy in self.last:
            copy.wait()
        for copy in self.kept:
            copy.wait()


class RingDP:
    def __init__(self, net, p, own, slot, part):
        self.net, self.p, self.slot, self.part = net, p, slot, part
        here = slot(p.dp)
        self.kept = net.copy(own, here)
        self.near = {k: net.remote(own, here, p.at_z(k)) for k in (1, 3)}
        self.rest = [net.remote(own, here, p.sibling())]
        self.far = {}

    def forward(self):
        net, p = self.net, self.p
        for k in (1, 3):
            self.near[k].wait_recv()
            block = self.slot(mod(p.z - k, 4) * 2 + p.core)
            cut = self.part(block, k // 2)
            self.far[k] = net.remote(cut, cut, p.at_z(k))
            self.rest.append(net.remote(block, block, p.sibling()))

    def finish(self):
        net, p = self.net, self.p
        for k in (1, 3):
            self.far[k].wait_recv()
            cut = self.part(self.slot(mod(p.z + 2, 4) * 2 + p.core), k // 2)
            self.rest.append(net.remote(cut, cut, p.sibling()))

    def end(self):
        for copy in (*self.near.values(), *self.far.values()):
            copy.wait_send()
        for copy in self.rest:
            copy.wait()
        self.kept.wait()


class RingSum:
    def __init__(self, net, peer, block, part, through, got):
        self.net, self.peer, self.block, self.part = net, peer, block, part
        self.through, self.got = through, got
        self.far, self.near = {}, []

    def start_far(self):
        for k in (1, 3):
            cut = self.part(self.block(2), k // 2)
            self.far[k] = self.net.remote(cut, self.through[k // 2], self.peer(k))

    def start_near(self, k):
        i = 1 - k // 2
        cut = self.part(self.block(k), i)
        self.near.append(self.net.remote(cut, self.part(self.got[k // 2], i), self.peer(k)))

    def start(self):
        self.start_far()
        for k in (1, 3):
            self.start_near(k)

    def forward(self):
        for k in (1, 3):
            i = k // 2
            self.far[k].wait_recv()
            cut = self.part(self.block(k), i)
            add_all(cut, [cut, self.through[i]])
            self.near.append(self.net.remote(cut, self.part(self.got[i], i), self.peer(k)))

    def end(self, out):
        for copy in self.far.values():
            copy.wait_send()
        for copy in self.near:
            copy.wait()
        add_all(out, [self.block(0), self.got[0], self.got[1]])


class SumDP:
    def __init__(self, net, p, part, cut, mine, sib, through, got, out):
        self.net, self.p, self.mine, self.sib, self.out = net, p, mine, sib, out
        self.ring = RingSum(
            net, p.at_z, lambda k: mine.at[mod(p.z + k, 4)], cut, through, got
        )
        self.loads = {}
        for k in (2, 1, 3, 0):
            z = mod(p.z + k, 4)
            swap = net.remote(part(2 * z + 1 - p.core), sib.at[z], p.sibling())
            self.loads[k] = (net.copy(part(2 * z + p.core), mine.at[z]), swap)

    def join(self, k):
        for copy in self.loads[k]:
            copy.wait()
        z = mod(self.p.z + k, 4)
        add_all(self.mine.at[z], [self.mine.at[z], self.sib.at[z]])

    def begin(self):
        self.join(2)
        self.ring.start_far()
        for k in (1, 3):
            self.join(k)
            self.ring.start_near(k)
        self.join(0)

    def forward(self):
        self.ring.forward()

    def end(self):
        self.ring.end(self.out)


class SumXY:
    def __init__(self, net, p, cut, part, first, second, piece):
        self.p, self.piece = p, piece
        self.cut = cut
        x, y = (lambda k: mod(p.x + k, 4)), (lambda k: mod(p.y + k, 4))
        self.one = [
            RingSum(net, p.at_x, lambda k: cut(0, None, x(k)), part, *first[0]),
            RingSum(net, p.at_y, lambda k: cut(1, y(k), None), part, *first[1]),
        ]
        self.two = [
            RingSum(net, p.at_y, lambda k: cut(0, y(k), p.x), part, *second[0]),
            RingSum(net, p.at_x, lambda k: cut(1, p.y, x(k)), part, *second[1]),
        ]

    def start(self):
        for ring in self.one:
            ring.start()

    def forward(self):
        for ring in self.one:
            ring.forward()

    def turn(self):
        p = self.p
        for h, own in ((0, self.cut(0, None, p.x)), (1, self.cut(1, p.y, None))):
            self.one[h].end(own)
            self.two[h].start()

    def finish(self):
        for ring in self.two:
            ring.forward()

    def end(self):
        for h in (0, 1):
            self.two[h].end(self.piece(h))


def add_all(out, terms):
    *lead, rows, lanes = out.shape
    step_rows = min(rows, max(16, (24 * 1024 // lanes) // 16 * 16))
    while rows % step_rows:
        step_rows -= 16
    steps = rows // step_rows
    count = steps
    for n in lead:
        count *= n

    def step(i, carry):
        j, r = i // steps, lax.rem(i, steps)
        index = []
        for n in reversed(lead):
            index.insert(0, lax.rem(j, n))
            j = j // n
        at = (*index, pl.ds(pl.multiple_of(r * step_rows, 16), step_rows), slice(None))
        total = terms[0][at].astype(F32)
        for term in terms[1:]:
            total = total + term[at].astype(F32)
        out[at] = total.astype(out.dtype)
        return carry

    lax.fori_loop(0, count, step, 0)


def call(body, ident, outs, out_places, remotes, locals_, scratch, *args, vmem=56):
    return pl.pallas_call(
        body,
        out_shape=outs,
        in_specs=[ANY] * len(args),
        out_specs=out_places,
        scratch_shapes=[
            *scratch,
            pltpu.SemaphoreType.DMA((remotes,)),
            pltpu.SemaphoreType.DMA((remotes,)),
            pltpu.SemaphoreType.DMA((locals_,)),
        ],
        compiler_params=pltpu.CompilerParams(
            collective_id=ident, has_side_effects=True, vmem_limit_bytes=vmem << 20
        ),
    )(*args)


def shape(*dims, dtype=BF):
    return jax.ShapeDtypeStruct(dims, dtype)


def rows_of(n):
    return lambda ref, i: ref.at[pl.ds(0, n)] if i == 0 else ref.at[pl.ds(n, ref.shape[0] - n)]


def half(ref, h, n=64):
    return ref.at[pl.ds(h * n, n)]


def first_exchange(h1, pos, wgrp, w_out_t, wpiece):
    def body(h1, pos, wgrp, w_out_t, wpiece, seq, posq, wjob, wo, wfp, send, recv, local):
        p = Place()
        net = Net(send, recv, local)
        greet(xy_peers(p) + [p.at_dp(k) for k in range(1, DP)])
        rows = RingXY(
            net,
            p,
            lambda h: half(h1, h),
            lambda h, y, x: seq.at[y * 4 + x, pl.ds(h * 64, 64)],
            rows_of(32),
        )
        spots = GatherXY(
            net, p, lambda h: half(pos, h, 8), lambda h, y, x: posq.at[y * 4 + x, pl.ds(h * 8, 8)]
        )
        job = RingDP(net, p, wgrp.at[p.ctx // 2], lambda i: wjob.at[i], rows_of(96))
        ffw = Exchange(net, p, lambda i: wpiece.at[i], lambda i: wfp.at[:, i])
        out = RingDP(net, p, w_out_t, lambda i: wo.at[i], rows_of(96))
        job.forward()
        rows.forward()
        spots.forward()
        out.forward()
        rows.middle()
        job.finish()
        out.finish()
        rows.finish()
        for part in (rows, spots, job, ffw, out):
            part.end()

    return call(
        body,
        1,
        (
            shape(CTX, BLOCK, D),
            shape(CTX, 16, BLOCK, dtype=F32),
            shape(DP, SHARD, GROUP),
            shape(DP, SHARD, D),
            shape(3, DP, 48, 128),
        ),
        [ANY] * 5,
        95,
        8,
        [],
        h1,
        pos,
        wgrp,
        w_out_t,
        wpiece,
    )


def middle_exchange(h2):
    def body(h2, h2_all, send, recv, local):
        p = Place()
        net = Net(send, recv, local)
        greet(near_z(p))
        hid = RingDP(net, p, h2, lambda i: h2_all.at[i], rows_of(64))
        hid.forward()
        hid.finish()
        hid.end()

    return call(body, 3, shape(DP, BLOCK, D), ANY, 10, 2, [], h2)


def sum_dp_scratch(rows=BLOCK, lanes=D):
    return [
        pltpu.VMEM((ZN, rows, lanes), BF),
        pltpu.VMEM((ZN, rows, lanes), BF),
        pltpu.VMEM((rows // 2, lanes), BF),
        pltpu.VMEM((rows // 2, lanes), BF),
        pltpu.VMEM((rows, lanes), BF),
        pltpu.VMEM((rows, lanes), BF),
    ]


def sum_dp(net, p, part, scratch, out):
    mine, sib, t0, t1, g0, g1 = scratch
    return SumDP(net, p, part, rows_of(mine.shape[1] // 2), mine, sib, (t0, t1), (g0, g1), out)


def ring_scratch(rows, lanes):
    return [pltpu.VMEM((3, n, rows, lanes), BF) for n in (2, 2, 4, 4)]


def ring_buffers(refs):
    return (refs[0], refs[1]), (refs[2], refs[3])


def back_exchange(dh2, dwf):
    def body(dh2, dwf, out, piece, part, *rest):
        scratch, rings, (send, recv, local) = rest[:6], rest[6:-3], rest[-3:]
        p = Place()
        net = Net(send, recv, local)
        greet(near_peers(p) + near_z(p))
        load = net.copy(dwf, part)
        hid = sum_dp(net, p, lambda i: dh2.at[i], scratch, out)

        def cut(h, y, x):
            rows = slice(None) if y is None else pl.ds(pl.multiple_of(y * 48, 16), 48)
            lanes = slice(None) if x is None else pl.ds(pl.multiple_of(x * 128, 128), 128)
            return part.at[:, pl.ds(4 * h, 4), rows, lanes]

        buffers = [ring_buffers(rings[4 * i : 4 * i + 4]) for i in range(4)]
        wts = SumXY(
            net,
            p,
            cut,
            lambda ref, i: ref.at[:, pl.ds(2 * i, 2)],
            buffers[:2],
            buffers[2:],
            lambda h: piece.at[:, pl.ds(4 * h, 4)],
        )
        load.wait()
        wts.start()
        hid.begin()
        hid.forward()
        wts.forward()
        hid.end()
        wts.turn()
        wts.finish()
        wts.end()

    return call(
        body,
        4,
        (shape(BLOCK, D, dtype=F32), shape(3, DP, 48, 128)),
        [VMEM] * 2,
        40,
        8,
        [
            pltpu.VMEM((3, DP, SHARD, FSH), BF),
            *sum_dp_scratch(),
            *ring_scratch(SHARD, 128),
            *ring_scratch(48, FSH),
            *ring_scratch(48, 128),
            *ring_scratch(48, 128),
        ],
        dh2,
        dwf,
    )


def heads_out(dat, att, da_t, piece):
    def body(dat, att, da_t, piece, heads, att_all, da_all, grads, send, recv, local):
        p = Place()
        net = Net(send, recv, local)
        greet([p.at_ctx(k) for k in range(1, CTX)] + [p.at_dp(k) for k in range(1, DP)])
        kept = net.copy(dat.at[p.ctx], heads.at[p.ctx])
        sent = [
            net.remote(dat.at[mod(p.ctx + k, CTX)], heads.at[p.ctx], p.at_ctx(k))
            for k in range(1, CTX)
        ]
        atts = RingDP(net, p, att, lambda i: att_all.at[i], rows_of(D // 2))
        das = Exchange(net, p, lambda i: da_t.at[i], lambda i: da_all.at[i])
        wts = Exchange(net, p, lambda i: piece.at[:, i], lambda i: grads.at[i])
        atts.forward()
        for copy in sent:
            copy.wait()
        kept.wait()
        atts.finish()
        for part in (atts, das, wts):
            part.end()

    return call(
        body,
        5,
        (
            shape(CTX, HD, BLOCK),
            shape(DP, D, BLOCK),
            shape(DP, SHARD, BLOCK),
            shape(DP, 3, 48, 128),
        ),
        [ANY] * 4,
        38,
        4,
        [],
        dat,
        att,
        da_t,
        piece,
    )


def grads_home(dqkv, dwj, dwo):
    def body(
        dqkv, dwj, dwo, out, pair, piece, full, away, f0, s0, w0, *rest
    ):
        scratch, (send, recv, local) = rest[:6], rest[6:]
        p = Place()
        net = Net(send, recv, local)
        group, rank = p.ctx // 2, lax.rem(p.ctx, 2)
        home = group == p.dp
        partner = (p.dp, p.ctx + 1 - 2 * rank)

        barrier = pltpu.get_barrier_semaphore()
        others = xy_peers(p) + z_peers(p)
        for peer in others:
            pl.semaphore_signal(barrier, inc=1, device_id=peer, device_id_type=MESH)
        for i in range(DP):
            for r in range(2):
                own = home & (p.dp == i) & (rank == r)

                @pl.when(jnp.logical_not(own))
                def _():
                    peer = (jnp.int32(i), 2 * p.dp + r)
                    pl.semaphore_signal(barrier, inc=1, device_id=peer, device_id_type=MESH)

        pl.semaphore_wait(barrier, CTX + len(others) - home.astype(jnp.int32))

        lanes = lambda c: pl.ds(pl.multiple_of(c * BLOCK, BLOCK), BLOCK)
        slot = p.dp * 2 + rank

        def message(k, spot):
            c = mod(p.ctx + k, CTX)
            return pltpu.make_async_remote_copy(
                src_ref=dqkv.at[:, lanes(c)],
                dst_ref=out.at[spot],
                send_sem=send.at[k],
                recv_sem=recv.at[spot],
                device_id=(group, c),
                device_id_type=MESH,
            )

        own = pltpu.make_async_copy(dqkv.at[:, lanes(p.ctx)], out.at[slot], local.at[0])
        net.m = 1

        @pl.when(home)
        def _():
            own.start()

        @pl.when(jnp.logical_not(home))
        def _():
            message(0, slot).start()

        for k in range(1, CTX):
            message(k, slot).start()
        net.n = CTX

        hid = sum_dp(net, p, lambda i: dwj.at[i], scratch, full)
        wide = [net.copy(dwo.at[:, pl.ds(pl.multiple_of(p.x * 384, 128), 384)], w0)]
        for k in (1, 3, 2):
            cut = dwo.at[:, pl.ds(pl.multiple_of(mod(p.x + k, 4) * 384, 128), 384)]
            wide.append(net.remote(cut, f0.at[k - 1], p.at_x(k)))
        hid.begin()
        for copy in wide:
            copy.wait()
        add_all(w0, [w0] + [f0.at[k] for k in range(3)])
        tall = []
        for k in (1, 3, 2):
            cut = w0.at[pl.ds(pl.multiple_of(mod(p.y + k, 4) * 48, 16), 48)]
            tall.append(net.remote(cut, s0.at[k - 1], p.at_y(k)))
        hid.forward()
        hid.end()
        theirs = full.at[pl.ds(pl.multiple_of((1 - rank) * 96, 16), 96)]
        swap = net.remote(theirs, away, partner)
        for copy in tall:
            copy.wait()
        add_all(piece, [w0.at[pl.ds(pl.multiple_of(p.y * 48, 16), 48)]] + [s0.at[k] for k in range(3)])
        swap.wait()
        add_all(pair, [full.at[pl.ds(pl.multiple_of(rank * 96, 16), 96)], away])

        for k in range(1, CTX):
            message(k, slot).wait_send()

        @pl.when(home)
        def _():
            own.wait()

        @pl.when(jnp.logical_not(home))
        def _():
            message(0, slot).wait_send()

        for spot in range(CTX):
            here = home & (slot == spot)

            @pl.when(jnp.logical_not(here))
            def _():
                message(0, spot).wait_recv()

    return call(
        body,
        6,
        (shape(CTX, 3 * HD, BLOCK), shape(96, GROUP), shape(48, 384)),
        [ANY, VMEM, VMEM],
        40,
        8,
        [
            pltpu.VMEM((SHARD, GROUP), BF),
            pltpu.VMEM((96, GROUP), BF),
            pltpu.VMEM((3, SHARD, 384), BF),
            pltpu.VMEM((3, 48, 384), BF),
            pltpu.VMEM((SHARD, 384), BF),
            *sum_dp_scratch(SHARD, GROUP),
        ],
        dqkv,
        dwj,
        dwo,
    )


def last_exchange(dh1, ypart, grads, pair, piece):
    def body(dh1, ypart, grads, pair, piece, e1, ysum, gff, gqkv, gout, *rest):
        scratch, (send, recv, local) = rest[:-3], rest[-3:]
        p = Place()
        net = Net(send, recv, local)
        greet(xy_peers(p) + z_peers(p))
        inp = sum_dp(net, p, lambda i: dh1.at[i], scratch[:6], e1)
        wts = RingXY(
            net,
            p,
            lambda h: grads.at[pl.ds(4 * h, 4)],
            lambda h, y, x: gff.at[
                pl.ds(4 * h, 4),
                :,
                pl.ds(pl.multiple_of(y * 48, 16), 48),
                pl.ds(pl.multiple_of(x * 128, 128), 128),
            ],
            rows_of(2),
        )
        qkv = RingXY(
            net,
            p,
            lambda h: half(pair, h, 48),
            lambda h, y, x: gqkv.at[y * 4 + x, pl.ds(h * 48, 48)],
            rows_of(32),
        )
        proj = GatherXY(
            net,
            p,
            lambda h: piece.at[pl.ds(32 * h, 32 - 16 * h)],
            lambda h, y, x: gout.at[
                pl.ds(pl.multiple_of(y * 48 + 32 * h, 16), 32 - 16 * h),
                pl.ds(pl.multiple_of(x * 384, 128), 384),
            ],
        )
        inp.begin()
        res = sum_dp(net, p, lambda i: ypart.at[i], scratch[6:], ysum)
        wts.forward()
        inp.forward()
        qkv.forward()
        proj.forward()
        wts.middle()
        inp.end()
        res.begin()
        qkv.middle()
        wts.finish()
        qkv.finish()
        res.forward()
        res.end()
        for part in (wts, qkv, proj):
            part.end()

    return call(
        body,
        7,
        (
            shape(BLOCK, D, dtype=F32),
            shape(BLOCK, D, dtype=F32),
            shape(DP, 3, SHARD, FSH),
            shape(CTX, 96, GROUP),
            shape(SHARD, D),
        ),
        [VMEM, VMEM, ANY, ANY, ANY],
        140,
        24,
        sum_dp_scratch() + sum_dp_scratch(),
        dh1,
        ypart,
        grads,
        pair,
        piece,
    )


CHUNK = 256
CHUNKS = LENGTH // CHUNK
SCALE = HD ** (-0.5)


def span(j):
    return max(0, j * CHUNK - WINDOW), (j + 1) * CHUNK


def score_block(k, q_t, hi, j):
    low, high = span(j)
    s = jnp.dot(k[low:high, :], q_t[:, j * CHUNK : (j + 1) * CHUNK], preferred_element_type=F32)
    s = s * SCALE
    key = low + lax.broadcasted_iota(jnp.int32, s.shape, 0)
    query = j * CHUNK + lax.broadcasted_iota(jnp.int32, s.shape, 1)
    last = hi[low:high, :]
    last = jnp.concatenate([last] * (CHUNK // 128), axis=1)
    return jnp.where((query >= key) & (query <= last), s, NEG_LARGE)


def turn(values, cosine, sine):
    a, b = values[: HD // 2], values[HD // 2 :]
    return jnp.concatenate([a * cosine - b * sine, b * cosine + a * sine], axis=0)


def attend(seq, wjob, cosine, sine, hi, wfp, dd, wgrp):
    def body(
        seq, wjob, cosine, sine, hi, wfp, dd, wgrp,
        q_t, k_t, v_t, top, total, home, wf, dd_all, wdh,
        rows, w, w_t, k, att, load, send, recv, local,
    ):
        p = Place()
        net = Net(send, recv, local)
        greet([p.at_ctx(k) for k in range(1, CTX)] + [p.at_dp(k) for k in range(1, DP)])
        rank = lax.rem(p.ctx, 2)
        loads = [pltpu.make_async_copy(wjob, w, load.at[CHUNKS])]
        for j in range(CHUNKS):
            loads.append(
                pltpu.make_async_copy(seq.at[pl.ds(2 * j, 2)], rows.at[pl.ds(2 * j, 2)], load.at[j])
            )
        for copy in loads:
            copy.start()

        def message(b):
            return pltpu.make_async_remote_copy(
                src_ref=att.at[:, pl.ds(b * BLOCK, BLOCK)],
                dst_ref=home.at[p.ctx],
                send_sem=send.at[b],
                recv_sem=recv.at[p.ctx],
                device_id=(p.dp, jnp.int32(b)),
                device_id_type=MESH,
            )

        def arrival(c):
            return pltpu.make_async_remote_copy(
                src_ref=att.at[:, pl.ds(0, BLOCK)],
                dst_ref=home.at[c],
                send_sem=send.at[c],
                recv_sem=recv.at[c],
                device_id=(p.dp, jnp.int32(c)),
                device_id_type=MESH,
            )

        def kept(b):
            return pltpu.make_async_copy(
                att.at[:, pl.ds(b * BLOCK, BLOCK)], home.at[p.ctx], local.at[0]
            )

        net.n, net.m = CTX, 1
        wts = RingXY(
            net,
            p,
            lambda h: wfp.at[:, pl.ds(4 * h, 4)],
            lambda h, y, x: wf.at[
                :,
                pl.ds(4 * h, 4),
                pl.ds(pl.multiple_of(y * 48, 16), 48),
                pl.ds(pl.multiple_of(x * 128, 128), 128),
            ],
            lambda ref, i: ref.at[:, pl.ds(2 * i, 2)],
        )
        cot = RingDP(net, p, dd, lambda i: dd_all.at[i], rows_of(64))
        grp = Exchange(net, p, lambda i: wgrp.at[i], lambda i: wdh.at[i])

        loads[0].wait()
        w_t[...] = w[...].reshape(D, GROUP).T
        w_own = jnp.concatenate(
            [w_t[pl.ds(pl.multiple_of(rank * HD, 16), HD), :], w_t[2 * HD :, :]], axis=0
        )
        for j in range(CHUNKS):
            at = slice(j * CHUNK, (j + 1) * CHUNK)
            loads[j + 1].wait()
            tokens = rows[2 * j : 2 * j + 2].reshape(CHUNK, D)
            proj = dot(w_own, tokens, ((1,), (1,)))
            cos, sin = cosine[:, at], sine[:, at]
            q_t[:, at] = turn(proj[:HD], cos, sin).astype(BF)
            key = turn(proj[HD : 2 * HD], cos, sin).astype(BF)
            k_t[:, at] = key
            k[at, :] = key.T
            v_t[:, at] = proj[2 * HD :].astype(BF)
            low, high = span(j)
            s = score_block(k, q_t, hi, j)
            m = jnp.max(s, axis=0, keepdims=True)
            e = jnp.exp(s - m)
            t = jnp.sum(e, axis=0, keepdims=True)
            prob = (e * (1.0 / t)).astype(BF)
            att[:, at] = jnp.dot(v_t[:, low:high], prob, preferred_element_type=F32).astype(BF)
            top[:, at] = m
            total[:, at] = t
            for b in (2 * j, 2 * j + 1):

                @pl.when(p.ctx == b)
                def _():
                    kept(b).start()

                @pl.when(p.ctx != b)
                def _():
                    message(b).start()

            if j == 3:
                wts.forward()
            if j == 4:
                cot.forward()
            if j == 5:
                wts.middle()
            if j == 6:
                cot.finish()
        wts.finish()
        for b in range(CTX):

            @pl.when(p.ctx == b)
            def _():
                kept(b).wait()

            @pl.when(p.ctx != b)
            def _():
                message(b).wait_send()
                arrival(b).wait_recv()

        for part in (cot, grp, wts):
            part.end()

    return pl.pallas_call(
        body,
        out_shape=(
            shape(HD, LENGTH),
            shape(HD, LENGTH),
            shape(HD, LENGTH),
            shape(1, LENGTH, dtype=F32),
            shape(1, LENGTH, dtype=F32),
            shape(CTX, HD, BLOCK),
            shape(3, DP, SHARD, FSH),
            shape(DP, BLOCK, D),
            shape(DP, SHARD, GROUP),
        ),
        in_specs=[ANY, ANY, VMEM, VMEM, VMEM, ANY, ANY, ANY],
        out_specs=[VMEM] * 5 + [ANY] * 4,
        scratch_shapes=[
            pltpu.VMEM((CTX, BLOCK, D), BF),
            pltpu.VMEM((DP, SHARD, GROUP), BF),
            pltpu.VMEM((GROUP, D), BF),
            pltpu.VMEM((LENGTH, HD), BF),
            pltpu.VMEM((HD, LENGTH), BF),
            pltpu.SemaphoreType.DMA((CHUNKS + 1,)),
            pltpu.SemaphoreType.DMA((72,)),
            pltpu.SemaphoreType.DMA((72,)),
            pltpu.SemaphoreType.DMA((8,)),
        ],
        compiler_params=pltpu.CompilerParams(
            collective_id=2, has_side_effects=True, vmem_limit_bytes=56 << 20
        ),
    )(seq, wjob, cosine, sine, hi, wfp, dd, wgrp)


def attend_back(seq, q_t, k_t, v_t, do_blocks, hi, top, total, cosine, sine):
    def body(
        seq, q_t, k_t, v_t, do_blocks, hi, top, total, cosine, sine,
        out, dwj, rows, k, v, q, do, do_t, dk, dv, wide, load,
    ):
        rank = lax.rem(lax.axis_index("ctx"), 2)
        fetch = pltpu.make_async_copy(seq, rows, load)
        fetch.start()
        k[...] = k_t[...].T
        v[...] = v_t[...].T
        q[...] = q_t[...].T
        for b in range(CTX):
            do_t[:, b * BLOCK : (b + 1) * BLOCK] = do_blocks[b]
        do[...] = do_t[...].T
        dk[...] = jnp.zeros_like(dk)
        dv[...] = jnp.zeros_like(dv)
        for j in range(CHUNKS):
            low, high = span(j)
            at = slice(j * CHUNK, (j + 1) * CHUNK)
            s = score_block(k, q_t, hi, j)
            prob = jnp.exp(s - top[:, at]) * (1.0 / total[:, at])
            dp = jnp.dot(v[low:high, :], do_t[:, at], preferred_element_type=F32)
            inner = jnp.sum(prob * dp, axis=0, keepdims=True)
            ds = (prob * (dp - inner)).astype(BF)
            dq = jnp.dot(k_t[:, low:high], ds, preferred_element_type=F32) * SCALE
            out[:HD, at] = turn(dq, cosine[:, at], -sine[:, at]).astype(BF)
            dk[low:high, :] += jnp.dot(ds, q[at, :], preferred_element_type=F32)
            dv[low:high, :] += jnp.dot(prob.astype(BF), do[at, :], preferred_element_type=F32)
        out[HD : 2 * HD, :] = turn(dk[...].T * SCALE, cosine[...], -sine[...]).astype(BF)
        out[2 * HD :, :] = dv[...].T.astype(BF)
        mine = pl.multiple_of(rank * HD, 16)
        other = pl.multiple_of((1 - rank) * HD, 16)
        wide[pl.ds(mine, HD), :] = out[:HD, :]
        wide[pl.ds(other, HD), :] = jnp.zeros((HD, LENGTH), BF)
        wide[2 * HD :, :] = out[HD:, :]
        fetch.wait()
        grad = jnp.dot(wide[...], rows[...].reshape(LENGTH, D), preferred_element_type=F32)
        dwj[...] = grad.T.astype(BF).reshape(DP, SHARD, GROUP)

    return pl.pallas_call(
        body,
        out_shape=(shape(3 * HD, LENGTH), shape(DP, SHARD, GROUP)),
        in_specs=[ANY] + [VMEM] * 9,
        out_specs=[VMEM] * 2,
        scratch_shapes=[
            pltpu.VMEM((CTX, BLOCK, D), BF),
            pltpu.VMEM((LENGTH, HD), BF),
            pltpu.VMEM((LENGTH, HD), BF),
            pltpu.VMEM((LENGTH, HD), BF),
            pltpu.VMEM((LENGTH, HD), BF),
            pltpu.VMEM((HD, LENGTH), BF),
            pltpu.VMEM((LENGTH, HD), F32),
            pltpu.VMEM((LENGTH, HD), F32),
            pltpu.VMEM((GROUP, LENGTH), BF),
            pltpu.SemaphoreType.DMA,
        ],
        compiler_params=pltpu.CompilerParams(vmem_limit_bytes=56 << 20),
        cost_estimate=pl.CostEstimate(flops=4_400_000_000, bytes_accessed=12 << 20, transcendentals=2_000_000),
    )(seq, q_t, k_t, v_t, do_blocks, hi, top, total, cosine, sine)


def finish_ff(gff, gain, w_gate, w_up):
    def body(gff, gain, w_gate, w_up, gate, up, down, dgain, total):
        f = pl.program_id(0)
        rows = gain[...]
        g, u = gff[0, 0].astype(F32), gff[0, 1].astype(F32)
        gate[...] = g * rows
        up[...] = u * rows
        down[...] = gff[0, 2].astype(F32)
        part = g * w_gate[...].astype(F32) + u * w_up[...].astype(F32)
        part = jnp.sum(part, axis=1, keepdims=True)

        @pl.when(f == 0)
        def _():
            total[...] = part

        @pl.when(f > 0)
        def _():
            total[...] += part

        dgain[...] = jnp.broadcast_to(total[...], (SHARD, 128)).T[:1]

    block = pl.BlockSpec((SHARD, FSH), lambda f: (0, f))
    column = pl.BlockSpec((SHARD, 1), lambda f: (0, 0))
    return pl.pallas_call(
        body,
        grid=(DP,),
        out_shape=(
            shape(SHARD, FF, dtype=F32),
            shape(SHARD, FF, dtype=F32),
            shape(SHARD, FF, dtype=F32),
            shape(1, SHARD, dtype=F32),
        ),
        in_specs=[pl.BlockSpec((1, 3, SHARD, FSH), lambda f: (f, 0, 0, 0)), column, block, block],
        out_specs=[block, block, block, pl.BlockSpec((1, SHARD), lambda f: (0, 0))],
        scratch_shapes=[pltpu.VMEM((SHARD, 1), F32)],
        compiler_params=pltpu.CompilerParams(vmem_limit_bytes=56 << 20),
    )(gff, gain, w_gate, w_up)


def finish_attention(gqkv, gout, gain, w_query, w_key, w_value):
    def body(gqkv, gout, gain, w_query, w_key, w_value, dq, dk, dv, do, dgain):
        rows = gain[...]
        for g in range(HK):
            block = gqkv[2 * g : 2 * g + 2].reshape(SHARD, GROUP).astype(F32)
            dq[:, g * 2 * HD : (g + 1) * 2 * HD] = block[:, : 2 * HD]
            dk[:, g * HD : (g + 1) * HD] = block[:, 2 * HD : 3 * HD]
            dv[:, g * HD : (g + 1) * HD] = block[:, 3 * HD :]
        total = jnp.zeros((SHARD, 1), F32)
        for grad, weight in ((dq, w_query), (dk, w_key), (dv, w_value)):
            total += jnp.sum(grad[...] * weight[...].astype(F32), axis=1, keepdims=True)
            grad[...] = grad[...] * rows
        dgain[...] = jnp.broadcast_to(total, (SHARD, 128)).T[:1]
        do[...] = gout[...].astype(F32)

    return pl.pallas_call(
        body,
        out_shape=(
            shape(SHARD, D, dtype=F32),
            shape(SHARD, HK * HD, dtype=F32),
            shape(SHARD, HK * HD, dtype=F32),
            shape(SHARD, D, dtype=F32),
            shape(1, SHARD, dtype=F32),
        ),
        in_specs=[VMEM] * 6,
        out_specs=[VMEM] * 5,
        compiler_params=pltpu.CompilerParams(vmem_limit_bytes=56 << 20),
    )(gqkv, gout, gain, w_query, w_key, w_value)


def dot(left, right, contract):
    return lax.dot_general(left, right, (contract, ((), ())), preferred_element_type=F32)


def on_device(
    layer_input,
    cotangent,
    attn_gain,
    w_query,
    w_key,
    w_value,
    w_out,
    mlp_gain,
    w_gate,
    w_up,
    w_down,
    doc_lengths,
    rope_pos,
    pad_lengths,
):
    ctx = lax.axis_index("ctx")
    row, col = ctx // 4, lax.rem(ctx, 4)
    rank = lax.rem(ctx, 2)
    gain_a = attn_gain.astype(F32)
    gain_m = mlp_gain.astype(F32)

    inputs = layer_input[0].astype(F32)
    inv_one = lax.rsqrt(jnp.mean(inputs * inputs, axis=-1, keepdims=True) + EPSILON)
    u1 = inputs * inv_one

    wgrp = jnp.concatenate(
        [w_query.reshape(SHARD, HK, 2 * HD), w_key.reshape(SHARD, HK, HD), w_value.reshape(SHARD, HK, HD)],
        axis=2,
    )
    wgrp = (wgrp.astype(F32) * gain_a[:, None, None]).astype(BF).transpose(1, 0, 2)
    w_out_t = w_out.T

    def wide_piece(w):
        rows = lax.dynamic_slice_in_dim(w, row * 48, 48, 0).reshape(48, DP, 4, 128)
        return lax.dynamic_slice_in_dim(rows, col, 1, 2)[:, :, 0].transpose(1, 0, 2)

    gains = lax.dynamic_slice_in_dim(gain_m, row * 48, 48, 0)[None, :, None]
    wpiece = jnp.stack(
        [
            (wide_piece(w_gate).astype(F32) * gains).astype(BF),
            (wide_piece(w_up).astype(F32) * gains).astype(BF),
            wide_piece(w_down.T),
        ],
        axis=1,
    )
    pos = jnp.broadcast_to(rope_pos.astype(F32), (16, BLOCK))

    seq, posq, wjob, wo, wfp = first_exchange(u1.astype(BF), pos, wgrp, w_out_t, wpiece)
    wo = wo.reshape(D, D)

    freq = THETA_BASE ** (-(jnp.arange(HD // 2).astype(F32) * 2.0 / HD))
    angles = freq[:, None] * posq[:, 0, :].reshape(1, LENGTH)
    cosine, sine = jnp.cos(angles), jnp.sin(angles)

    ends = jnp.cumsum(doc_lengths[0])
    token = jnp.arange(LENGTH, dtype=jnp.int32)
    seg = jnp.sum(token[:, None] >= ends[None, :], axis=-1)
    doc_end = jnp.sum(jnp.where(seg[:, None] == jnp.arange(4)[None, :], ends[None, :], 0), axis=-1)
    hi = jnp.minimum(token + WINDOW - 1, doc_end - 1)
    hi = jnp.where(token >= LENGTH - pad_lengths[0], token, hi)
    hi = jnp.broadcast_to(hi[:, None], (LENGTH, 128)).astype(jnp.int32)

    dd = cotangent[0]
    q_t, k_t, v_t, top, total, att, wf, cot, wdh = attend(
        seq, wjob, cosine, sine, hi, wfp, dd, wgrp
    )
    att = att.reshape(D, BLOCK)
    resid = inputs + dot(att, wo, ((0,), (1,)))
    inv_two = lax.rsqrt(jnp.mean(resid * resid, axis=-1, keepdims=True) + EPSILON)
    u2 = resid * inv_two
    hid = middle_exchange(u2.astype(BF)).reshape(DP * BLOCK, D)
    cot = cot.reshape(DP * BLOCK, D)
    wf = wf.reshape(3, D, FSH)
    gate = dot(hid, wf[0], ((1,), (0,)))
    up = dot(hid, wf[1], ((1,), (0,)))
    sig = jax.nn.sigmoid(gate)
    act = gate * sig
    mixed = (act * up).astype(BF)
    dmix = dot(cot, wf[2], ((1,), (0,)))
    dgate = (dmix * up * sig * (1.0 + gate * (1.0 - sig))).astype(BF)
    dup = (dmix * act).astype(BF)
    ypart = dot(mixed, wf[2], ((1,), (1,))).astype(BF).reshape(DP, BLOCK, D)
    epart = dot(dgate, wf[0], ((1,), (1,))) + dot(dup, wf[1], ((1,), (1,)))
    dwf = jnp.stack(
        [
            dot(hid, dgate, ((0,), (0,))).astype(BF),
            dot(hid, dup, ((0,), (0,))).astype(BF),
            dot(cot, mixed, ((0,), (0,))).astype(BF),
        ]
    ).reshape(3, DP, SHARD, FSH)

    e2, piece = back_exchange(epart.astype(BF).reshape(DP, BLOCK, D), dwf)
    dy = dd.astype(F32)
    dresid = dy + inv_two * (e2 - u2 * jnp.mean(e2 * u2, axis=-1, keepdims=True))
    da = dresid.astype(BF)
    dat = dot(wo, da, ((0,), (1,))).astype(BF).reshape(CTX, HD, BLOCK)
    da_t = da.T.reshape(DP, SHARD, BLOCK)

    do_blocks, att_all, da_all, grads = heads_out(dat, att, da_t, piece)
    dqkv, dwj = attend_back(seq, q_t, k_t, v_t, do_blocks, hi, top, total, cosine, sine)
    dwo = dot(da_all, att_all, ((0, 2), (0, 2))).astype(BF)

    back, pair, opiece = grads_home(dqkv, dwj, dwo)
    back = back.reshape(DP, 2, 3 * HD, BLOCK)
    both = back[:, 0, HD:].astype(F32) + back[:, 1, HD:].astype(F32)
    group = jnp.concatenate([back[:, 0, :HD], back[:, 1, :HD], both.astype(BF)], axis=1)
    dh1 = lax.dot_general(
        group.transpose(0, 2, 1).reshape(DP * BLOCK, GROUP),
        wdh.reshape(D, GROUP),
        (((1,), (1,)), ((), ())),
        preferred_element_type=F32,
    )

    e1, ysum, gff, gqkv, gout = last_exchange(
        dh1.astype(BF).reshape(DP, BLOCK, D), ypart, grads, pair, opiece
    )
    output = (resid + ysum).astype(BF)
    grad_in = dresid + inv_one * (e1 - u1 * jnp.mean(e1 * u1, axis=-1, keepdims=True))

    dwg, dwu, dwd, dgain_m = finish_ff(gff, gain_m[:, None], w_gate, w_up)
    dwq, dwk, dwv, dwo, dgain_a = finish_attention(
        gqkv, gout, gain_a[:, None], w_query, w_key, w_value
    )
    return (
        output[None],
        grad_in.astype(BF)[None],
        dgain_a[0],
        dwq,
        dwk,
        dwv,
        dwo.T,
        dgain_m[0],
        dwg,
        dwu,
        dwd.T,
    )


def solution(mesh):
    in_specs = (
        P("dp", "ctx", None),
        P("dp", "ctx", None),
        P("dp"),
        P("dp", None),
        P("dp", None),
        P("dp", None),
        P(None, "dp"),
        P("dp"),
        P("dp", None),
        P("dp", None),
        P(None, "dp"),
        P("dp", None),
        P("dp", "ctx"),
        P("dp"),
    )
    out_specs = (
        P("dp", "ctx", None),
        P("dp", "ctx", None),
        P("dp"),
        P("dp", None),
        P("dp", None),
        P("dp", None),
        P(None, "dp"),
        P("dp"),
        P("dp", None),
        P("dp", None),
        P(None, "dp"),
    )
    return jax.shard_map(
        on_device, mesh=mesh, in_specs=in_specs, out_specs=out_specs, check_vma=False
    )
```

time: 442 us -> 366 us (0.83)
  the two profiles are of different devices: /device:TPU:1 before, /device:TPU:24 now
where the time goes in v2:
time: 366 us; the launch traced here: 361 us
  Pallas kernels  290 us (79%)
  matrix products  37.1 us (10%)
  local copies, waits for them, and re-layouts  17.1 us (5%)
  other arithmetic  14.1 us (4%)
    pallas_call x6, Pallas kernels, call(): pl.pallas_call(body, out_shape=outs, in_specs=[ANY] * len(args), out_spec...  220 us
    pallas_call x1, Pallas kernels, attend(): pl.pallas_call(body, out_shape=(shape(HD, LENGTH), shape(HD, LENGTH), sha...  42.1 us
    dot_general x12, matrix products, dot(): lax.dot_general(left, right, (contract, ((), ())), preferred_element_type...  32.3 us
    pallas_call x1, Pallas kernels, attend_back(): pl.pallas_call(body, out_shape=(shape(3 * HD, LENGTH), shape(DP, SHARD, G...  14 us
    pallas_call x1, Pallas kernels, finish_ff(): pl.pallas_call(body, grid=(DP,), out_shape=(shape(SHARD, FF, dtype=F32),...  9.92 us

profile of v2, /device:TPU:24, one launch (start us, length us, event | category | flops | bytes accessed | tf_op | source)
XLA Modules:
  0.0 360.6 jit_solution(12125678701420647733)
XLA Ops:
  0.7 1.3 constant_dynamic-slice_fusion.2
  2.0 0.3 reshape.177
  2.3 0.2 constant_dynamic-slice_fusion.1
  2.5 0.3 reshape.176
  2.8 0.2 constant_dynamic-slice_fusion.3
  3.1 0.1 fusion.18
  3.2 0.3 reshape.178
  3.5 0.2 constant_dynamic-slice_fusion
  3.8 0.7 pad_maximum_fusion.2.wpiece
  4.6 0.6 reshape.173
  5.2 0.2 copy.44
  5.3 0.4 reshape.174
  5.9 0.4 reshape.175
  6.4 1.6 fusion.2.wgrp
  8.0 0.2 fusion.11
  8.2 0.9 fusion.5.h1
  9.1 0.6 broadcast_in_dim.25.pos
  9.7 44.2 %shard_map.221 = (bf16[16,128,1536]{2,1,0:T(8,128)(2,1)}, f32[16,16,128]{2,1,0:T(8,128)}, bf16[8,192,384]{2,1,0:T(8,128)(2,1)}, bf16[8,192,1536]{2,1,0:T(8,128)(2,1)}, bf16[3,8,48,128]{3,2,1,0:T(8,128)(2,1)}) custom-call(bf16[128,1536]{1,0:T(8,128)(2,1)} %fusion.5.h1, f32[16,128]{1,0:T(8,128)} %broadcast_in_dim.25.pos, bf16[8,192,384]{2,1,0:T(8,128)(2,1)} %fusion.2.wgrp, ...), custom_call_target="tpu_custom_call" | custom-call | tf_op jit(solution)/shard_map/pallas_call | solution.py:393
  53.9 0.8 slice.30
  54.7 2.5 multiply_sine_fusion
  57.2 0.2 reduce-window.8
  57.4 0.1 convert_reduce_fusion
  58.3 1.4 broadcast_in_dim.27.hi
  59.6 42.1 %shard_map.222 = (bf16[96,2048]{1,0:T(8,128)(2,1)}, bf16[96,2048]{1,0:T(8,128)(2,1)}, bf16[96,2048]{1,0:T(8,128)(2,1)}, f32[1,2048]{1,0:T(1,128)}, f32[1,2048]{1...) custom-call(bf16[16,128,1536]{2,1,0:T(8,128)(2,1)} %get-tuple-elemen, ...), custom_call_target="tpu_custom_call" | custom-call | tf_op jit(solution)/shard_map/pallas_call | solution.py:938
  101.8 4.0 %fusion.20 = (bf16[1,8,192,512]{3,2,1,0:T(8,128)(2,1)S(1)}, bf16[1,8,192,512]{3,2,1,0:T(8,128)(2,1)}, bf16[1,8,192,512]{3,2,1,0:T(8,128)(2,1)S(1)}) fusion(bf16[3,8,192,512]{3,2,1,0:T(8,128)(2,1)} %get-tuple-element.60), kind=kLoop, calls=%fused_computation.71 | loop fusion | bytes 9437184 | tf_op jit(solution)/shard_map/slice | solution.py:1179
  105.8 3.1 fusion.23
  108.9 1.7 multiply_reduce_fusion.1
  110.7 0.9 multiply_convert_fusion.4.h2
  111.5 18.9 %shard_map.223 = bf16[8,128,1536]{2,1,0:T(8,128)(2,1)} custom-call(bf16[128,1536]{1,0:T(8,128)(2,1)} %multiply_convert_fusion.4.h2), custom_call_target="tpu_custom_call" | custom-call | tf_op jit(solution)/shard_map/pallas_call | solution.py:393
  130.5 4.3 %fusion.24 = f32[1024,512]{1,0:T(8,128)S(1)} fusion(bf16[1024,1536]{1,0:T(8,128)(2,1)} %bitcast.121, bf16[1536,512]{1,0:T(8,128)(2,1)} %bitcast.127), kind=kOutput, calls=%fused_computation.75 | convolution fusion | flops 1610612736 | bytes 6815744 | tf_op jit(solution)/shard_map/dot_general | solution.py:1101
  134.8 2.6 multiply_convert_fusion.1
  137.5 3.5 convolution_convert_fusion
  141.0 1.9 convolution_convert_fusion.4
  142.8 1.9 convolution_convert_fusion.3
  144.7 1.8 convolution_convert_fusion.2
  146.6 2.5 pad_maximum_fusion.dwf
  149.0 1.8 fusion.25
  150.9 3.5 add_convert_fusion
  154.4 43.8 %shard_map.224 = (f32[128,1536]{1,0:T(8,128)}, bf16[3,8,48,128]{3,2,1,0:T(8,128)(2,1)}) custom-call(bf16[8,128,1536]{2,1,0:T(8,128)(2,1)} %bitcast.117, bf16[3,8,192,512]{3,2,1,0:T(8,128)(2,1)} %pad_maximum_fusion.dwf), custom_call_target="tpu_custom_call" | custom-call | tf_op jit(solution)/shard_map/pallas_call | solution.py:393
  198.2 1.4 multiply_reduce_fusion
  199.7 0.2 convert_bitcast_fusion
  199.9 2.2 convolution_convert_fusion.5
  202.1 0.9 copy.51
  203.0 27.1 %shard_map.225 = (bf16[16,96,128]{2,1,0:T(8,128)(2,1)}, bf16[8,1536,128]{2,1,0:T(8,128)(2,1)}, bf16[8,192,128]{2,1,0:T(8,128)(2,1)}, bf16[8,3,48,128]{3,2,1,0:T(8,128)(2,1)}) custom-call(bf16[16,96,128]{2,1,0:T(8,128)(2,1)} %bitcast.136, bf16[1536,128]{1,0:T(8,128)(2,1)} %bitcast.134, bf16[8,192,128]{2,1,0:T(8,128)(2,1)} %bitcast.137, ...), custom_call_target="tpu_custom_call" | custom-call | tf_op jit(solution)/shard_map/pallas_call | solution.py:393
  230.1 4.0 %fusion.dwo = bf16[192,1536]{1,0:T(8,128)(2,1)} fusion(bf16[8,192,128]{2,1,0:T(8,128)(2,1)} %get-tuple-element.68, bf16[8,1536,128]{2,1,0:T(8,128)(2,1)} %get-tuple-element.69), kind=kOutput, calls=%fused_computation.8 | convolution fusion | flops 604274688 | bytes 4128768 | tf_op jit(solution)/shard_map/dot_general | solution.py:1101
  234.1 14.0 %shard_map.226 = (bf16[288,2048]{1,0:T(8,128)(2,1)}, bf16[8,192,384]{2,1,0:T(8,128)(2,1)}) custom-call(bf16[16,128,1536]{2,1,0:T(8,128)(2,1)} %get-tuple-element.50.seq, bf16[96,2048]{1,0:T(8,128)(2,1)} %get-tuple-element.56.q_t, bf16[96,2048]{1,0:T(8,128)(2,1)} %get-tuple-element.57.k_t, bf16[96,2048]{1,0:T(8,128)(2,1)} %get-tuple-element.58.v_t, ...), custom_call_target="tpu_custom_call" | custom-call | flops 4400000000 | bytes 12582912 | tf_op jit(solution)/shard_map/pallas_call | solution.py:1009
  248.1 38.0 %shard_map.227 = (bf16[16,288,128]{2,1,0:T(8,128)(2,1)}, bf16[96,384]{1,0:T(8,128)(2,1)}, bf16[48,384]{1,0:T(8,128)(2,1)}) custom-call(bf16[288,2048]{1,0:T(8,128)(2,1)} %get-tuple-element.66.dqkv, bf16[8,192,384]{2,1,0:T(8,128)(2,1)} %get-tuple-element.67.dwj, bf16[192,1536]{1,0:T(8,128)(2,1)} %fusion.dwo), custom_call_target="tpu_custom_call" | custom-call | tf_op jit(solution)/shard_map/pallas_call | solution.py:393
  286.1 1.2 fusion.22
  287.3 0.2 copy.63
  287.5 0.2 copy.64
  287.7 0.1 fusion.12
  287.9 1.1 fusion.21
  288.9 0.2 copy.61
  289.1 0.2 copy.62
  289.3 0.4 pad_maximum_fusion.1
  289.8 4.8 %convolution_convert_fusion.1 = bf16[1024,1536]{1,0:T(8,128)(2,1)} fusion(bf16[1024,384]{1,0:T(8,128)(2,1)S(1)} %bitcast.142, bf16[1536,384]{1,0:T(8,128)(2,1)} %bitcast.153), kind=kOutput, calls=%fused_computation.3 | convolution fusion | flops 1209532416 | bytes 5111808 | tf_op jit(solution)/shard_map/dot_general | solution.py:1211
  294.5 47.7 %shard_map.228 = (f32[128,1536]{1,0:T(8,128)}, f32[128,1536]{1,0:T(8,128)}, bf16[8,3,192,512]{3,2,1,0:T(8,128)(2,1)}, bf16[16,96,384]{2,1,0:T(8,128)(2,1)}, bf16[192,1536]{1,0:T(8,128)(2,1)}) custom-call(bf16[8,128,1536]{2,1,0:T(8,128)(2,1)} %bitcast.125, bf16[8,128,1536]{2,1,0:T(8,128)(2,1)} %bitcast.120, bf16[8,3,48,128]{3,2,1,0:T(8,128)(2,1)} %get-tuple-element.72.grads, ...), custom_call_target="tpu_custom_call" | custom-call | tf_op jit(solution)/shard_map/pallas_call | solution.py:393
  342.3 0.8 copy.57.gain
  343.1 9.9 %shard_map.230 = (f32[192,4096]{1,0:T(8,128)}, f32[192,4096]{1,0:T(8,128)}, f32[192,4096]{1,0:T(8,128)}, f32[1,192]{1,0:T(1,128)}) custom-call(bf16[8,3,192,512]{3,2,1,0:T(8,128)(2,1)} %get-tuple-element.84.gff, f32[192,1]{1,0:T(8,128)} %copy.57.gain, bf16[192,4096]{1,0:T(8,128)(2,1)} %w_gate.1, bf16[192,4096]{1,0:T(8,128)(2,1)} %w_up.1), custom_call_target="tpu_custom_call" | custom-call | tf_op jit(solution)/shard_map/pallas_call | solution.py:1054
  353.0 0.8 copy.56.gain
  353.8 4.4 %shard_map.229 = (f32[192,1536]{1,0:T(8,128)}, f32[192,768]{1,0:T(8,128)}, f32[192,768]{1,0:T(8,128)}, f32[192,1536]{1,0:T(8,128)}, f32[1,192]{1,0:T(1,128)}) custom-call(bf16[16,96,384]{2,1,0:T(8,128)(2,1)} %get-tuple-element.77.gqkv, bf16[192,1536]{1,0:T(8,128)(2,1)} %get-tuple-element.78.gout, f32[192,1]{1,0:T(8,128)} %copy.56.gain, ...), custom_call_target="tpu_custom_call" | custom-call | tf_op jit(solution)/shard_map/pallas_call | solution.py:1085
  358.2 0.3 fusion.6
  358.5 1.1 fusion.14
  359.5 0.8 fusion.13
  (66 shorter events, 0.5 us)
Async XLA Ops:
  0.6 2.5 copy-start
  0.7 2.3 copy-start.21
  2.7 1.8 copy-start.18
  2.8 1.8 copy-start.7
  3.5 1.8 copy-start.14
  4.5 1.3 copy-start.13
  5.9 2.1 copy-start.2
  6.4 2.7 copy-start.19
  8.1 49.1 %copy-start.20 = (s32[1,4]{1,0:T(1,128)S(1)}, s32[1,4]{1,0:T(1,128)}, u32[]{:S(2)}) copy-start(s32[1,4]{1,0:T(1,128)} %param.25) | copy-start | bytes 52
  101.7 4.0 %copy-start.16 = (bf16[8,128,1536]{2,1,0:T(8,128)(2,1)S(1)}, bf16[8,128,1536]{2,1,0:T(8,128)(2,1)}, u32[]{:S(2)}) copy-start(bf16[8,128,1536]{2,1,0:T(8,128)(2,1)} %get-tuple-element.59) | copy-start | bytes 9437188
  101.7 7.1 %slice-start = ((s8[4718592]{0:T(1024)(128)(4,1)}), s8[4194304]{0:T(1024)(128)(4,1)S(1)}, s32[]{:S(2)}) async-start(s8[4718592]{0:T(1024)(128)(4,1)} %bitcast.113), calls=%async_computation | async-start | bytes 8388608
  105.8 3.1 copy-start.10
  105.8 3.1 slice-start.1
  105.8 3.1 copy-start.12
  130.5 4.3 %copy-start.3 = (bf16[8,128,1536]{2,1,0:T(8,128)(2,1)S(1)}, bf16[8,128,1536]{2,1,0:T(8,128)(2,1)}, u32[]{:S(2)}) copy-start(bf16[8,128,1536]{2,1,0:T(8,128)(2,1)} %shard_map.223) | copy-start | bytes 9437188
  130.5 4.3 %copy-start.22 = (f32[1024,512]{1,0:T(8,128)S(1)}, f32[1024,512]{1,0:T(8,128)}, u32[]{:S(2)}) copy-start(f32[1024,512]{1,0:T(8,128)} %fusion.23) | copy-start | bytes 6291460
  134.8 2.7 copy-start.11
  142.8 1.9 copy-start.17
  146.6 2.5 copy-start.9
  154.4 45.3 %copy-start.8 = (bf16[1,128,1536]{2,1,0:T(8,128)(2,1)S(1)}, bf16[1,128,1536]{2,1,0:T(8,128)(2,1)}, u32[]{:S(2)}) copy-start(bf16[1,128,1536]{2,1,0:T(8,128)(2,1)} %param.15) | copy-start | bytes 1179652
  198.2 1.5 copy-start.6
  353.0 5.2 %copy-start.4 = (f32[128,1536]{1,0:T(8,128)S(1)}, f32[128,1536]{1,0:T(8,128)}, u32[]{:S(2)}) copy-start(f32[128,1536]{1,0:T(8,128)} %get-tuple-element.76) | copy-start | bytes 2359300
  353.8 4.7 %copy-start.5 = (f32[128,1536]{1,0:T(8,128)S(1)}, f32[128,1536]{1,0:T(8,128)}, u32[]{:S(2)}) copy-start(f32[128,1536]{1,0:T(8,128)} %get-tuple-element.76) | copy-start | bytes 2359300
  358.2 1.3 copy-start.15
  358.4 1.9 copy-start.1

commit v3 on v2

--- a/solution.py
+++ b/solution.py
@@ -227,33 +227,41 @@
     def __init__(self, net, p, own, slot, part):
         self.net, self.p, self.slot, self.part = net, p, slot, part
         here = slot(p.dp)
-        self.kept = net.copy(own, here)
+        self.kept = [] if own is None else [net.copy(own, here)]
+        own = here if own is None else own
         self.near = {k: net.remote(own, here, p.at_z(k)) for k in (1, 3)}
-        self.rest = [net.remote(own, here, p.sibling())]
+        self.swap = {0: [net.remote(own, here, p.sibling())]}
         self.far = {}
 
-    def forward(self):
+    def forward(self, *ks):
         net, p = self.net, self.p
-        for k in (1, 3):
+        for k in ks or (1, 3):
             self.near[k].wait_recv()
             block = self.slot(mod(p.z - k, 4) * 2 + p.core)
             cut = self.part(block, k // 2)
             self.far[k] = net.remote(cut, cut, p.at_z(k))
-            self.rest.append(net.remote(block, block, p.sibling()))
+            self.swap[k] = [net.remote(block, block, p.sibling())]
 
     def finish(self):
         net, p = self.net, self.p
+        self.swap[2] = []
         for k in (1, 3):
             self.far[k].wait_recv()
             cut = self.part(self.slot(mod(p.z + 2, 4) * 2 + p.core), k // 2)
-            self.rest.append(net.remote(cut, cut, p.sibling()))
-
-    def end(self):
+            self.swap[2].append(net.remote(cut, cut, p.sibling()))
+
+    def arrive(self, k):
+        for copy in self.swap[k]:
+            copy.wait_recv()
+
+    def end(self, arrived=False):
         for copy in (*self.near.values(), *self.far.values()):
             copy.wait_send()
-        for copy in self.rest:
+        for copies in self.swap.values():
+            for copy in copies:
+                copy.wait_send() if arrived else copy.wait()
+        for copy in self.kept:
             copy.wait()
-        self.kept.wait()
 
 
 class RingSum:
@@ -294,24 +302,27 @@
 
 
 class SumDP:
-    def __init__(self, net, p, part, cut, mine, sib, through, got, out):
-        self.net, self.p, self.mine, self.sib, self.out = net, p, mine, sib, out
-        self.ring = RingSum(
-            net, p.at_z, lambda k: mine.at[mod(p.z + k, 4)], cut, through, got
-        )
-        self.loads = {}
-        for k in (2, 1, 3, 0):
-            z = mod(p.z + k, 4)
-            swap = net.remote(part(2 * z + 1 - p.core), sib.at[z], p.sibling())
-            self.loads[k] = (net.copy(part(2 * z + p.core), mine.at[z]), swap)
+    def __init__(self, net, p, part, cut, mine, sib, through, got, out, load=True):
+        self.net, self.p, self.part, self.mine, self.sib, self.out = net, p, part, mine, sib, out
+        self.ring = RingSum(net, p.at_z, lambda k: mine(mod(p.z + k, 4)), cut, through, got)
+        self.load, self.copies = load, {}
+
+    def swap(self, k):
+        net, p = self.net, self.p
+        z = mod(p.z + k, 4)
+        self.copies[k] = [net.remote(self.part(2 * z + 1 - p.core), self.sib.at[z], p.sibling())]
+        if self.load:
+            self.copies[k].append(net.copy(self.part(2 * z + p.core), self.mine(z)))
 
     def join(self, k):
-        for copy in self.loads[k]:
+        for copy in self.copies[k]:
             copy.wait()
         z = mod(self.p.z + k, 4)
-        add_all(self.mine.at[z], [self.mine.at[z], self.sib.at[z]])
+        add_all(self.mine(z), [self.mine(z), self.sib.at[z]])
 
     def begin(self):
+        for k in (2, 1, 3, 0):
+            self.swap(k)
         self.join(2)
         self.ring.start_far()
         for k in (1, 3):
@@ -470,17 +481,144 @@
     )
 
 
-def middle_exchange(h2):
-    def body(h2, h2_all, send, recv, local):
+def feed_forward(x, att, wo, cot, wf):
+    def body(
+        x, att, wo, cot, wf,
+        resid, dresid, dat, da_t, ypart, dwf,
+        xv, attv, wov, cotv, wfv, hid, mixed, dgate, dup, epart, e2, sib, t0, t1, g0, g1,
+        send, recv, local,
+    ):
         p = Place()
         net = Net(send, recv, local)
         greet(near_z(p))
-        hid = RingDP(net, p, h2, lambda i: h2_all.at[i], rows_of(64))
-        hid.forward()
-        hid.finish()
-        hid.end()
-
-    return call(body, 3, shape(DP, BLOCK, D), ANY, 10, 2, [], h2)
+        loads = [net.copy(a, b) for a, b in ((att, attv), (wo, wov), (x, xv))]
+        later = [net.copy(a, b) for a, b in ((wf, wfv), (cot, cotv))]
+        for copy in loads:
+            copy.wait()
+        rows = attv[...].reshape(D, BLOCK).T
+        y1 = xv[...].astype(F32) + dot(rows, wov[...].reshape(D, D), ((1,), (1,)))
+        resid[...] = y1
+        inv = lax.rsqrt(jnp.mean(y1 * y1, axis=-1, keepdims=True) + EPSILON)
+        hid[p.dp] = (y1 * inv).astype(BF)
+        ring = RingDP(net, p, None, lambda i: hid.at[i], rows_of(64))
+        for copy in later:
+            copy.wait()
+        w_gate, w_up, w_down = (wfv.at[i] for i in range(3))
+
+        def part(i):
+            return epart.at[i]
+
+        total = SumDP(
+            net, p, part, rows_of(64), lambda z: epart.at[2 * z + p.core], sib, (t0, t1), (g0, g1), e2,
+            load=False,
+        )
+
+        def work(k):
+            z = mod(p.z + k, 4)
+            pair = pl.ds(2 * z, 2)
+            rows = hid[pair].reshape(2 * BLOCK, D)
+            wg, wu = w_gate[...].reshape(D, FSH), w_up[...].reshape(D, FSH)
+            gate = jnp.dot(rows, wg, preferred_element_type=F32)
+            up = jnp.dot(rows, wu, preferred_element_type=F32)
+            sig = jax.nn.sigmoid(gate)
+            act = gate * sig
+            mixed[pair] = (act * up).astype(BF).reshape(2, BLOCK, FSH)
+            wd = w_down[...].reshape(D, FSH)
+            dmix = jnp.dot(cotv[pair].reshape(2 * BLOCK, D), wd, preferred_element_type=F32)
+            dg = (dmix * up * sig * (1.0 + gate * (1.0 - sig))).astype(BF)
+            du = (dmix * act).astype(BF)
+            dgate[pair] = dg.reshape(2, BLOCK, FSH)
+            dup[pair] = du.reshape(2, BLOCK, FSH)
+            e = dot(dg, wg, ((1,), (1,))) + dot(du, wu, ((1,), (1,)))
+            epart[pair] = e.astype(BF).reshape(2, BLOCK, D)
+            total.swap(k)
+
+        ring.arrive(0)
+        work(0)
+        ring.forward()
+        ring.arrive(1)
+        work(3)
+        ring.finish()
+        ring.arrive(3)
+        work(1)
+        total.join(3)
+        total.ring.start_near(3)
+        ring.arrive(2)
+        work(2)
+        total.join(1)
+        total.ring.start_near(1)
+        total.join(2)
+        total.ring.start_far()
+
+        def weights(i, left, right):
+            right = right[...].reshape(DP * BLOCK, FSH)
+            for c in range(4):
+                block = left[:, :, c * 384 : (c + 1) * 384].reshape(DP * BLOCK, 384)
+                grad = dot(block, right, ((0,), (0,)))
+                dwf[i, 2 * c : 2 * c + 2] = grad.astype(BF).reshape(2, SHARD, FSH)
+
+        weights(0, hid, dgate)
+        total.join(0)
+        total.forward()
+        weights(1, hid, dup)
+        total.end()
+        y1 = resid[...]
+        inv = lax.rsqrt(jnp.mean(y1 * y1, axis=-1, keepdims=True) + EPSILON)
+        u2 = y1 * inv
+        e = e2[...]
+        d = cotv[p.dp].astype(F32) + inv * (e - u2 * jnp.mean(e * u2, axis=-1, keepdims=True))
+        dresid[...] = d
+        da = d.astype(BF)
+        da_t[...] = da.T.reshape(DP, SHARD, BLOCK)
+        back = jnp.dot(da, wov[...].reshape(D, D), preferred_element_type=F32).astype(BF)
+        dat[...] = back.T.reshape(CTX, HD, BLOCK)
+        weights(2, cotv, mixed)
+        wd = w_down[...].reshape(D, FSH)
+        for z in range(ZN):
+            y = dot(mixed[2 * z : 2 * z + 2].reshape(2 * BLOCK, FSH), wd, ((1,), (1,)))
+            ypart[2 * z : 2 * z + 2] = y.astype(BF).reshape(2, BLOCK, D)
+        ring.end(arrived=True)
+
+    tokens = (DP, BLOCK, D)
+    hidden = (DP, BLOCK, FSH)
+    return call(
+        body,
+        3,
+        (
+            shape(BLOCK, D, dtype=F32),
+            shape(BLOCK, D, dtype=F32),
+            shape(CTX, HD, BLOCK),
+            shape(DP, SHARD, BLOCK),
+            shape(*tokens),
+            shape(3, DP, SHARD, FSH),
+        ),
+        [VMEM] * 6,
+        22,
+        6,
+        [
+            pltpu.VMEM((BLOCK, D), BF),
+            pltpu.VMEM((CTX, HD, BLOCK), BF),
+            pltpu.VMEM((DP, SHARD, D), BF),
+            pltpu.VMEM(tokens, BF),
+            pltpu.VMEM((3, DP, SHARD, FSH), BF),
+            pltpu.VMEM(tokens, BF),
+            pltpu.VMEM(hidden, BF),
+            pltpu.VMEM(hidden, BF),
+            pltpu.VMEM(hidden, BF),
+            pltpu.VMEM(tokens, BF),
+            pltpu.VMEM((BLOCK, D), F32),
+            pltpu.VMEM((ZN, BLOCK, D), BF),
+            pltpu.VMEM((BLOCK // 2, D), BF),
+            pltpu.VMEM((BLOCK // 2, D), BF),
+            pltpu.VMEM((BLOCK, D), BF),
+            pltpu.VMEM((BLOCK, D), BF),
+        ],
+        x,
+        att,
+        wo,
+        cot,
+        wf,
+    )
 
 
 def sum_dp_scratch(rows=BLOCK, lanes=D):
@@ -496,7 +634,8 @@
 
 def sum_dp(net, p, part, scratch, out):
     mine, sib, t0, t1, g0, g1 = scratch
-    return SumDP(net, p, part, rows_of(mine.shape[1] // 2), mine, sib, (t0, t1), (g0, g1), out)
+    cut = rows_of(sib.shape[1] // 2)
+    return SumDP(net, p, part, cut, lambda z: mine.at[z], sib, (t0, t1), (g0, g1), out)
 
 
 def ring_scratch(rows, lanes):
@@ -505,292 +644,6 @@
 
 def ring_buffers(refs):
     return (refs[0], refs[1]), (refs[2], refs[3])
-
-
-def back_exchange(dh2, dwf):
-    def body(dh2, dwf, out, piece, part, *rest):
-        scratch, rings, (send, recv, local) = rest[:6], rest[6:-3], rest[-3:]
-        p = Place()
-        net = Net(send, recv, local)
-        greet(near_peers(p) + near_z(p))
-        load = net.copy(dwf, part)
-        hid = sum_dp(net, p, lambda i: dh2.at[i], scratch, out)
-
-        def cut(h, y, x):
-            rows = slice(None) if y is None else pl.ds(pl.multiple_of(y * 48, 16), 48)
-            lanes = slice(None) if x is None else pl.ds(pl.multiple_of(x * 128, 128), 128)
-            return part.at[:, pl.ds(4 * h, 4), rows, lanes]
-
-        buffers = [ring_buffers(rings[4 * i : 4 * i + 4]) for i in range(4)]
-        wts = SumXY(
-            net,
-            p,
-            cut,
-            lambda ref, i: ref.at[:, pl.ds(2 * i, 2)],
-            buffers[:2],
-            buffers[2:],
-            lambda h: piece.at[:, pl.ds(4 * h, 4)],
-        )
-        load.wait()
-        wts.start()
-        hid.begin()
-        hid.forward()
-        wts.forward()
-        hid.end()
-        wts.turn()
-        wts.finish()
-        wts.end()
-
-    return call(
-        body,
-        4,
-        (shape(BLOCK, D, dtype=F32), shape(3, DP, 48, 128)),
-        [VMEM] * 2,
-        40,
-        8,
-        [
-            pltpu.VMEM((3, DP, SHARD, FSH), BF),
-            *sum_dp_scratch(),
-            *ring_scratch(SHARD, 128),
-            *ring_scratch(48, FSH),
-            *ring_scratch(48, 128),
-            *ring_scratch(48, 128),
-        ],
-        dh2,
-        dwf,
-    )
-
-
-def heads_out(dat, att, da_t, piece):
-    def body(dat, att, da_t, piece, heads, att_all, da_all, grads, send, recv, local):
-        p = Place()
-        net = Net(send, recv, local)
-        greet([p.at_ctx(k) for k in range(1, CTX)] + [p.at_dp(k) for k in range(1, DP)])
-        kept = net.copy(dat.at[p.ctx], heads.at[p.ctx])
-        sent = [
-            net.remote(dat.at[mod(p.ctx + k, CTX)], heads.at[p.ctx], p.at_ctx(k))
-            for k in range(1, CTX)
-        ]
-        atts = RingDP(net, p, att, lambda i: att_all.at[i], rows_of(D // 2))
-        das = Exchange(net, p, lambda i: da_t.at[i], lambda i: da_all.at[i])
-        wts = Exchange(net, p, lambda i: piece.at[:, i], lambda i: grads.at[i])
-        atts.forward()
-        for copy in sent:
-            copy.wait()
-        kept.wait()
-        atts.finish()
-        for part in (atts, das, wts):
-            part.end()
-
-    return call(
-        body,
-        5,
-        (
-            shape(CTX, HD, BLOCK),
-            shape(DP, D, BLOCK),
-            shape(DP, SHARD, BLOCK),
-            shape(DP, 3, 48, 128),
-        ),
-        [ANY] * 4,
-        38,
-        4,
-        [],
-        dat,
-        att,
-        da_t,
-        piece,
-    )
-
-
-def grads_home(dqkv, dwj, dwo):
-    def body(
-        dqkv, dwj, dwo, out, pair, piece, full, away, f0, s0, w0, *rest
-    ):
-        scratch, (send, recv, local) = rest[:6], rest[6:]
-        p = Place()
-        net = Net(send, recv, local)
-        group, rank = p.ctx // 2, lax.rem(p.ctx, 2)
-        home = group == p.dp
-        partner = (p.dp, p.ctx + 1 - 2 * rank)
-
-        barrier = pltpu.get_barrier_semaphore()
-        others = xy_peers(p) + z_peers(p)
-        for peer in others:
-            pl.semaphore_signal(barrier, inc=1, device_id=peer, device_id_type=MESH)
-        for i in range(DP):
-            for r in range(2):
-                own = home & (p.dp == i) & (rank == r)
-
-                @pl.when(jnp.logical_not(own))
-                def _():
-                    peer = (jnp.int32(i), 2 * p.dp + r)
-                    pl.semaphore_signal(barrier, inc=1, device_id=peer, device_id_type=MESH)
-
-        pl.semaphore_wait(barrier, CTX + len(others) - home.astype(jnp.int32))
-
-        lanes = lambda c: pl.ds(pl.multiple_of(c * BLOCK, BLOCK), BLOCK)
-        slot = p.dp * 2 + rank
-
-        def message(k, spot):
-            c = mod(p.ctx + k, CTX)
-            return pltpu.make_async_remote_copy(
-                src_ref=dqkv.at[:, lanes(c)],
-                dst_ref=out.at[spot],
-                send_sem=send.at[k],
-                recv_sem=recv.at[spot],
-                device_id=(group, c),
-                device_id_type=MESH,
-            )
-
-        own = pltpu.make_async_copy(dqkv.at[:, lanes(p.ctx)], out.at[slot], local.at[0])
-        net.m = 1
-
-        @pl.when(home)
-        def _():
-            own.start()
-
-        @pl.when(jnp.logical_not(home))
-        def _():
-            message(0, slot).start()
-
-        for k in range(1, CTX):
-            message(k, slot).start()
-        net.n = CTX
-
-        hid = sum_dp(net, p, lambda i: dwj.at[i], scratch, full)
-        wide = [net.copy(dwo.at[:, pl.ds(pl.multiple_of(p.x * 384, 128), 384)], w0)]
-        for k in (1, 3, 2):
-            cut = dwo.at[:, pl.ds(pl.multiple_of(mod(p.x + k, 4) * 384, 128), 384)]
-            wide.append(net.remote(cut, f0.at[k - 1], p.at_x(k)))
-        hid.begin()
-        for copy in wide:
-            copy.wait()
-        add_all(w0, [w0] + [f0.at[k] for k in range(3)])
-        tall = []
-        for k in (1, 3, 2):
-            cut = w0.at[pl.ds(pl.multiple_of(mod(p.y + k, 4) * 48, 16), 48)]
-            tall.append(net.remote(cut, s0.at[k - 1], p.at_y(k)))
-        hid.forward()
-        hid.end()
-        theirs = full.at[pl.ds(pl.multiple_of((1 - rank) * 96, 16), 96)]
-        swap = net.remote(theirs, away, partner)
-        for copy in tall:
-            copy.wait()
-        add_all(piece, [w0.at[pl.ds(pl.multiple_of(p.y * 48, 16), 48)]] + [s0.at[k] for k in range(3)])
-        swap.wait()
-        add_all(pair, [full.at[pl.ds(pl.multiple_of(rank * 96, 16), 96)], away])
-
-        for k in range(1, CTX):
-            message(k, slot).wait_send()
-
-        @pl.when(home)
-        def _():
-            own.wait()
-
-        @pl.when(jnp.logical_not(home))
-        def _():
-            message(0, slot).wait_send()
-
-        for spot in range(CTX):
-            here = home & (slot == spot)
-
-            @pl.when(jnp.logical_not(here))
-            def _():
-                message(0, spot).wait_recv()
-
-    return call(
-        body,
-        6,
-        (shape(CTX, 3 * HD, BLOCK), shape(96, GROUP), shape(48, 384)),
-        [ANY, VMEM, VMEM],
-        40,
-        8,
-        [
-            pltpu.VMEM((SHARD, GROUP), BF),
-            pltpu.VMEM((96, GROUP), BF),
-            pltpu.VMEM((3, SHARD, 384), BF),
-            pltpu.VMEM((3, 48, 384), BF),
-            pltpu.VMEM((SHARD, 384), BF),
-            *sum_dp_scratch(SHARD, GROUP),
-        ],
-        dqkv,
-        dwj,
-        dwo,
-    )
-
-
-def last_exchange(dh1, ypart, grads, pair, piece):
-    def body(dh1, ypart, grads, pair, piece, e1, ysum, gff, gqkv, gout, *rest):
-        scratch, (send, recv, local) = rest[:-3], rest[-3:]
-        p = Place()
-        net = Net(send, recv, local)
-        greet(xy_peers(p) + z_peers(p))
-        inp = sum_dp(net, p, lambda i: dh1.at[i], scratch[:6], e1)
-        wts = RingXY(
-            net,
-            p,
-            lambda h: grads.at[pl.ds(4 * h, 4)],
-            lambda h, y, x: gff.at[
-                pl.ds(4 * h, 4),
-                :,
-                pl.ds(pl.multiple_of(y * 48, 16), 48),
-                pl.ds(pl.multiple_of(x * 128, 128), 128),
-            ],
-            rows_of(2),
-        )
-        qkv = RingXY(
-            net,
-            p,
-            lambda h: half(pair, h, 48),
-            lambda h, y, x: gqkv.at[y * 4 + x, pl.ds(h * 48, 48)],
-            rows_of(32),
-        )
-        proj = GatherXY(
-            net,
-            p,
-            lambda h: piece.at[pl.ds(32 * h, 32 - 16 * h)],
-            lambda h, y, x: gout.at[
-                pl.ds(pl.multiple_of(y * 48 + 32 * h, 16), 32 - 16 * h),
-                pl.ds(pl.multiple_of(x * 384, 128), 384),
-            ],
-        )
-        inp.begin()
-        res = sum_dp(net, p, lambda i: ypart.at[i], scratch[6:], ysum)
-        wts.forward()
-        inp.forward()
-        qkv.forward()
-        proj.forward()
-        wts.middle()
-        inp.end()
-        res.begin()
-        qkv.middle()
-        wts.finish()
-        qkv.finish()
-        res.forward()
-        res.end()
-        for part in (wts, qkv, proj):
-            part.end()
-
-    return call(
-        body,
-        7,
-        (
-            shape(BLOCK, D, dtype=F32),
-            shape(BLOCK, D, dtype=F32),
-            shape(DP, 3, SHARD, FSH),
-            shape(CTX, 96, GROUP),
-            shape(SHARD, D),
-        ),
-        [VMEM, VMEM, ANY, ANY, ANY],
-        140,
-        24,
-        sum_dp_scratch() + sum_dp_scratch(),
-        dh1,
-        ypart,
-        grads,
-        pair,
-        piece,
-    )
 
 
 CHUNK = 256
@@ -967,23 +820,99 @@
     )(seq, wjob, cosine, sine, hi, wfp, dd, wgrp)
 
 
-def attend_back(seq, q_t, k_t, v_t, do_blocks, hi, top, total, cosine, sine):
+def backward(dat, att, da_t, dwf, ypart, wdh, seq, q_t, k_t, v_t, hi, top, total, cosine, sine):
     def body(
-        seq, q_t, k_t, v_t, do_blocks, hi, top, total, cosine, sine,
-        out, dwj, rows, k, v, q, do, do_t, dk, dv, wide, load,
+        dat, att, da_t, dwf, ypart, wdh, seq, q_t, k_t, v_t, hi, top, total, cosine, sine,
+        e1, ysum, gff, gatt,
+        rows, k, v, q, do, do_t, dk, dv, out, wide, heads, att_all, da_all, dwj, full, away, comb,
+        dwo, w0, f0, s0, back, wdh_v, dh1, part, piece, grads, *rest,
     ):
-        rank = lax.rem(lax.axis_index("ctx"), 2)
-        fetch = pltpu.make_async_copy(seq, rows, load)
-        fetch.start()
+        rings, rest = rest[:16], rest[16:]
+        j_sib, j_t0, j_t1, j_g0, j_g1, *rest = rest
+        h_sib, h_t0, h_t1, h_g0, h_g1, *rest = rest
+        y_scratch, (send, recv, local) = rest[:6], rest[6:]
+        p = Place()
+        net = Net(send, recv, local)
+        group, rank = p.ctx // 2, lax.rem(p.ctx, 2)
+        home = group == p.dp
+        partner = (p.dp, p.ctx + 1 - 2 * rank)
+
+        barrier = pltpu.get_barrier_semaphore()
+        others = [p.at_ctx(i) for i in range(1, CTX)] + [p.at_dp(i) for i in range(1, DP)]
+        for peer in others:
+            pl.semaphore_signal(barrier, inc=1, device_id=peer, device_id_type=MESH)
+        for i in range(DP):
+            for r in range(2):
+
+                @pl.when(jnp.logical_not(home & (p.dp == i) & (rank == r)))
+                def _():
+                    peer = (jnp.int32(i), 2 * p.dp + r)
+                    pl.semaphore_signal(barrier, inc=1, device_id=peer, device_id_type=MESH)
+
+        pl.semaphore_wait(barrier, CTX + len(others) - home.astype(jnp.int32))
+
+        slot = p.dp * 2 + rank
+
+        def message(b, spot):
+            return pltpu.make_async_remote_copy(
+                src_ref=out.at[:, pl.ds(b * BLOCK, BLOCK)],
+                dst_ref=back.at[spot],
+                send_sem=send.at[b],
+                recv_sem=recv.at[spot],
+                device_id=(group, jnp.int32(b)),
+                device_id_type=MESH,
+            )
+
+        def own(b):
+            return pltpu.make_async_copy(
+                out.at[:, pl.ds(b * BLOCK, BLOCK)], back.at[slot], local.at[0]
+            )
+
+        net.n, net.m = CTX, 1
+
+        kept = net.copy(dat.at[p.ctx], heads.at[p.ctx])
+        sent = [
+            net.remote(dat.at[mod(p.ctx + i, CTX)], heads.at[p.ctx], p.at_ctx(i))
+            for i in range(1, CTX)
+        ]
+        load_part = net.copy(dwf, part)
+        atts = RingDP(net, p, att, lambda i: att_all.at[i], rows_of(D // 2))
+        das = Exchange(net, p, lambda i: da_t.at[i], lambda i: da_all.at[i])
+        load_rows = net.copy(seq, rows)
+        load_wdh = net.copy(wdh, wdh_v)
+
+        def cut(h, y, x):
+            at_rows = slice(None) if y is None else pl.ds(pl.multiple_of(y * 48, 16), 48)
+            lanes = slice(None) if x is None else pl.ds(pl.multiple_of(x * 128, 128), 128)
+            return part.at[:, pl.ds(4 * h, 4), at_rows, lanes]
+
+        buffers = [ring_buffers(rings[4 * i : 4 * i + 4]) for i in range(4)]
+        wts = SumXY(
+            net,
+            p,
+            cut,
+            lambda ref, i: ref.at[:, pl.ds(2 * i, 2)],
+            buffers[:2],
+            buffers[2:],
+            lambda h: piece.at[:, pl.ds(4 * h, 4)],
+        )
+        res = sum_dp(net, p, lambda i: ypart.at[i], y_scratch, ysum)
+
         k[...] = k_t[...].T
         v[...] = v_t[...].T
         q[...] = q_t[...].T
-        for b in range(CTX):
-            do_t[:, b * BLOCK : (b + 1) * BLOCK] = do_blocks[b]
-        do[...] = do_t[...].T
         dk[...] = jnp.zeros_like(dk)
         dv[...] = jnp.zeros_like(dv)
-        for j in range(CHUNKS):
+        for copy in sent:
+            copy.wait()
+        kept.wait()
+        load_part.wait()
+        wts.start()
+        for b in range(CTX):
+            do_t[:, b * BLOCK : (b + 1) * BLOCK] = heads[b]
+        do[...] = do_t[...].T
+
+        def chunk(j):
             low, high = span(j)
             at = slice(j * CHUNK, (j + 1) * CHUNK)
             s = score_block(k, q_t, hi, j)
@@ -992,40 +921,210 @@
             inner = jnp.sum(prob * dp, axis=0, keepdims=True)
             ds = (prob * (dp - inner)).astype(BF)
             dq = jnp.dot(k_t[:, low:high], ds, preferred_element_type=F32) * SCALE
-            out[:HD, at] = turn(dq, cosine[:, at], -sine[:, at]).astype(BF)
             dk[low:high, :] += jnp.dot(ds, q[at, :], preferred_element_type=F32)
             dv[low:high, :] += jnp.dot(prob.astype(BF), do[at, :], preferred_element_type=F32)
-        out[HD : 2 * HD, :] = turn(dk[...].T * SCALE, cosine[...], -sine[...]).astype(BF)
-        out[2 * HD :, :] = dv[...].T.astype(BF)
+            cos, sin = cosine[:, at], -sine[:, at]
+            out[:HD, at] = turn(dq, cos, sin).astype(BF)
+            out[HD : 2 * HD, at] = turn(dk[at, :].T * SCALE, cos, sin).astype(BF)
+            out[2 * HD :, at] = dv[at, :].T.astype(BF)
+            for b in (2 * j, 2 * j + 1):
+                here = home & (p.ctx == b)
+
+                @pl.when(here)
+                def _():
+                    own(b).start()
+
+                @pl.when(jnp.logical_not(here))
+                def _():
+                    message(b, slot).start()
+
+        for j in reversed(range(CHUNKS)):
+            chunk(j)
+            if j == 5:
+                atts.forward()
+            if j == 2:
+                wts.forward()
+                atts.finish()
+
         mine = pl.multiple_of(rank * HD, 16)
         other = pl.multiple_of((1 - rank) * HD, 16)
         wide[pl.ds(mine, HD), :] = out[:HD, :]
         wide[pl.ds(other, HD), :] = jnp.zeros((HD, LENGTH), BF)
         wide[2 * HD :, :] = out[HD:, :]
-        fetch.wait()
+        load_rows.wait()
         grad = jnp.dot(wide[...], rows[...].reshape(LENGTH, D), preferred_element_type=F32)
         dwj[...] = grad.T.astype(BF).reshape(DP, SHARD, GROUP)
-
+        proj = SumDP(
+            net, p, lambda i: dwj.at[i], rows_of(96), lambda z: dwj.at[2 * z + p.core], j_sib,
+            (j_t0, j_t1), (j_g0, j_g1), full, load=False,
+        )
+        proj.begin()
+        wts.turn()
+
+        for i in (1, 3, 2):
+            atts.arrive(i)
+        atts.arrive(0)
+        atts.end(arrived=True)
+        das.end()
+        grad = dot(da_all[0], att_all[0], ((1,), (1,)))
+        for i in range(1, DP):
+            grad += dot(da_all[i], att_all[i], ((1,), (1,)))
+        dwo[...] = grad.astype(BF)
+        wide_cuts = [net.copy(dwo.at[:, pl.ds(pl.multiple_of(p.x * 384, 128), 384)], w0)]
+        for i in (1, 3, 2):
+            lanes = pl.ds(pl.multiple_of(mod(p.x + i, 4) * 384, 128), 384)
+            wide_cuts.append(net.remote(dwo.at[:, lanes], f0.at[i - 1], p.at_x(i)))
+        proj.forward()
+
+        load_wdh.wait()
+        for spot in range(CTX):
+
+            @pl.when(jnp.logical_not(home & (slot == spot)))
+            def _():
+                message(0, spot).wait_recv()
+
+        for b in range(CTX):
+            here = home & (p.ctx == b)
+
+            @pl.when(here)
+            def _():
+                own(b).wait()
+
+            @pl.when(jnp.logical_not(here))
+            def _():
+                message(b, slot).wait_send()
+
+        inp = SumDP(
+            net, p, lambda i: dh1.at[i], rows_of(64), lambda z: dh1.at[2 * z + p.core], h_sib,
+            (h_t0, h_t1), (h_g0, h_g1), e1, load=False,
+        )
+        for step in (2, 1, 3, 0):
+            z = mod(p.z + step, 4)
+            for core in (0, 1):
+                i = 2 * z + core
+                first, second = back[2 * i].astype(F32), back[2 * i + 1].astype(F32)
+                turned = jnp.concatenate(
+                    [first[:HD], second[:HD], first[HD:] + second[HD:]], axis=0
+                ).T.astype(BF)
+                grad = dot(turned, wdh_v[...].reshape(D, GROUP), ((1,), (1,)))
+                dh1[i] = grad.astype(BF)
+            inp.swap(step)
+        inp.join(2)
+        inp.ring.start_far()
+        for step in (1, 3):
+            inp.join(step)
+            inp.ring.start_near(step)
+        inp.join(0)
+
+        wts.finish()
+        wts.end()
+        swap = Exchange(net, p, lambda i: piece.at[:, i], lambda i: grads.at[i])
+        proj.end()
+        theirs = full.at[pl.ds(pl.multiple_of((1 - rank) * 96, 16), 96)]
+        trade = net.remote(theirs, away, partner)
+        for copy in wide_cuts:
+            copy.wait()
+        add_all(w0, [w0] + [f0.at[i] for i in range(3)])
+        tall = []
+        for i in (1, 3, 2):
+            at = pl.ds(pl.multiple_of(mod(p.y + i, 4) * 48, 16), 48)
+            tall.append(net.remote(w0.at[at], s0.at[i - 1], p.at_y(i)))
+        swap.end()
+        gather = RingXY(
+            net,
+            p,
+            lambda h: grads.at[pl.ds(4 * h, 4)],
+            lambda h, y, x: gff.at[
+                pl.ds(4 * h, 4),
+                :,
+                pl.ds(pl.multiple_of(y * 48, 16), 48),
+                pl.ds(pl.multiple_of(x * 128, 128), 128),
+            ],
+            rows_of(2),
+        )
+        trade.wait()
+        add_all(
+            comb.at[pl.ds(0, 96)], [full.at[pl.ds(pl.multiple_of(rank * 96, 16), 96)], away]
+        )
+        for copy in tall:
+            copy.wait()
+        at = pl.ds(pl.multiple_of(p.y * 48, 16), 48)
+        add_all(comb.at[pl.ds(96, 48)], [w0.at[at]] + [s0.at[i] for i in range(3)])
+        small = RingXY(
+            net,
+            p,
+            lambda h: comb.at[pl.ds(80 * h, 80 - 16 * h)],
+            lambda h, y, x: gatt.at[y * 4 + x, pl.ds(80 * h, 80 - 16 * h)],
+            rows_of(48),
+        )
+        inp.forward()
+        gather.forward()
+        small.forward()
+        inp.end()
+        res.begin()
+        gather.middle()
+        small.middle()
+        res.forward()
+        gather.finish()
+        small.finish()
+        res.end()
+        gather.end()
+        small.end()
+
+    heads = pltpu.VMEM((LENGTH, HD), BF)
     return pl.pallas_call(
         body,
-        out_shape=(shape(3 * HD, LENGTH), shape(DP, SHARD, GROUP)),
-        in_specs=[ANY] + [VMEM] * 9,
-        out_specs=[VMEM] * 2,
+        out_shape=(
+            shape(BLOCK, D, dtype=F32),
+            shape(BLOCK, D, dtype=F32),
+            shape(DP, 3, SHARD, FSH),
+            shape(CTX, 144, GROUP),
+        ),
+        in_specs=[ANY] * 7 + [VMEM] * 8,
+        out_specs=[VMEM, VMEM, ANY, ANY],
         scratch_shapes=[
             pltpu.VMEM((CTX, BLOCK, D), BF),
-            pltpu.VMEM((LENGTH, HD), BF),
-            pltpu.VMEM((LENGTH, HD), BF),
-            pltpu.VMEM((LENGTH, HD), BF),
-            pltpu.VMEM((LENGTH, HD), BF),
+            heads,
+            heads,
+            heads,
+            heads,
             pltpu.VMEM((HD, LENGTH), BF),
             pltpu.VMEM((LENGTH, HD), F32),
             pltpu.VMEM((LENGTH, HD), F32),
+            pltpu.VMEM((3 * HD, LENGTH), BF),
             pltpu.VMEM((GROUP, LENGTH), BF),
-            pltpu.SemaphoreType.DMA,
+            pltpu.VMEM((CTX, HD, BLOCK), BF),
+            pltpu.VMEM((DP, D, BLOCK), BF),
+            pltpu.VMEM((DP, SHARD, BLOCK), BF),
+            pltpu.VMEM((DP, SHARD, GROUP), BF),
+            pltpu.VMEM((SHARD, GROUP), BF),
+            pltpu.VMEM((96, GROUP), BF),
+            pltpu.VMEM((144, GROUP), BF),
+            pltpu.VMEM((SHARD, D), BF),
+            pltpu.VMEM((SHARD, 384), BF),
+            pltpu.VMEM((3, SHARD, 384), BF),
+            pltpu.VMEM((3, 48, 384), BF),
+            pltpu.VMEM((CTX, 3 * HD, BLOCK), BF),
+            pltpu.VMEM((DP, SHARD, GROUP), BF),
+            pltpu.VMEM((DP, BLOCK, D), BF),
+            pltpu.VMEM((3, DP, SHARD, FSH), BF),
+            pltpu.VMEM((3, DP, 48, 128), BF),
+            pltpu.VMEM((DP, 3, 48, 128), BF),
+            *ring_scratch(SHARD, 128),
+            *ring_scratch(48, FSH),
+            *ring_scratch(48, 128),
+            *ring_scratch(48, 128),
+            *sum_dp_scratch(SHARD, GROUP)[1:],
+            *sum_dp_scratch()[1:],
+            *sum_dp_scratch(),
+            pltpu.SemaphoreType.DMA((200,)),
+            pltpu.SemaphoreType.DMA((200,)),
+            pltpu.SemaphoreType.DMA((24,)),
         ],
-        compiler_params=pltpu.CompilerParams(vmem_limit_bytes=56 << 20),
-        cost_estimate=pl.CostEstimate(flops=4_400_000_000, bytes_accessed=12 << 20, transcendentals=2_000_000),
-    )(seq, q_t, k_t, v_t, do_blocks, hi, top, total, cosine, sine)
+        compiler_params=pltpu.CompilerParams(
+            collective_id=4, has_side_effects=True, vmem_limit_bytes=60 << 20
+        ),
+    )(dat, att, da_t, dwf, ypart, wdh, seq, q_t, k_t, v_t, hi, top, total, cosine, sine)
 
 
 def finish_ff(gff, gain, w_gate, w_up):
@@ -1067,11 +1166,14 @@
     )(gff, gain, w_gate, w_up)
 
 
-def finish_attention(gqkv, gout, gain, w_query, w_key, w_value):
-    def body(gqkv, gout, gain, w_query, w_key, w_value, dq, dk, dv, do, dgain):
+def finish_attention(gatt, gain, w_query, w_key, w_value):
+    def body(gatt, gain, w_query, w_key, w_value, dq, dk, dv, do, dgain):
         rows = gain[...]
+        for c in range(CTX):
+            y, x = divmod(c, 4)
+            do[y * 48 : (y + 1) * 48, x * 384 : (x + 1) * 384] = gatt[c, 96:].astype(F32)
         for g in range(HK):
-            block = gqkv[2 * g : 2 * g + 2].reshape(SHARD, GROUP).astype(F32)
+            block = gatt[2 * g : 2 * g + 2, :96].reshape(SHARD, GROUP).astype(F32)
             dq[:, g * 2 * HD : (g + 1) * 2 * HD] = block[:, : 2 * HD]
             dk[:, g * HD : (g + 1) * HD] = block[:, 2 * HD : 3 * HD]
             dv[:, g * HD : (g + 1) * HD] = block[:, 3 * HD :]
@@ -1080,7 +1182,6 @@
             total += jnp.sum(grad[...] * weight[...].astype(F32), axis=1, keepdims=True)
             grad[...] = grad[...] * rows
         dgain[...] = jnp.broadcast_to(total, (SHARD, 128)).T[:1]
-        do[...] = gout[...].astype(F32)
 
     return pl.pallas_call(
         body,
@@ -1091,10 +1192,10 @@
             shape(SHARD, D, dtype=F32),
             shape(1, SHARD, dtype=F32),
         ),
-        in_specs=[VMEM] * 6,
+        in_specs=[VMEM] * 5,
         out_specs=[VMEM] * 5,
         compiler_params=pltpu.CompilerParams(vmem_limit_bytes=56 << 20),
-    )(gqkv, gout, gain, w_query, w_key, w_value)
+    )(gatt, gain, w_query, w_key, w_value)
 
 
 def dot(left, right, contract):
@@ -1150,7 +1251,6 @@
     pos = jnp.broadcast_to(rope_pos.astype(F32), (16, BLOCK))
 
     seq, posq, wjob, wo, wfp = first_exchange(u1.astype(BF), pos, wgrp, w_out_t, wpiece)
-    wo = wo.reshape(D, D)
 
     freq = THETA_BASE ** (-(jnp.arange(HD // 2).astype(F32) * 2.0 / HD))
     angles = freq[:, None] * posq[:, 0, :].reshape(1, LENGTH)
@@ -1168,63 +1268,16 @@
     q_t, k_t, v_t, top, total, att, wf, cot, wdh = attend(
         seq, wjob, cosine, sine, hi, wfp, dd, wgrp
     )
-    att = att.reshape(D, BLOCK)
-    resid = inputs + dot(att, wo, ((0,), (1,)))
-    inv_two = lax.rsqrt(jnp.mean(resid * resid, axis=-1, keepdims=True) + EPSILON)
-    u2 = resid * inv_two
-    hid = middle_exchange(u2.astype(BF)).reshape(DP * BLOCK, D)
-    cot = cot.reshape(DP * BLOCK, D)
-    wf = wf.reshape(3, D, FSH)
-    gate = dot(hid, wf[0], ((1,), (0,)))
-    up = dot(hid, wf[1], ((1,), (0,)))
-    sig = jax.nn.sigmoid(gate)
-    act = gate * sig
-    mixed = (act * up).astype(BF)
-    dmix = dot(cot, wf[2], ((1,), (0,)))
-    dgate = (dmix * up * sig * (1.0 + gate * (1.0 - sig))).astype(BF)
-    dup = (dmix * act).astype(BF)
-    ypart = dot(mixed, wf[2], ((1,), (1,))).astype(BF).reshape(DP, BLOCK, D)
-    epart = dot(dgate, wf[0], ((1,), (1,))) + dot(dup, wf[1], ((1,), (1,)))
-    dwf = jnp.stack(
-        [
-            dot(hid, dgate, ((0,), (0,))).astype(BF),
-            dot(hid, dup, ((0,), (0,))).astype(BF),
-            dot(cot, mixed, ((0,), (0,))).astype(BF),
-        ]
-    ).reshape(3, DP, SHARD, FSH)
-
-    e2, piece = back_exchange(epart.astype(BF).reshape(DP, BLOCK, D), dwf)
-    dy = dd.astype(F32)
-    dresid = dy + inv_two * (e2 - u2 * jnp.mean(e2 * u2, axis=-1, keepdims=True))
-    da = dresid.astype(BF)
-    dat = dot(wo, da, ((0,), (1,))).astype(BF).reshape(CTX, HD, BLOCK)
-    da_t = da.T.reshape(DP, SHARD, BLOCK)
-
-    do_blocks, att_all, da_all, grads = heads_out(dat, att, da_t, piece)
-    dqkv, dwj = attend_back(seq, q_t, k_t, v_t, do_blocks, hi, top, total, cosine, sine)
-    dwo = dot(da_all, att_all, ((0, 2), (0, 2))).astype(BF)
-
-    back, pair, opiece = grads_home(dqkv, dwj, dwo)
-    back = back.reshape(DP, 2, 3 * HD, BLOCK)
-    both = back[:, 0, HD:].astype(F32) + back[:, 1, HD:].astype(F32)
-    group = jnp.concatenate([back[:, 0, :HD], back[:, 1, :HD], both.astype(BF)], axis=1)
-    dh1 = lax.dot_general(
-        group.transpose(0, 2, 1).reshape(DP * BLOCK, GROUP),
-        wdh.reshape(D, GROUP),
-        (((1,), (1,)), ((), ())),
-        preferred_element_type=F32,
-    )
-
-    e1, ysum, gff, gqkv, gout = last_exchange(
-        dh1.astype(BF).reshape(DP, BLOCK, D), ypart, grads, pair, opiece
+    resid, dresid, dat, da_t, ypart, dwf = feed_forward(layer_input[0], att, wo, cot, wf)
+    e1, ysum, gff, gatt = backward(
+        dat, att.reshape(D, BLOCK), da_t, dwf, ypart, wdh,
+        seq, q_t, k_t, v_t, hi, top, total, cosine, sine,
     )
     output = (resid + ysum).astype(BF)
     grad_in = dresid + inv_one * (e1 - u1 * jnp.mean(e1 * u1, axis=-1, keepdims=True))
 
     dwg, dwu, dwd, dgain_m = finish_ff(gff, gain_m[:, None], w_gate, w_up)
-    dwq, dwk, dwv, dwo, dgain_a = finish_attention(
-        gqkv, gout, gain_a[:, None], w_query, w_key, w_value
-    )
+    dwq, dwk, dwv, dwo, dgain_a = finish_attention(gatt, gain_a[:, None], w_query, w_key, w_value)
     return (
         output[None],
         grad_in.astype(BF)[None],

time: 366 us -> 299 us (0.82)
  the two profiles are of different devices: /device:TPU:24 before, /device:TPU:1 now
where the time goes in v3:
time: 299 us; the launch traced here: 294 us
  Pallas kernels  274 us (92%)
  local copies, waits for them, and re-layouts  9.01 us (3%)
  other arithmetic  8.78 us (3%)
    pallas_call x1, Pallas kernels, backward(): pl.pallas_call(body, out_shape=(shape(BLOCK, D, dtype=F32), shape(BLOCK,...  120 us
    pallas_call x2, Pallas kernels, call(): pl.pallas_call(body, out_shape=outs, in_specs=[ANY] * len(args), out_spec...  98.1 us
    pallas_call x1, Pallas kernels, attend(): pl.pallas_call(body, out_shape=(shape(HD, LENGTH), shape(HD, LENGTH), sha...  41.7 us
    pallas_call x1, Pallas kernels, finish_ff(): pl.pallas_call(body, grid=(DP,), out_shape=(shape(SHARD, FF, dtype=F32),...  9.92 us

profile of v3, /device:TPU:1, one launch (start us, length us, event | category | flops | bytes accessed | tf_op | source)
XLA Modules:
  0.0 293.6 jit_solution(14974513788338854660)
XLA Ops:
  0.6 0.0 copy-start
  0.7 0.0 copy-start.14
  0.7 1.3 constant_dynamic-slice_fusion.2
  2.0 0.3 reshape.112
  2.3 0.2 constant_dynamic-slice_fusion.1
  2.5 0.0 copy-start.11
  2.5 0.0 copy-start.5
  2.5 0.3 reshape.111
  2.8 0.2 constant_dynamic-slice_fusion.3
  3.0 0.0 copy-done.14
  3.0 0.1 dynamic_slice.23
  3.1 0.1 fusion.14
  3.2 0.0 copy-done
  3.2 0.0 copy-start.7
  3.3 0.3 reshape.113
  3.5 0.2 constant_dynamic-slice_fusion
  3.8 0.7 pad_maximum_fusion.wpiece
  4.5 0.0 copy-done.11
  4.5 0.0 copy-start.6
  4.5 0.0 copy-done.5
  4.6 0.6 reshape.108
  5.2 0.2 copy.36
  5.3 0.0 copy-done.7
  5.3 0.4 reshape.109
  5.8 0.0 copy-start.2
  5.8 0.1 copy.37
  5.9 0.0 copy-done.6
  5.9 0.4 reshape.110
  6.3 0.0 copy-start.12
  6.3 0.1 copy.38
  6.4 1.6 fusion.wgrp
  8.0 0.0 copy-done.2
  8.0 0.0 copy-start.13
  8.0 0.2 fusion.9
  8.2 0.9 fusion.3.h1
  9.0 0.0 copy-done.12
  9.1 0.6 broadcast_in_dim.25.pos
  9.7 44.7 %shard_map.221 = (bf16[16,128,1536]{2,1,0:T(8,128)(2,1)}, f32[16,16,128]{2,1,0:T(8,128)}, bf16[8,192,384]{2,1,0:T(8,128)(2,1)}, bf16[8,192,1536]{2,1,0:T(8,128)(2,1)}, bf16[3,8,48,128]{3,2,1,0:T(8,128)(2,1)}) custom-call(bf16[128,1536]{1,0:T(8,128)(2,1)} %fusion.3.h1, f32[16,128]{1,0:T(8,128)} %broadcast_in_dim.25.pos, bf16[8,192,384]{2,1,0:T(8,128)(2,1)} %fusion.wgrp, ...), custom_call_target="tpu_custom_call" | custom-call | tf_op jit(solution)/shard_map/pallas_call | solution.py:404
  54.3 0.8 slice.3
  55.2 2.7 multiply_sine_fusion
  57.9 0.0 copy-done.13
  57.9 0.2 reduce-window.8
  58.1 0.1 convert_reduce_fusion
  58.2 0.1 select_reduce_fusion
  59.0 1.3 broadcast_in_dim.27.hi
  60.3 41.7 %shard_map.222 = (bf16[96,2048]{1,0:T(8,128)(2,1)}, bf16[96,2048]{1,0:T(8,128)(2,1)}, bf16[96,2048]{1,0:T(8,128)(2,1)}, f32[1,2048]{1,0:T(1,128)}, f32[1,2048]{1...) custom-call(bf16[16,128,1536]{2,1,0:T(8,128)(2,1)} %get-tuple-elemen, ...), custom_call_target="tpu_custom_call" | custom-call | tf_op jit(solution)/shard_map/pallas_call | solution.py:791
  102.0 53.4 %shard_map.223 = (f32[128,1536]{1,0:T(8,128)}, f32[128,1536]{1,0:T(8,128)}, bf16[16,96,128]{2,1,0:T(8,128)(2,1)}, bf16[8,192,128]{2,1,0:T(8,128)(2,1)}, bf16[8,1...) custom-call(bf16[128,1536]{1,0:T(8,128)(2,1)} %bitcast.55, bf16[16,96,128]{2,1,0:T(8,128)(2,1)} %get-tuple-element.48.att, ...), custom_call_target="tpu_custom_call" | custom-call | tf_op jit(solution)/shard_map/pallas_call | solution.py:404
  155.4 119.7 %shard_map.224 = (f32[128,1536]{1,0:T(8,128)}, f32[128,1536]{1,0:T(8,128)}, bf16[8,3,192,512]{3,2,1,0:T(8,128)(2,1)}, bf16[16,144,384]{2,1,0:T(8,128)(2,1)}) custom-call(bf16[16,96,128]{2,1,0:T(8,128)(2,1)} %get-tuple-element.53.dat, bf16[1536,128]{1,0:T(8,128)(2,1)} %bitcast.56, bf16[8,192,128]{2,1,0:T(8,128)(2,1)} %get-tuple-element.54.da_t, ...), custom_call_target="tpu_custom_call" | custom-call | tf_op jit(solution)/shard_map/pallas_call | solution.py:1075
  275.2 0.8 copy.44.gain
  275.9 9.9 %shard_map.226 = (f32[192,4096]{1,0:T(8,128)}, f32[192,4096]{1,0:T(8,128)}, f32[192,4096]{1,0:T(8,128)}, f32[1,192]{1,0:T(1,128)}) custom-call(bf16[8,3,192,512]{3,2,1,0:T(8,128)(2,1)} %get-tuple-element.72.gff, f32[192,1]{1,0:T(8,128)} %copy.44.gain, bf16[192,4096]{1,0:T(8,128)(2,1)} %w_gate.1, bf16[192,4096]{1,0:T(8,128)(2,1)} %w_up.1), custom_call_target="tpu_custom_call" | custom-call | tf_op jit(solution)/shard_map/pallas_call | solution.py:1153
  285.9 0.0 copy-start.3
  285.9 0.0 copy-start.9
  285.9 0.8 copy.43.gain
  286.6 4.4 %shard_map.225 = (f32[192,1536]{1,0:T(8,128)}, f32[192,768]{1,0:T(8,128)}, f32[192,768]{1,0:T(8,128)}, f32[192,1536]{1,0:T(8,128)}, f32[1,192]{1,0:T(1,128)}) custom-call(bf16[16,144,384]{2,1,0:T(8,128)(2,1)} %get-tuple-element.66.gatt, f32[192,1]{1,0:T(8,128)} %copy.43.gain, bf16[192,1536]{1,0:T(8,128)(2,1)} %w_query.1, bf16[192,768]{1,0:T(8,128)(2,1)} %w_key.1, ...), custom_call_target="tpu_custom_call" | custom-call | tf_op jit(solution)/shard_map/pallas_call | solution.py:1186
  291.0 0.0 copy-done.3
  291.0 0.0 copy-done.4
  291.0 0.0 copy-start.1
  291.0 0.3 fusion.4
  291.3 0.0 copy-done.9
  291.3 1.1 fusion.11
  292.4 0.0 copy-done.8
  292.4 0.0 copy-done.10
  292.4 0.8 fusion.10
  293.2 0.0 copy-done.1
  (12 shorter events, 0.1 us)
Async XLA Ops:
  0.6 2.5 copy-start
  0.7 2.3 copy-start.14
  2.5 2.1 copy-start.11
  2.5 2.1 copy-start.5
  3.2 2.1 copy-start.7
  4.5 1.3 copy-start.6
  5.8 2.2 copy-start.2
  6.3 2.7 copy-start.12
  8.0 49.9 %copy-start.13 = (s32[1,4]{1,0:T(1,128)S(1)}, s32[1,4]{1,0:T(1,128)}, u32[]{:S(2)}) copy-start(s32[1,4]{1,0:T(1,128)} %param.25) | copy-start | bytes 52
  285.9 5.2 %copy-start.3 = (bf16[1,128,1536]{2,1,0:T(8,128)(2,1)S(1)}, bf16[1,128,1536]{2,1,0:T(8,128)(2,1)}, u32[]{:S(2)}) copy-start(bf16[1,128,1536]{2,1,0:T(8,128)(2,1)} %param.14) | copy-start | bytes 1179652
  285.9 5.2 %copy-start.4 = (f32[128,1536]{1,0:T(8,128)S(1)}, f32[128,1536]{1,0:T(8,128)}, u32[]{:S(2)}) copy-start(f32[128,1536]{1,0:T(8,128)} %get-tuple-element.65) | copy-start | bytes 2359300
  285.9 5.4 %copy-start.9 = (f32[128,1536]{1,0:T(8,128)S(1)}, f32[128,1536]{1,0:T(8,128)}, u32[]{:S(2)}) copy-start(f32[128,1536]{1,0:T(8,128)} %get-tuple-element.64) | copy-start | bytes 2359300
  291.0 1.4 copy-start.8
  291.0 1.4 copy-start.10
  291.0 2.2 copy-start.1
